TPU v7x, 32 devices: a whole 2x2x4 slice. The times are simulated.
32 devices in a mesh: ctx: 16 (over z, y, core), tp: 2 (over x).
Axes of the slice: x: 2, y: 2, z: 4, core: 2. Of those that a mesh axis runs over, the one named last changes fastest.
Arguments:
- tokens: bfloat16 [5120, 6144], P('ctx', 'tp'), may hold values from -6 to 6
- norm_gain_vector: bfloat16 [6144], P('tp'), may hold values from 0.099609375 to 1.8984375
- keys: bfloat16 [5120, 3072], P('ctx', 'tp'), may hold values from -67 to 67
- values: bfloat16 [5120, 3072], P('ctx', 'tp'), may hold values from -6 to 6
- query_frozen_weight: bfloat16 [6144, 3072], P(None, 'tp'), may hold values from -0.078125 to 0.078125
- output_frozen_weight: bfloat16 [3072, 6144], P('tp'), may hold values from -2 to 2
- query_update_first: bfloat16 [16, 6144, 64], P('ctx'), may hold values from -0.078125 to 0.078125
- query_update_second: bfloat16 [16, 64, 3072], P('ctx', None, 'tp'), may hold values from -0.75 to 0.75
- output_update_first: bfloat16 [16, 3072, 64], P('ctx', 'tp'), may hold values from -0.109375 to 0.109375
- output_update_second: bfloat16 [16, 64, 6144], P('ctx'), may hold values from -6 to 6
- owners: int32 [4], replicated, may hold values from 0 to 15
- frame_block_number: int32 [80], replicated, may hold values from 0 to 19, never falling along the last dimension, each value on 1 to 8 neighbouring positions
Outputs:
- mixed: bfloat16 [5120, 6144], P('ctx', 'tp')
Inputs may be any that keep to these rules, and one draw needn't show every extreme that they name: `frame_block_number`: never falls along the frames; every block holds 1 to 8 frames, one exactly 8.
All inputs are finite; a program needn't handle non-finite values.
Results may differ from a plain program's by a relative error of at most 0.02.
The roundings to bfloat16 on the way count: a program that leaves them out, or rounds other values in their place, can miss the bound.
Values may be sent and summed in bfloat16 or wider, within the bound.
A program may use at most 192 MiB of HBM per device.

v0:
```python
import jax
import jax.numpy as jnp
from jax import lax
from jax.sharding import PartitionSpec as P

HS = 128
FTOK = 64


norm_eps = 1e-06
masked_score = -1e30


def spread(block, axis, source):
    block = jnp.where(lax.axis_index(axis) == source, block, jnp.zeros_like(block))
    return lax.psum(block, axis)


def merge_weight(base, down_factor, up_factor):
    return (
        base.astype(jnp.float32)
        + jnp.dot(down_factor, up_factor, preferred_element_type=jnp.float32)
    ).astype(jnp.bfloat16)


def block_width(total_rows):
    best = FTOK
    for candidate in range(FTOK, min(total_rows, 1280) + 1, FTOK):
        if total_rows % candidate == 0:
            best = candidate
    return best


def shards(
    tokens,
    norm_gain_vector,
    keys,
    values,
    query_frozen_weight,
    output_frozen_weight,
    query_update_first,
    query_update_second,
    output_update_first,
    output_update_second,
    owners,
    frame_block_number,
):
    tok_rows = tokens.shape[0]
    ctx_rank = lax.axis_index("ctx")
    trainer_positions = (
        query_update_first[0],
        query_update_second[0],
        output_update_first[0],
        output_update_second[0],
    )

    def fetch(slot, which):
        return spread(slot, "ctx", owners[which])

    query_down_factor, query_up_factor, output_down_factor, output_up_factor = [
        fetch(trainer_positions[which], which) for which in range(4)
    ]
    whole, gain = (
        lax.all_gather(tokens, "tp", axis=1, tiled=True),
        lax.all_gather(norm_gain_vector, "tp", axis=0, tiled=True),
    )
    features = whole.astype(jnp.float32)
    mean_square = jnp.mean(features * features, axis=-1, keepdims=True)
    normed = (features * lax.rsqrt(mean_square + norm_eps) * gain.astype(jnp.float32)).astype(
        jnp.bfloat16
    )
    query_merged = merge_weight(query_frozen_weight, query_down_factor, query_up_factor)
    queries = jnp.dot(normed, query_merged, preferred_element_type=jnp.float32).astype(jnp.bfloat16)
    local_heads = queries.shape[1] // HS
    queries = queries.reshape(tok_rows, local_heads, HS)
    frames_dev = tok_rows // FTOK
    own_frames = lax.dynamic_slice_in_dim(frame_block_number, ctx_rank * frames_dev, frames_dev, 0)
    query_block = jnp.broadcast_to(own_frames[:, None], (frames_dev, FTOK)).reshape(tok_rows)
    scale = HS ** (-0.5)
    initial = (
        jnp.full((local_heads, tok_rows), masked_score, jnp.float32),
        jnp.zeros((local_heads, tok_rows), jnp.float32),
        jnp.zeros((local_heads, tok_rows, HS), jnp.float32),
    )
    key_rows = lax.all_gather(keys, "ctx", axis=0, tiled=True)
    value_rows = lax.all_gather(values, "ctx", axis=0, tiled=True)
    total_rows = key_rows.shape[0]
    width = block_width(total_rows)

    def one_block(step_index, running):
        offset = step_index * width
        key_block = lax.dynamic_slice_in_dim(key_rows, offset, width, 0).reshape(
            width, local_heads, HS
        )
        value_block = lax.dynamic_slice_in_dim(value_rows, offset, width, 0).reshape(
            width, local_heads, HS
        )
        block_frames = lax.dynamic_slice_in_dim(
            frame_block_number, offset // FTOK, width // FTOK, 0
        )
        key_block_ids = jnp.broadcast_to(block_frames[:, None], (width // FTOK, FTOK)).reshape(
            width
        )
        seen = key_block_ids[None, :] <= query_block[:, None]
        top_old, total_old, summed_old = running
        scores = (
            jnp.einsum("qhd,khd->hqk", queries, key_block, preferred_element_type=jnp.float32)
            * scale
        )
        scores = jnp.where(seen[None], scores, masked_score)
        top_new = jnp.maximum(top_old, jnp.max(scores, axis=-1))
        factor = jnp.exp(top_old - top_new)
        weights = jnp.where(seen[None], jnp.exp(scores - top_new[..., None]), 0.0)
        total_new = total_old * factor + jnp.sum(weights, axis=-1)
        product = jnp.einsum(
            "hqk,khd->hqd",
            weights.astype(jnp.bfloat16),
            value_block,
            preferred_element_type=jnp.float32,
        )
        return (top_new, total_new, summed_old * factor[..., None] + product)

    top_final, total_final, summed_final = lax.fori_loop(0, total_rows // width, one_block, initial)
    attended = (
        (summed_final / total_final[..., None])
        .transpose(1, 0, 2)
        .reshape(tok_rows, local_heads * HS)
        .astype(jnp.bfloat16)
    )
    out_merged = merge_weight(output_frozen_weight, output_down_factor, output_up_factor)
    partial_value = jnp.dot(attended, out_merged, preferred_element_type=jnp.float32)
    return lax.psum_scatter(
        partial_value.astype(jnp.bfloat16), "tp", scatter_dimension=1, tiled=True
    )


def solution(mesh):
    in_specs = (
        P("ctx", "tp"),
        P("tp"),
        P("ctx", "tp"),
        P("ctx", "tp"),
        P(None, "tp"),
        P("tp", None),
        P("ctx", None, None),
        P("ctx", None, "tp"),
        P("ctx", "tp", None),
        P("ctx", None, None),
        P(),
        P(),
    )
    out_specs = P("ctx", "tp")
    return jax.shard_map(shards, mesh=mesh, in_specs=in_specs, out_specs=out_specs, check_vma=False)
```

profile of v0, /device:TPU:28, one launch (start us, length us, event | category | flops | bytes accessed | tf_op | source)
XLA Modules:
  0.0 573.7 jit_solution(2455793766652147901)
XLA Ops:
  16.9 4.4 all_gather.14
  21.3 43.2 %all-gather.6.cloned.1.call-done = bf16[320,6144]{1,0:T(8,128)(2,1)} async-done(((bf16[320,3072]{1,0:T(8,128)(2,1)}), bf16[320,6144]{1,0:T(8,128)(2,1)}) %all-gather.6.cloned.1.call-update) | async-done | bytes 3932176 | tf_op jit(solution)/shard_map/all_gather | solution.py:64
  67.6 124.6 %all-reduce.3.cloned.1.call-done = (bf16[6144,64]{0,1:T(8,128)(2,1)}, bf16[64,1536]{1,0:T(8,128)(2,1)}, bf16[1536,64]{0,1:T(8,128)(2,1)}, bf16[64,6144]{1,0:T(8,128)(2,1)}) async-done(((bf16[6144,64]{0,1:T(8,128)(2,1)}, bf16[64,1536]{1,0:T(8,128)(2,1)}, bf16[1536,64]{0,1:T(8,128)(2,1)}, bf16[64,6144]{1,0:T(8,128)(2,1)}), (bf16[6144,64]{0,1:T(8,128)(2,1)}, bf16[64,1536]{1,0:T(8,128)(2,1)}, ...) | async-done | bytes 1966096 | tf_op jit(solution)/shard_map/psum | solution.py:16
  192.1 16.7 %fusion.21 = bf16[320,1536]{1,0:T(8,128)(2,1)S(1)} fusion(bf16[6144,1536]{1,0:T(8,128)(2,1)} %param.18, bf16[6144,64]{0,1:T(8,128)(2,1)} %get-tuple-element.307, bf16[64,1536]{1,0:T(8,128)(2,1)} %get-tuple-element.308, bf16[320,6144]{1,0:T(8,128)(2,1)} %all-gather.6.cloned.1.call-done, f32[6144]{0:T(1024)S(1)} %convert_element_type.47, ...), kind=kOutput, calls=%fused_computation.30 | convolution fusion | flops 7284424704 | bytes 24798464 | tf_op jit(solution)/shard_map/dot_general | solution.py:73
  210.4 101.5 %all-gather.8.cloned.1.call-done = bf16[5120,1536]{1,0:T(8,128)(2,1)} async-done(((bf16[320,1536]{1,0:T(8,128)(2,1)}), bf16[5120,1536]{1,0:T(8,128)(2,1)}) %all-gather.8.cloned.1.call-update) | async-done | bytes 15728656 | tf_op jit(solution)/shard_map/all_gather | solution.py:86
  311.8 182.0 %while.20 = (s32[]{:T(128)}, f32[12,320]{1,0:T(8,128)S(1)}, f32[12,320]{1,0:T(8,128)S(1)}, f32[12,320,128]{2,1,0:T(8,128)}, s32[80]{0:T(128)S(1)}, /*index=5*/bf...) while((s32[]{:T(128)}, f32[12,320]{1,0:T(8,128)S(1)}, ...), condition=%wide.region_6.7_spmd.clone, body=%wide.region_3.6_spmd.clone.sunk | while | flops 2562722560 | bytes 199501552 | solution.py:123
  312.5 7.0 %constant_dynamic-slice_fusion.3 = (bf16[1280,1536]{1,0:T(8,128)(2,1)}, bf16[1280,1536]{1,0:T(8,128)(2,1)}) fusion(bf16[5120,1536]{1,0:T(8,128)(2,1)} %get-tuple-element.429, s32[]{:T(128)S(6)} %select_n.143, bf16[5120,1536]{1,0:T(8,128)(2,1)} %get-tuple-element.427), kind=kLoop, calls=%fused_computation.16.clone.1 | loop fusion | bytes 15728644 | tf_op jit(solution)/shard_map/while/body/eval_jaxpr/dynamic_slice | solution.py:95
  319.5 6.1 %copy.34 = bf16[1280,1536]{0,1:T(8,128)(2,1)} copy(bf16[1280,1536]{1,0:T(8,128)(2,1)} %get-tuple-element.382) | data formatting | bytes 7864320 | tf_op jit(solution)/shard_map/while/body/eval_jaxpr/dynamic_slice | solution.py:92
  325.7 6.3 %copy.35 = bf16[1280,1536]{0,1:T(8,128)(2,1)} copy(bf16[1280,1536]{1,0:T(8,128)(2,1)} %get-tuple-element.386) | data formatting | bytes 7864320 | tf_op jit(solution)/shard_map/while/body/eval_jaxpr/dynamic_slice | solution.py:95
  331.9 5.7 fusion.47
  337.7 5.2 fusion.48
  344.9 11.2 %fusion.50 = f32[12,320,128]{2,1,0:T(8,128)S(1)} fusion(f32[12,320,128]{2,1,0:T(8,128)S(1)} %copy-done.1, bf16[1280,12,128]{0,2,1:T(8,128)(2,1)} %bitcast.39, f32[12,320,1280]{2,1,0:T(8,128)} %copy-done, f32[12,320]{1,0:T(8,128)S(1)} %select_maximum_fusion.2, pred[320,1280]{1,0:T(8,128)(4,1)S(1)} %broadcast_compare_fusion.2, ...), kind=kOutput, calls=%fused_computation.10.clone.1 | convolution fusion | flops 1274511360 | bytes 27965440 | tf_op jit(solution)/shard_map/while/body/eval_jaxpr/hqk,khd->hqd/dot_general | solution.py:115
  358.0 7.0 %constant_dynamic-slice_fusion.3 = (bf16[1280,1536]{1,0:T(8,128)(2,1)}, bf16[1280,1536]{1,0:T(8,128)(2,1)}) fusion(bf16[5120,1536]{1,0:T(8,128)(2,1)} %get-tuple-element.429, s32[]{:T(128)S(6)} %select_n.143, bf16[5120,1536]{1,0:T(8,128)(2,1)} %get-tuple-element.427), kind=kLoop, calls=%fused_computation.16.clone.1 | loop fusion | bytes 15728644 | tf_op jit(solution)/shard_map/while/body/eval_jaxpr/dynamic_slice | solution.py:95
  365.0 6.1 %copy.34 = bf16[1280,1536]{0,1:T(8,128)(2,1)} copy(bf16[1280,1536]{1,0:T(8,128)(2,1)} %get-tuple-element.382) | data formatting | bytes 7864320 | tf_op jit(solution)/shard_map/while/body/eval_jaxpr/dynamic_slice | solution.py:92
  371.2 6.3 %copy.35 = bf16[1280,1536]{0,1:T(8,128)(2,1)} copy(bf16[1280,1536]{1,0:T(8,128)(2,1)} %get-tuple-element.386) | data formatting | bytes 7864320 | tf_op jit(solution)/shard_map/while/body/eval_jaxpr/dynamic_slice | solution.py:95
  377.5 5.7 fusion.47
  383.2 5.2 fusion.48
  390.4 11.2 %fusion.50 = f32[12,320,128]{2,1,0:T(8,128)S(1)} fusion(f32[12,320,128]{2,1,0:T(8,128)S(1)} %copy-done.1, bf16[1280,12,128]{0,2,1:T(8,128)(2,1)} %bitcast.39, f32[12,320,1280]{2,1,0:T(8,128)} %copy-done, f32[12,320]{1,0:T(8,128)S(1)} %select_maximum_fusion.2, pred[320,1280]{1,0:T(8,128)(4,1)S(1)} %broadcast_compare_fusion.2, ...), kind=kOutput, calls=%fused_computation.10.clone.1 | convolution fusion | flops 1274511360 | bytes 27965440 | tf_op jit(solution)/shard_map/while/body/eval_jaxpr/hqk,khd->hqd/dot_general | solution.py:115
  403.5 7.0 %constant_dynamic-slice_fusion.3 = (bf16[1280,1536]{1,0:T(8,128)(2,1)}, bf16[1280,1536]{1,0:T(8,128)(2,1)}) fusion(bf16[5120,1536]{1,0:T(8,128)(2,1)} %get-tuple-element.429, s32[]{:T(128)S(6)} %select_n.143, bf16[5120,1536]{1,0:T(8,128)(2,1)} %get-tuple-element.427), kind=kLoop, calls=%fused_computation.16.clone.1 | loop fusion | bytes 15728644 | tf_op jit(solution)/shard_map/while/body/eval_jaxpr/dynamic_slice | solution.py:95
  410.5 6.1 %copy.34 = bf16[1280,1536]{0,1:T(8,128)(2,1)} copy(bf16[1280,1536]{1,0:T(8,128)(2,1)} %get-tuple-element.382) | data formatting | bytes 7864320 | tf_op jit(solution)/shard_map/while/body/eval_jaxpr/dynamic_slice | solution.py:92
  416.7 6.3 %copy.35 = bf16[1280,1536]{0,1:T(8,128)(2,1)} copy(bf16[1280,1536]{1,0:T(8,128)(2,1)} %get-tuple-element.386) | data formatting | bytes 7864320 | tf_op jit(solution)/shard_map/while/body/eval_jaxpr/dynamic_slice | solution.py:95
  423.0 5.7 fusion.47
  428.7 5.2 fusion.48
  435.9 11.2 %fusion.50 = f32[12,320,128]{2,1,0:T(8,128)S(1)} fusion(f32[12,320,128]{2,1,0:T(8,128)S(1)} %copy-done.1, bf16[1280,12,128]{0,2,1:T(8,128)(2,1)} %bitcast.39, f32[12,320,1280]{2,1,0:T(8,128)} %copy-done, f32[12,320]{1,0:T(8,128)S(1)} %select_maximum_fusion.2, pred[320,1280]{1,0:T(8,128)(4,1)S(1)} %broadcast_compare_fusion.2, ...), kind=kOutput, calls=%fused_computation.10.clone.1 | convolution fusion | flops 1274511360 | bytes 27965440 | tf_op jit(solution)/shard_map/while/body/eval_jaxpr/hqk,khd->hqd/dot_general | solution.py:115
  449.0 7.0 %constant_dynamic-slice_fusion.3 = (bf16[1280,1536]{1,0:T(8,128)(2,1)}, bf16[1280,1536]{1,0:T(8,128)(2,1)}) fusion(bf16[5120,1536]{1,0:T(8,128)(2,1)} %get-tuple-element.429, s32[]{:T(128)S(6)} %select_n.143, bf16[5120,1536]{1,0:T(8,128)(2,1)} %get-tuple-element.427), kind=kLoop, calls=%fused_computation.16.clone.1 | loop fusion | bytes 15728644 | tf_op jit(solution)/shard_map/while/body/eval_jaxpr/dynamic_slice | solution.py:95
  456.1 6.1 %copy.34 = bf16[1280,1536]{0,1:T(8,128)(2,1)} copy(bf16[1280,1536]{1,0:T(8,128)(2,1)} %get-tuple-element.382) | data formatting | bytes 7864320 | tf_op jit(solution)/shard_map/while/body/eval_jaxpr/dynamic_slice | solution.py:92
  462.2 6.3 %copy.35 = bf16[1280,1536]{0,1:T(8,128)(2,1)} copy(bf16[1280,1536]{1,0:T(8,128)(2,1)} %get-tuple-element.386) | data formatting | bytes 7864320 | tf_op jit(solution)/shard_map/while/body/eval_jaxpr/dynamic_slice | solution.py:95
  468.5 5.7 fusion.47
  474.2 5.2 fusion.48
  481.4 11.2 %fusion.50 = f32[12,320,128]{2,1,0:T(8,128)S(1)} fusion(f32[12,320,128]{2,1,0:T(8,128)S(1)} %copy-done.1, bf16[1280,12,128]{0,2,1:T(8,128)(2,1)} %bitcast.39, f32[12,320,1280]{2,1,0:T(8,128)} %copy-done, f32[12,320]{1,0:T(8,128)S(1)} %select_maximum_fusion.2, pred[320,1280]{1,0:T(8,128)(4,1)S(1)} %broadcast_compare_fusion.2, ...), kind=kOutput, calls=%fused_computation.10.clone.1 | convolution fusion | flops 1274511360 | bytes 27965440 | tf_op jit(solution)/shard_map/while/body/eval_jaxpr/hqk,khd->hqd/dot_general | solution.py:115
  496.8 16.5 %convolution_convert_fusion = bf16[320,6144]{1,0:T(8,128)(2,1)} fusion(bf16[320,1536]{0,1:T(8,128)(2,1)S(1)} %bitcast.41, bf16[1536,6144]{1,0:T(8,128)(2,1)} %param.19, bf16[1536,64]{0,1:T(8,128)(2,1)S(1)} %copy-done.5, bf16[64,6144]{1,0:T(8,128)(2,1)S(1)} %copy-done.4), kind=kOutput, calls=%fused_computation.23 | convolution fusion | flops 7278034944 | bytes 24772608 | tf_op jit(solution)/shard_map/dot_general | solution.py:131
  513.3 53.3 %reduce-scatter.2.cloned.1.call-done = bf16[320,3072]{1,0:T(8,128)(2,1)} async-done(((bf16[320,6144]{1,0:T(8,128)(2,1)}), bf16[320,3072]{1,0:T(8,128)(2,1)}) %reduce-scatter.2.cloned.1.call-update) | async-done | bytes 1966096 | tf_op jit(solution)/shard_map/reduce_scatter | solution.py:132
  (95 shorter events, 30.0 us)
Async XLA Ops:
  7.4 9.5 %copy-start.3 = (bf16[3072]{0:T(1024)(128)(2,1)S(1)}, bf16[3072]{0:T(1024)(128)(2,1)}, u32[]{:S(2)}) copy-start(bf16[3072]{0:T(1024)(128)(2,1)} %param.15) | copy-start | bytes 18436
  7.4 13.9 %copy-start.6 = (s32[80]{0:T(128)S(1)}, s32[80]{0:T(128)}, u32[]{:S(2)}) copy-start(s32[80]{0:T(128)} %param.25) | copy-start | bytes 964
  7.4 57.2 %all-gather.6.cloned.1.call-start = ((), (), s32[]{:S(2)}) async-start(), calls=%async_computation.2 | async-start | bytes 5898240 | tf_op jit(solution)/shard_map/all_gather | solution.py:64
  8.1 184.0 %all-reduce.3.cloned.1.call-start = ((), (), s32[]{:S(2)}) async-start(), calls=%async_computation.5 | async-start | bytes 3932160 | tf_op jit(solution)/shard_map/psum | solution.py:16
  15.3 195.0 %all-gather.4.cloned.1.call-start = ((), (), s32[]{:S(2)}) async-start(), calls=%async_computation.1 | async-start | bytes 16711680 | tf_op jit(solution)/shard_map/all_gather | solution.py:85
  16.1 295.8 %all-gather.8.cloned.1.call-start = ((), (), s32[]{:S(2)}) async-start(), calls=%async_computation.3 | async-start | bytes 16711680 | tf_op jit(solution)/shard_map/all_gather | solution.py:86
  16.8 549.7 %reduce-scatter.2.cloned.1.call-start = ((), (), s32[]{:S(2)}) async-start(), calls=%async_computation.4 | async-start | bytes 5898240 | tf_op jit(solution)/shard_map/reduce_scatter | solution.py:132
  311.8 184.9 %copy-start.4 = (bf16[64,6144]{1,0:T(8,128)(2,1)S(1)}, bf16[64,6144]{1,0:T(8,128)(2,1)}, u32[]{:S(2)}) copy-start(bf16[64,6144]{1,0:T(8,128)(2,1)} %get-tuple-element.310) | copy-start | bytes 2359300
  311.8 184.9 %copy-start.5 = (bf16[1536,64]{0,1:T(8,128)(2,1)S(1)}, bf16[1536,64]{0,1:T(8,128)(2,1)}, u32[]{:S(2)}) copy-start(bf16[1536,64]{0,1:T(8,128)(2,1)} %get-tuple-element.309) | copy-start | bytes 589828
  337.6 7.2 %copy-start = (f32[12,320,1280]{2,1,0:T(8,128)}, f32[12,320,1280]{2,1,0:T(8,128)S(1)}, u32[]{:S(2)}) copy-start(f32[12,320,1280]{2,1,0:T(8,128)S(1)} %get-tuple-element.384) | copy-start | bytes 58982404 | tf_op jit(solution)/shard_map/while
  337.7 7.2 %copy-start.1 = (f32[12,320,128]{2,1,0:T(8,128)S(1)}, f32[12,320,128]{2,1,0:T(8,128)}, u32[]{:S(2)}) copy-start(f32[12,320,128]{2,1,0:T(8,128)} %get-tuple-element.408) | copy-start | bytes 5898244 | tf_op jit(solution)/shard_map/while
  356.1 1.3 copy-start.2
  383.1 7.2 %copy-start = (f32[12,320,1280]{2,1,0:T(8,128)}, f32[12,320,1280]{2,1,0:T(8,128)S(1)}, u32[]{:S(2)}) copy-start(f32[12,320,1280]{2,1,0:T(8,128)S(1)} %get-tuple-element.384) | copy-start | bytes 58982404 | tf_op jit(solution)/shard_map/while
  383.2 7.2 %copy-start.1 = (f32[12,320,128]{2,1,0:T(8,128)S(1)}, f32[12,320,128]{2,1,0:T(8,128)}, u32[]{:S(2)}) copy-start(f32[12,320,128]{2,1,0:T(8,128)} %get-tuple-element.408) | copy-start | bytes 5898244 | tf_op jit(solution)/shard_map/while
  401.6 1.3 copy-start.2
  428.6 7.2 %copy-start = (f32[12,320,1280]{2,1,0:T(8,128)}, f32[12,320,1280]{2,1,0:T(8,128)S(1)}, u32[]{:S(2)}) copy-start(f32[12,320,1280]{2,1,0:T(8,128)S(1)} %get-tuple-element.384) | copy-start | bytes 58982404 | tf_op jit(solution)/shard_map/while
  428.7 7.2 %copy-start.1 = (f32[12,320,128]{2,1,0:T(8,128)S(1)}, f32[12,320,128]{2,1,0:T(8,128)}, u32[]{:S(2)}) copy-start(f32[12,320,128]{2,1,0:T(8,128)} %get-tuple-element.408) | copy-start | bytes 5898244 | tf_op jit(solution)/shard_map/while
  447.1 1.3 copy-start.2
  474.2 7.2 %copy-start = (f32[12,320,1280]{2,1,0:T(8,128)}, f32[12,320,1280]{2,1,0:T(8,128)S(1)}, u32[]{:S(2)}) copy-start(f32[12,320,1280]{2,1,0:T(8,128)S(1)} %get-tuple-element.384) | copy-start | bytes 58982404 | tf_op jit(solution)/shard_map/while
  474.2 7.2 %copy-start.1 = (f32[12,320,128]{2,1,0:T(8,128)S(1)}, f32[12,320,128]{2,1,0:T(8,128)}, u32[]{:S(2)}) copy-start(f32[12,320,128]{2,1,0:T(8,128)} %get-tuple-element.408) | copy-start | bytes 5898244 | tf_op jit(solution)/shard_map/while
  492.6 1.3 copy-start.2
Sparse Core Ops, SparseCore 0:
  9.7 54.7 all-gather.5
  66.9 123.7 all-gather.3
  192.9 118.8 all-gather.7
  513.4 53.0 reduce-scatter.1
Sparse Core Ops, SparseCore 1:
  15.4 176.7 all-reduce.2
where the time goes:
time: 577 us; the launch traced here: 574 us
  waiting for transfers between devices  325 us (56%)
  matrix products  101 us (18%)
  local copies, waits for them, and re-layouts  95.7 us (17%)
  other arithmetic  30.6 us (5%)
  between operations  17.1 us (3%)
    psum x1, waiting for transfers between devices, spread(): return lax.psum(block, axis)  125 us
    all_gather x1, waiting for transfers between devices, shards(): value_rows = lax.all_gather(values, 'ctx', axis=0, tiled=True)  101 us
    reduce_scatter x1, waiting for transfers between devices, shards(): lax.psum_scatter(partial_value.astype(jnp.bfloat16), 'tp', scatter_dimens...  53.3 us
    dynamic_slice x8, local copies, waits for them, and re-layouts, one_block(): lax.dynamic_slice_in_dim(value_rows, offset, width, 0)  53.1 us
    dot_general x4, matrix products, one_block(): jnp.einsum('hqk,khd->hqd', weights.astype(jnp.bfloat16), value_block, pre...  44.8 us
    all_gather x1, waiting for transfers between devices, shards(): lax.all_gather(tokens, 'tp', axis=1, tiled=True)  43.2 us
    dynamic_slice x4, local copies, waits for them, and re-layouts, one_block(): lax.dynamic_slice_in_dim(key_rows, offset, width, 0)  24.6 us
    dot_general x4, matrix products, one_block(): jnp.einsum('qhd,khd->hqk', queries, key_block, preferred_element_type=jnp...  22.7 us
  transfers between devices with their start and end apart: 5, of which 4 were waited for; matrix products, arithmetic and copies ran while one was open for 5% of the time, Pallas kernels for 0%

commit v1 on v0

v1 whole, which is shorter than its diff:
```python
import functools

import jax
import jax.numpy as jnp
from jax import lax
from jax.experimental import pallas as pl
from jax.experimental.pallas import tpu as pltpu
from jax.sharding import PartitionSpec as P

HS = 128
FTOK = 64
norm_eps = 1e-06
masked_score = -1e30
LOG2E = 1.4426950408889634


def swap(x, bit):
    n = lax.axis_size("ctx")
    return lax.ppermute(x, "ctx", [(i, i ^ bit) for i in range(n)])


def fetch_pair(down, up, down_owner, up_owner):
    n = lax.axis_size("ctx")
    me = lax.axis_index("ctx")
    cols = down.shape[0]
    buf = jnp.concatenate([down.T, up], axis=1)
    owner = jnp.where(jnp.arange(buf.shape[1]) < cols, down_owner, up_owner)[None, :]
    halved = []
    bit = 1
    while bit < n:
        high = (me & bit) != 0
        if bit <= 2:
            half = buf.shape[1] // 2
            low_part, high_part = buf[:, :half], buf[:, half:]
            received = swap(jnp.where(high, low_part, high_part), bit)
            kept = jnp.where(high, high_part, low_part)
            owner = jnp.where(high, owner[:, half:], owner[:, :half])
            halved.append(bit)
        else:
            received = swap(buf, bit)
            kept = buf
        buf = jnp.where((owner & bit) == (me & bit), kept, received)
        bit *= 2
    for bit in reversed(halved):
        high = (me & bit) != 0
        other = swap(buf, bit)
        buf = jnp.concatenate(
            [jnp.where(high, other, buf), jnp.where(high, buf, other)], axis=1
        )
    return buf[:, :cols], buf[:, cols:]


def merge_weight(base, down_t, up):
    product = lax.dot_general(
        down_t, up, (((0,), (0,)), ((), ())), preferred_element_type=jnp.float32
    )
    return (base.astype(jnp.float32) + product).astype(jnp.bfloat16)


def attention_kernel(groups, ranks, heads, rows, *refs):
    n = groups * ranks
    info, kid, qid = refs[:3]
    q_in = refs[3 : 3 + groups]
    kv_in = refs[3 + groups : 3 + groups + n]
    outs = refs[3 + groups + n : 3 + 2 * groups + n]
    q_buf, kv_buf, o_buf, top, total, acc, q_sem, kv_sem, o_sem = refs[3 + 2 * groups + n :]
    loads = [pltpu.make_async_copy(q_in[i], q_buf.at[i], q_sem.at[i]) for i in range(groups)]
    loads += [pltpu.make_async_copy(kv_in[i], kv_buf.at[i], kv_sem.at[i]) for i in range(n)]
    for load in loads:
        load.start()
    for load in loads:
        load.wait()
    my_group, my_rank = info[2 * groups], info[2 * groups + 1]
    rate = HS ** (-0.5) * LOG2E

    def group_body(g, carry):
        top[...] = jnp.full(top.shape, masked_score, jnp.float32)
        total[...] = jnp.zeros(total.shape, jnp.float32)
        acc[...] = jnp.zeros(acc.shape, jnp.float32)

        def chunk(c, masked):
            first = 2 * c
            slots = []
            for r in (first, first + 1):
                slots.append((r // ranks ^ my_group) * ranks + (r % ranks ^ my_rank))
            if masked:
                seen = kid[c] <= qid[g]
            for h in range(heads):
                cut = slice(h * HS, (h + 1) * HS)
                k = jnp.concatenate([kv_buf[s, :rows, cut] for s in slots], axis=0)
                v = jnp.concatenate([kv_buf[s, rows:, cut] for s in slots], axis=0)
                scores = lax.dot_general(
                    q_buf[g, :, cut], k, (((1,), (1,)), ((), ())),
                    preferred_element_type=jnp.float32,
                )
                if masked:
                    scores = jnp.where(seen, scores, masked_score)
                old = top[h]
                new = jnp.maximum(old, jnp.max(scores, axis=1, keepdims=True))
                weights = jnp.exp2((scores - new[:, :1]) * rate)
                factor = jnp.exp2((old - new) * rate)
                top[h] = new
                total[h] = total[h] * factor + jnp.sum(weights, axis=1, keepdims=True)
                acc[h] = acc[h] * factor + jnp.dot(
                    weights.astype(jnp.bfloat16), v, preferred_element_type=jnp.float32
                )

        def plain(c, carry):
            chunk(c, False)
            return carry

        def edge(c, carry):
            chunk(c, True)
            return carry

        lax.fori_loop(0, info[g], plain, 0)
        lax.fori_loop(info[g], info[groups + g], edge, 0)
        for h in range(heads):
            o_buf[g, :, h * HS : (h + 1) * HS] = (acc[h] / total[h]).astype(jnp.bfloat16)
        return carry

    lax.fori_loop(0, groups, group_body, 0)
    stores = [pltpu.make_async_copy(o_buf.at[i], outs[i], o_sem.at[i]) for i in range(groups)]
    for store in stores:
        store.start()
    for store in stores:
        store.wait()


def attend(q_parts, kv_parts, groups, ranks, frame_block_number):
    rows, width = q_parts[0].shape
    heads = width // HS
    n = groups * ranks
    me = lax.axis_index("ctx")
    my_group, my_rank = me // ranks, me % ranks
    frames = rows // FTOK
    chunk_frames = 2 * frames
    blocks = frame_block_number.reshape(n, frames)
    q_ranks = (jnp.arange(groups) ^ my_group) * ranks + my_rank
    own = blocks[q_ranks]
    full = jnp.sum(frame_block_number[None, :] <= own[:, :1], axis=1) // chunk_frames
    some = jnp.sum(frame_block_number[None, :] <= own[:, -1:], axis=1)
    some = (some + chunk_frames - 1) // chunk_frames
    info = jnp.concatenate([full, some, jnp.stack([my_group, my_rank])]).astype(jnp.int32)
    kid = jnp.repeat(frame_block_number, FTOK).reshape(n // 2, 1, 2 * rows)
    qid = jnp.repeat(own, FTOK, axis=1).reshape(groups, rows, 1)
    bf16, f32 = jnp.bfloat16, jnp.float32
    any_spec = pl.BlockSpec(memory_space=pl.ANY)
    return pl.pallas_call(
        functools.partial(attention_kernel, groups, ranks, heads, rows),
        out_shape=[jax.ShapeDtypeStruct((rows, width), bf16)] * groups,
        in_specs=[
            pl.BlockSpec(memory_space=pltpu.SMEM),
            pl.BlockSpec(memory_space=pltpu.VMEM),
            pl.BlockSpec(memory_space=pltpu.VMEM),
        ]
        + [any_spec] * (groups + n),
        out_specs=[any_spec] * groups,
        scratch_shapes=[
            pltpu.VMEM((groups, rows, width), bf16),
            pltpu.VMEM((n, 2 * rows, width), bf16),
            pltpu.VMEM((groups, rows, width), bf16),
            pltpu.VMEM((heads, rows, HS), f32),
            pltpu.VMEM((heads, rows, HS), f32),
            pltpu.VMEM((heads, rows, HS), f32),
            pltpu.SemaphoreType.DMA((groups,)),
            pltpu.SemaphoreType.DMA((n,)),
            pltpu.SemaphoreType.DMA((groups,)),
        ],
        compiler_params=pltpu.CompilerParams(vmem_limit_bytes=48 * 2**20),
        cost_estimate=pl.CostEstimate(
            flops=2 * groups * rows * n * rows * width,
            bytes_accessed=(2 * n + 2 * groups) * rows * width * 2,
            transcendentals=groups * rows * n * rows * heads // 2,
        ),
        name="block_attention",
    )(info, kid, qid, *q_parts, *kv_parts)


def shards(
    tokens,
    norm_gain_vector,
    keys,
    values,
    query_frozen_weight,
    output_frozen_weight,
    query_update_first,
    query_update_second,
    output_update_first,
    output_update_second,
    owners,
    frame_block_number,
):
    n, tp = lax.axis_size("ctx"), lax.axis_size("tp")
    me, mine = lax.axis_index("ctx"), lax.axis_index("tp")
    local_heads = keys.shape[1] // HS
    groups = next(g for g in (4, 2, 1) if local_heads % g == 0 and n % (2 * g) == 0)
    ranks = n // groups
    width = keys.shape[1] // groups
    my_group = me // ranks

    def columns(x, step):
        return lax.dynamic_slice_in_dim(x, (my_group ^ step) * width, width, 1)

    whole = lax.all_gather(tokens, "tp", axis=1, tiled=True)
    gain = lax.all_gather(norm_gain_vector, "tp", axis=0, tiled=True)
    query_down_t, query_up = fetch_pair(
        query_update_first[0], query_update_second[0], owners[0], owners[1]
    )

    kv_parts = []
    for step in range(groups):
        part = jnp.concatenate([columns(keys, step), columns(values, step)], axis=0)
        if step:
            part = swap(part, step * ranks)
        have = {0: part}
        bit = ranks // 2
        while bit:
            have.update({j | bit: swap(x, bit) for j, x in list(have.items())})
            bit //= 2
        kv_parts += [have[j] for j in range(ranks)]

    features = whole.astype(jnp.float32)
    mean_square = jnp.mean(features * features, axis=-1, keepdims=True)
    normed = (features * lax.rsqrt(mean_square + norm_eps) * gain.astype(jnp.float32)).astype(
        jnp.bfloat16
    )
    query_merged = merge_weight(query_frozen_weight, query_down_t, query_up)
    queries = jnp.dot(normed, query_merged, preferred_element_type=jnp.float32).astype(jnp.bfloat16)

    q_parts = []
    for step in range(groups):
        part = columns(queries, step)
        q_parts.append(swap(part, step * ranks) if step else part)

    out_down_t, out_up = fetch_pair(
        output_update_first[0], output_update_second[0], owners[2], owners[3]
    )
    out_merged = merge_weight(output_frozen_weight, out_down_t, out_up)

    o_parts = attend(q_parts, kv_parts, groups, ranks, frame_block_number)
    stacked = jnp.stack([swap(o, i * ranks) if i else o for i, o in enumerate(o_parts)])
    attended = jnp.concatenate(
        [lax.dynamic_index_in_dim(stacked, my_group ^ g, 0, keepdims=False) for g in range(groups)],
        axis=1,
    )
    if tp != 2:
        partial_value = jnp.dot(attended, out_merged, preferred_element_type=jnp.float32)
        return lax.psum_scatter(
            partial_value.astype(jnp.bfloat16), "tp", scatter_dimension=1, tiled=True
        )
    half = out_merged.shape[1] // 2
    pieces = 4
    step = half // pieces
    received = []
    for i in range(pieces):
        theirs = lax.dynamic_slice_in_dim(out_merged, (1 - mine) * half + i * step, step, 1)
        product = jnp.dot(attended, theirs, preferred_element_type=jnp.float32)
        received.append(lax.ppermute(product.astype(jnp.bfloat16), "tp", [(0, 1), (1, 0)]))
    own = lax.dynamic_slice_in_dim(out_merged, mine * half, half, 1)
    product = jnp.dot(attended, own, preferred_element_type=jnp.float32)
    return jnp.concatenate(
        [
            (product[:, i * step : (i + 1) * step] + received[i].astype(jnp.float32)).astype(
                jnp.bfloat16
            )
            for i in range(pieces)
        ],
        axis=1,
    )


def solution(mesh):
    in_specs = (
        P("ctx", "tp"),
        P("tp"),
        P("ctx", "tp"),
        P("ctx", "tp"),
        P(None, "tp"),
        P("tp", None),
        P("ctx", None, None),
        P("ctx", None, "tp"),
        P("ctx", "tp", None),
        P("ctx", None, None),
        P(),
        P(),
    )
    out_specs = P("ctx", "tp")
    return jax.shard_map(shards, mesh=mesh, in_specs=in_specs, out_specs=out_specs, check_vma=False)
```

time: 577 us -> 311 us (0.54)
  the two profiles are of different devices: /device:TPU:28 before, /device:TPU:13 now
where the time goes in v1:
time: 311 us; the launch traced here: 310 us
  waiting for transfers between devices  130 us (42%)
  Pallas kernels  52.7 us (17%)
  matrix products  41.7 us (13%)
  starting transfers between devices  38.1 us (12%)
  other arithmetic  21.2 us (7%)
  between operations  13.7 us (4%)
  local copies, waits for them, and re-layouts  8.95 us (3%)
  blocking collectives  3.63 us (1%)
    ppermute x33, waiting for transfers between devices, swap(): return lax.ppermute(x, 'ctx', [(i, i ^ bit) for i in range(n)])  92.7 us
    pallas_call x1, Pallas kernels, attend(): pl.pallas_call(functools.partial(attention_kernel, groups, ranks, heads,...  52.7 us
    ppermute x4, waiting for transfers between devices, shards(): lax.ppermute(product.astype(jnp.bfloat16), 'tp', [(0, 1), (1, 0)])  37.6 us
    ppermute x33, starting transfers between devices, swap(): return lax.ppermute(x, 'ctx', [(i, i ^ bit) for i in range(n)])  35.1 us
    dot_general x1, matrix products, shards(): jnp.dot(normed, query_merged, preferred_element_type=jnp.float32)  17.5 us
    dot_general x1, matrix products, merge_weight(): lax.dot_general(down_t, up, (((0,), (0,)), ((), ())), preferred_element_t...  12.9 us
    dot_general x4, matrix products, shards(): product = jnp.dot(attended, theirs, preferred_element_type=jnp.float32)  7.98 us
  transfers between devices with their start and end apart: 38, of which 17 were waited for; matrix products, arithmetic and copies ran while one was open for 18% of the time, Pallas kernels for 0%

profile of v1, /device:TPU:13, one launch (start us, length us, event | category | flops | bytes accessed | tf_op | source)
XLA Modules:
  0.0 310.2 jit_solution(10683331072170822058)
XLA Ops:
  6.5 2.5 constant_dynamic-slice_fusion
  10.4 2.2 broadcast_select_fusion.2
  15.8 2.3 collective-permute-start.16
  22.7 3.6 %all_gather.7 = bf16[6144]{0:T(1024)(128)(2,1)S(1)} all-gather(bf16[3072]{0:T(1024)(128)(2,1)S(1)} %copy-done.6), channel_id=1, replica_groups=mesh['ctx'=16,'tp'=2] {'tp'}, dimensions={0}, use_global_device_ids=true | all-gather | bytes 18432 | tf_op jit(solution)/shard_map/all_gather | solution.py:206
  33.3 3.7 %collective-permute-done.1 = bf16[64,1920]{1,0:T(8,128)(2,1)S(1)} collective-permute-done((bf16[64,1920]{1,0:T(8,128)(2,1)S(1)}, bf16[64,1920]{1,0:T(8,128)(2,1)S(1)}, u32[]{:S(2)}, u32[]{:S(2)}) %collective-permute-start.1) | collective-permute-done | bytes 245792 | tf_op jit(solution)/shard_map/ppermute | solution.py:19
  38.2 4.2 %collective-permute-done.28 = bf16[64,1920]{1,0:T(8,128)(2,1)S(1)} collective-permute-done((bf16[64,1920]{1,0:T(8,128)(2,1)S(1)}, bf16[64,1920]{1,0:T(8,128)(2,1)S(1)}, u32[]{:S(2)}, u32[]{:S(2)}) %collective-permute-start.28) | collective-permute-done | bytes 245792 | tf_op jit(solution)/shard_map/ppermute | solution.py:19
  43.7 10.6 %collective-permute-done.2 = bf16[64,1920]{1,0:T(8,128)(2,1)S(1)} collective-permute-done((bf16[64,1920]{1,0:T(8,128)(2,1)S(1)}, bf16[64,1920]{1,0:T(8,128)(2,1)S(1)}, u32[]{:S(2)}, u32[]{:S(2)}) %collective-permute-start.2) | collective-permute-done | bytes 245792 | tf_op jit(solution)/shard_map/ppermute | solution.py:19
  54.3 2.3 collective-permute-start.29
  56.7 6.1 %collective-permute-done.29 = bf16[64,1920]{1,0:T(8,128)(2,1)S(1)} collective-permute-done((bf16[64,1920]{1,0:T(8,128)(2,1)S(1)}, bf16[64,1920]{1,0:T(8,128)(2,1)S(1)}, u32[]{:S(2)}, u32[]{:S(2)}) %collective-permute-start.29) | collective-permute-done | bytes 245792 | tf_op jit(solution)/shard_map/ppermute | solution.py:19
  64.0 10.9 %collective-permute-done.3 = bf16[64,1920]{1,0:T(8,128)(2,1)S(1)} collective-permute-done((bf16[64,1920]{1,0:T(8,128)(2,1)S(1)}, bf16[64,1920]{1,0:T(8,128)(2,1)S(1)}, u32[]{:S(2)}, u32[]{:S(2)}) %collective-permute-start.3) | collective-permute-done | bytes 245792 | tf_op jit(solution)/shard_map/ppermute | solution.py:19
  74.9 3.1 collective-permute-start.30
  78.0 10.5 %collective-permute-done.30 = bf16[64,1920]{1,0:T(8,128)(2,1)S(1)} collective-permute-done((bf16[64,1920]{1,0:T(8,128)(2,1)S(1)}, bf16[64,1920]{1,0:T(8,128)(2,1)S(1)}, u32[]{:S(2)}, u32[]{:S(2)}) %collective-permute-start.30) | collective-permute-done | bytes 245792 | tf_op jit(solution)/shard_map/ppermute | solution.py:19
  89.9 5.7 %collective-permute-done.4 = bf16[64,1920]{1,0:T(8,128)(2,1)S(1)} collective-permute-done((bf16[64,1920]{1,0:T(8,128)(2,1)S(1)}, bf16[64,1920]{1,0:T(8,128)(2,1)S(1)}, u32[]{:S(2)}, u32[]{:S(2)}) %collective-permute-start.4) | collective-permute-done | bytes 245792 | tf_op jit(solution)/shard_map/ppermute | solution.py:19
  97.0 4.7 %collective-permute-done.31 = bf16[64,1920]{1,0:T(8,128)(2,1)S(1)} collective-permute-done((bf16[64,1920]{1,0:T(8,128)(2,1)S(1)}, bf16[64,1920]{1,0:T(8,128)(2,1)S(1)}, u32[]{:S(2)}, u32[]{:S(2)}) %collective-permute-start.31) | collective-permute-done | bytes 245792 | tf_op jit(solution)/shard_map/ppermute | solution.py:19
  101.7 2.3 collective-permute-start.5
  109.0 3.0 fusion.2
  112.0 16.5 %collective-permute-done.20.refs_19_ = bf16[640,384]{1,0:T(8,128)(2,1)} collective-permute-done((bf16[640,384]{1,0:T(8,128)(2,1)}, bf16[640,384]{1,0:T(8,128)(2,1)}, u32[]{:S(2)}, u32[]{:S(2)}) %collective-permute-start.20) | collective-permute-done | bytes 491552 | tf_op jit(solution)/shard_map/ppermute | solution.py:19
  131.5 17.5 %fusion.9 = bf16[320,1536]{1,0:T(8,128)(2,1)} fusion(bf16[6144,1536]{1,0:T(8,128)(2,1)} %param.16, bf16[320,6144]{1,0:T(8,128)(2,1)} %all-gather.2.cloned.1.call-done, f32[6144]{0:T(1024)S(1)} %convert_element_type.69, f32[320]{0:T(512)S(1)} %add_rsqrt_fusion, bf16[64,3840]{1,0:T(8,128)(2,1)} %get-tuple-element.48, bf16[64,3840]{1,0:T(8,128)(2,1)} %get-tuple-element.47), kind=kOutput, calls=%fused_computation.13 | convolution fusion | flops 7285997568 | bytes 24995072 | tf_op jit(solution)/shard_map/dot_general | solution.py:229
  151.6 4.3 %collective-permute-start.7 = (bf16[320,384]{1,0:T(8,128)(2,1)S(1)}, bf16[320,384]{1,0:T(8,128)(2,1)S(1)}, u32[]{:S(2)}, u32[]{:S(2)}) collective-permute-start(bf16[320,384]{1,0:T(8,128)(2,1)S(1)} %get-tuple-element.44), channel_id=1, source_target_pairs={{0,16},{2,18},{4,20},{6,22},{8,24},{10,26},{12,28},{14,30},{16,0},... | collective-permute-start | bytes 737288 | tf_op jit(solution)/shard_map/ppermute | solution.py:19
  158.1 10.7 %collective-permute-done.8.refs_6_ = bf16[320,384]{1,0:T(8,128)(2,1)S(1)} collective-permute-done((bf16[320,384]{1,0:T(8,128)(2,1)S(1)}, bf16[320,384]{1,0:T(8,128)(2,1)S(1)}, u32[]{:S(2)}, u32[]{:S(2)}) %collective-permute-start.8) | collective-permute-done | bytes 245792 | tf_op jit(solution)/shard_map/ppermute | solution.py:19
  168.8 3.7 %collective-permute-done.7.refs_5_ = bf16[320,384]{1,0:T(8,128)(2,1)S(1)} collective-permute-done((bf16[320,384]{1,0:T(8,128)(2,1)S(1)}, bf16[320,384]{1,0:T(8,128)(2,1)S(1)}, u32[]{:S(2)}, u32[]{:S(2)}) %collective-permute-start.7) | collective-permute-done | bytes 245792 | tf_op jit(solution)/shard_map/ppermute | solution.py:19
  172.5 52.7 %block_attention.1 = (bf16[320,384]{1,0:T(8,128)(2,1)S(1)}, bf16[320,384]{1,0:T(8,128)(2,1)}, bf16[320,384]{1,0:T(8,128)(2,1)}, bf16[320,384]{1,0:T(8,128)(2,1)S(1)}) custom-call(s32[10]{0:T(128)S(1)} %pad_add_fusion.refs_0_, s32[8,1,640]{2,1,0:T(1,128)S(1)} %broadcast_in_dim.117.refs_1_, s32[4,320,1]{2,1,0:T(8,128)} %reshape_reshape.5.refs_2_, ...), custom_call_target="tpu_custom_call" | custom-call | flops 5033164800 | bytes 9830400 | tf_op jit(solution)/shard_map/block_attention/pallas_call | solution.py:149
  225.2 2.8 collective-permute-start.24
  229.3 12.9 %add_convert_fusion = bf16[1536,6144]{1,0:T(8,128)(2,1)} fusion(bf16[1536,6144]{1,0:T(8,128)(2,1)} %param.17, bf16[64,3840]{1,0:T(8,128)(2,1)} %get-tuple-element.50, bf16[64,3840]{1,0:T(8,128)(2,1)} %get-tuple-element.49), kind=kOutput, calls=%fused_computation.1 | convolution fusion | flops 1237843968 | bytes 38928384 | tf_op jit(solution)/shard_map/dot_general | solution.py:54
  243.2 4.4 %collective-permute-done.26 = bf16[320,384]{1,0:T(8,128)(2,1)S(1)} collective-permute-done((bf16[320,384]{1,0:T(8,128)(2,1)S(1)}, bf16[320,384]{1,0:T(8,128)(2,1)S(1)}, u32[]{:S(2)}, u32[]{:S(2)}) %collective-permute-start.26) | collective-permute-done | bytes 245792 | tf_op jit(solution)/shard_map/ppermute | solution.py:19
  247.9 2.8 fusion.29
  250.6 3.3 %fusion.26 = bf16[320,768]{1,0:T(8,128)(2,1)S(1)} fusion(bf16[1536,6144]{1,0:T(8,128)(2,1)} %add_convert_fusion, s32[]{:T(128)S(6)} %select_n.271, bf16[320,384]{1,0:T(8,128)(2,1)S(1)} %get-tuple-element.32, bf16[320,384]{1,0:T(8,128)(2,1)S(1)} %get-tuple-element.33, bf16[320,384]{1,0:T(8,128)(2,1)S(1)} %get-tuple-element.34, ...), kind=kOutput, calls=%fused_computation.25 | convolution fusion | flops 759152640 | bytes 3833860 | tf_op jit(solution)/shard_map/dot_general | solution.py:258
  260.5 3.3 %fusion = f32[320,3072]{1,0:T(8,128)S(1)} fusion(bf16[1536,6144]{1,0:T(8,128)(2,1)S(1)} %copy-done, s32[]{:T(128)S(6)} %select_n.268, bf16[320,384]{1,0:T(8,128)(2,1)S(1)} %get-tuple-element.32, bf16[320,384]{1,0:T(8,128)(2,1)S(1)} %get-tuple-element.33, bf16[320,384]{1,0:T(8,128)(2,1)S(1)} %get-tuple-element.34, bf16[320,384]{1,0:T(8,128)(2,1)S(1)} %get-tuple-element.31), kind=kOutput, calls=%fused_computation.5 | convolution fusion | flops 3023831040 | bytes 14352388 | tf_op jit(solution)/shard_map/dot_general | solution.py:261
  263.8 7.0 %collective-permute-done.33 = bf16[320,768]{1,0:T(8,128)(2,1)S(1)} collective-permute-done((bf16[320,768]{1,0:T(8,128)(2,1)S(1)}, bf16[320,768]{1,0:T(8,128)(2,1)S(1)}, u32[]{:S(2)}, u32[]{:S(2)}) %collective-permute-start.33) | collective-permute-done | bytes 491552 | tf_op jit(solution)/shard_map/ppermute | solution.py:259
  270.8 10.5 %collective-permute-done.34 = bf16[320,768]{1,0:T(8,128)(2,1)S(1)} collective-permute-done((bf16[320,768]{1,0:T(8,128)(2,1)S(1)}, bf16[320,768]{1,0:T(8,128)(2,1)S(1)}, u32[]{:S(2)}, u32[]{:S(2)}) %collective-permute-start.34) | collective-permute-done | bytes 491552 | tf_op jit(solution)/shard_map/ppermute | solution.py:259
  281.3 10.5 %collective-permute-done.35 = bf16[320,768]{1,0:T(8,128)(2,1)S(1)} collective-permute-done((bf16[320,768]{1,0:T(8,128)(2,1)S(1)}, bf16[320,768]{1,0:T(8,128)(2,1)S(1)}, u32[]{:S(2)}, u32[]{:S(2)}) %collective-permute-start.35) | collective-permute-done | bytes 491552 | tf_op jit(solution)/shard_map/ppermute | solution.py:259
  291.8 9.5 %collective-permute-done.36 = bf16[320,768]{1,0:T(8,128)(2,1)S(1)} collective-permute-done((bf16[320,768]{1,0:T(8,128)(2,1)S(1)}, bf16[320,768]{1,0:T(8,128)(2,1)S(1)}, u32[]{:S(2)}, u32[]{:S(2)}) %collective-permute-start.36) | collective-permute-done | bytes 491552 | tf_op jit(solution)/shard_map/ppermute | solution.py:259
  (123 shorter events, 46.4 us)
Async XLA Ops:
  6.5 102.5 %all-gather.2.cloned.1.call-start = ((), (), s32[]{:S(2)}) async-start(), calls=%async_computation | async-start | bytes 5898240 | tf_op jit(solution)/shard_map/all_gather | solution.py:205
  9.1 99.4 %collective-permute-start.10 = (bf16[640,384]{1,0:T(8,128)(2,1)S(1)}, bf16[640,384]{1,0:T(8,128)(2,1)S(1)}, u32[]{:S(2)}, u32[]{:S(2)}) collective-permute-start(bf16[640,384]{1,0:T(8,128)(2,1)S(1)} %pad_maximum_fusion.11.refs_7_), channel_id=1, source_target_pairs={{0,4},{2,6},{4,0},{6,2},{8,12},{10,14},{12,8},{14,10},{16,20},{18,... | collective-permute-start | bytes 1474568 | tf_op jit(solution)/shard_map/ppermute | solution.py:19
  9.4 99.3 %collective-permute-start.9 = (bf16[640,384]{1,0:T(8,128)(2,1)S(1)}, bf16[640,384]{1,0:T(8,128)(2,1)S(1)}, u32[]{:S(2)}, u32[]{:S(2)}) collective-permute-start(bf16[640,384]{1,0:T(8,128)(2,1)S(1)} %pad_maximum_fusion.11.refs_7_), channel_id=1, source_target_pairs={{0,2},{2,0},{4,6},{6,4},{8,10},{10,8},{12,14},{14,12},{16,18},{18,... | collective-permute-start | bytes 1474568 | tf_op jit(solution)/shard_map/ppermute | solution.py:19
  12.6 18.1 %collective-permute-start.27 = (bf16[64,3840]{1,0:T(8,128)(2,1)}, bf16[64,3840]{1,0:T(8,128)(2,1)}, u32[]{:S(2)}, u32[]{:S(2)}) collective-permute-start(bf16[64,3840]{1,0:T(8,128)(2,1)} %broadcast_select_fusion.2), channel_id=1, source_target_pairs={{0,2},{2,0},{4,6},{6,4},{8,10},{10,8},{12,14},{14,12},{16,18},{18,... | collective-permute-start | bytes 1474568 | tf_op jit(solution)/shard_map/ppermute | solution.py:19
  14.5 14.7 %collective-permute-start = (bf16[64,3840]{1,0:T(8,128)(2,1)}, bf16[64,3840]{1,0:T(8,128)(2,1)}, u32[]{:S(2)}, u32[]{:S(2)}) collective-permute-start(bf16[64,3840]{1,0:T(8,128)(2,1)} %broadcast_select_fusion.5), channel_id=1, source_target_pairs={{0,2},{2,0},{4,6},{6,4},{8,10},{10,8},{12,14},{14,12},{16,18},{18,... | collective-permute-start | bytes 1474568 | tf_op jit(solution)/shard_map/ppermute | solution.py:19
  15.8 89.1 %collective-permute-start.16 = (bf16[640,384]{1,0:T(8,128)(2,1)}, bf16[640,384]{1,0:T(8,128)(2,1)}, u32[]{:S(2)}, u32[]{:S(2)}) collective-permute-start(bf16[640,384]{1,0:T(8,128)(2,1)} %pad_maximum_fusion.13), channel_id=1, source_target_pairs={{0,16},{2,18},{4,20},{6,22},{8,24},{10,26},{12,28},{14,30},{16,0},... | collective-permute-start | bytes 1474568 | tf_op jit(solution)/shard_map/ppermute | solution.py:19
  29.1 78.8 %collective-permute-start.12 = (bf16[640,384]{1,0:T(8,128)(2,1)S(1)}, bf16[640,384]{1,0:T(8,128)(2,1)S(1)}, u32[]{:S(2)}, u32[]{:S(2)}) collective-permute-start(bf16[640,384]{1,0:T(8,128)(2,1)S(1)} %pad_maximum_fusion.12), channel_id=1, source_target_pairs={{0,8},{2,10},{4,12},{6,14},{8,0},{10,2},{12,4},{14,6},{16,24},{18,... | collective-permute-start | bytes 1474568 | tf_op jit(solution)/shard_map/ppermute | solution.py:19
  42.4 11.9 %collective-permute-start.2 = (bf16[64,1920]{1,0:T(8,128)(2,1)S(1)}, bf16[64,1920]{1,0:T(8,128)(2,1)S(1)}, u32[]{:S(2)}, u32[]{:S(2)}) collective-permute-start(bf16[64,1920]{1,0:T(8,128)(2,1)S(1)} %select_select_fusion.3), channel_id=1, source_target_pairs={{0,8},{2,10},{4,12},{6,14},{8,0},{10,2},{12,4},{14,6},{16,24},{18,... | collective-permute-start | bytes 737288 | tf_op jit(solution)/shard_map/ppermute | solution.py:19
  54.3 8.4 %collective-permute-start.29 = (bf16[64,1920]{1,0:T(8,128)(2,1)S(1)}, bf16[64,1920]{1,0:T(8,128)(2,1)S(1)}, u32[]{:S(2)}, u32[]{:S(2)}) collective-permute-start(bf16[64,1920]{1,0:T(8,128)(2,1)S(1)} %select_select_fusion.2), channel_id=1, source_target_pairs={{0,8},{2,10},{4,12},{6,14},{8,0},{10,2},{12,4},{14,6},{16,24},{18,... | collective-permute-start | bytes 737288 | tf_op jit(solution)/shard_map/ppermute | solution.py:19
  62.7 12.2 %collective-permute-start.3 = (bf16[64,1920]{1,0:T(8,128)(2,1)S(1)}, bf16[64,1920]{1,0:T(8,128)(2,1)S(1)}, u32[]{:S(2)}, u32[]{:S(2)}) collective-permute-start(bf16[64,1920]{1,0:T(8,128)(2,1)S(1)} %broadcast_select_fusion.8), channel_id=1, source_target_pairs={{0,16},{2,18},{4,20},{6,22},{8,24},{10,26},{12,28},{14,30},{16,0},... | collective-permute-start | bytes 737288 | tf_op jit(solution)/shard_map/ppermute | solution.py:19
  74.9 13.7 %collective-permute-start.30 = (bf16[64,1920]{1,0:T(8,128)(2,1)S(1)}, bf16[64,1920]{1,0:T(8,128)(2,1)S(1)}, u32[]{:S(2)}, u32[]{:S(2)}) collective-permute-start(bf16[64,1920]{1,0:T(8,128)(2,1)S(1)} %broadcast_select_fusion.6), channel_id=1, source_target_pairs={{0,16},{2,18},{4,20},{6,22},{8,24},{10,26},{12,28},{14,30},{16,0},... | collective-permute-start | bytes 737288 | tf_op jit(solution)/shard_map/ppermute | solution.py:19
  104.9 23.7 %collective-permute-start.20 = (bf16[640,384]{1,0:T(8,128)(2,1)}, bf16[640,384]{1,0:T(8,128)(2,1)}, u32[]{:S(2)}, u32[]{:S(2)}) collective-permute-start(bf16[640,384]{1,0:T(8,128)(2,1)} %pad_maximum_fusion.14), channel_id=1, source_target_pairs={{0,24},{2,26},{4,28},{6,30},{8,16},{10,18},{12,20},{14,22},{16,8},... | collective-permute-start | bytes 1474568 | tf_op jit(solution)/shard_map/ppermute | solution.py:19
  105.4 24.4 %collective-permute-start.18 = (bf16[640,384]{1,0:T(8,128)(2,1)}, bf16[640,384]{1,0:T(8,128)(2,1)}, u32[]{:S(2)}, u32[]{:S(2)}) collective-permute-start(bf16[640,384]{1,0:T(8,128)(2,1)} %collective-permute-done.16.refs_15_), channel_id=1, source_target_pairs={{0,4},{2,6},{4,0},{6,2},{8,12},{10,14},{12,8},{14,10},{16,20},{18,... | collective-permute-start | bytes 1474568 | tf_op jit(solution)/shard_map/ppermute | solution.py:19
  107.9 23.0 %collective-permute-start.17 = (bf16[640,384]{1,0:T(8,128)(2,1)}, bf16[640,384]{1,0:T(8,128)(2,1)}, u32[]{:S(2)}, u32[]{:S(2)}) collective-permute-start(bf16[640,384]{1,0:T(8,128)(2,1)} %collective-permute-done.16.refs_15_), channel_id=1, source_target_pairs={{0,2},{2,0},{4,6},{6,4},{8,10},{10,8},{12,14},{14,12},{16,18},{18,... | collective-permute-start | bytes 1474568 | tf_op jit(solution)/shard_map/ppermute | solution.py:19
  108.5 22.5 %collective-permute-start.14 = (bf16[640,384]{1,0:T(8,128)(2,1)S(1)}, bf16[640,384]{1,0:T(8,128)(2,1)S(1)}, u32[]{:S(2)}, u32[]{:S(2)}) collective-permute-start(bf16[640,384]{1,0:T(8,128)(2,1)S(1)} %collective-permute-done.12.refs_11_), channel_id=1, source_target_pairs={{0,4},{2,6},{4,0},{6,2},{8,12},{10,14},{12,8},{14,10},{16,20},{18,... | collective-permute-start | bytes 1474568 | tf_op jit(solution)/shard_map/ppermute | solution.py:19
  108.7 22.8 %collective-permute-start.13 = (bf16[640,384]{1,0:T(8,128)(2,1)S(1)}, bf16[640,384]{1,0:T(8,128)(2,1)S(1)}, u32[]{:S(2)}, u32[]{:S(2)}) collective-permute-start(bf16[640,384]{1,0:T(8,128)(2,1)S(1)} %collective-permute-done.12.refs_11_), channel_id=1, source_target_pairs={{0,2},{2,0},{4,6},{6,4},{8,10},{10,8},{12,14},{14,12},{16,18},{18,... | collective-permute-start | bytes 1474568 | tf_op jit(solution)/shard_map/ppermute | solution.py:19
  128.6 22.2 %collective-permute-start.22 = (bf16[640,384]{1,0:T(8,128)(2,1)}, bf16[640,384]{1,0:T(8,128)(2,1)}, u32[]{:S(2)}, u32[]{:S(2)}) collective-permute-start(bf16[640,384]{1,0:T(8,128)(2,1)} %collective-permute-done.20.refs_19_), channel_id=1, source_target_pairs={{0,4},{2,6},{4,0},{6,2},{8,12},{10,14},{12,8},{14,10},{16,20},{18,... | collective-permute-start | bytes 1474568 | tf_op jit(solution)/shard_map/ppermute | solution.py:19
  129.9 21.1 %collective-permute-start.21 = (bf16[640,384]{1,0:T(8,128)(2,1)}, bf16[640,384]{1,0:T(8,128)(2,1)}, u32[]{:S(2)}, u32[]{:S(2)}) collective-permute-start(bf16[640,384]{1,0:T(8,128)(2,1)} %collective-permute-done.20.refs_19_), channel_id=1, source_target_pairs={{0,2},{2,0},{4,6},{6,4},{8,10},{10,8},{12,14},{14,12},{16,18},{18,... | collective-permute-start | bytes 1474568 | tf_op jit(solution)/shard_map/ppermute | solution.py:19
  130.9 19.5 %collective-permute-start.11 = (bf16[640,384]{1,0:T(8,128)(2,1)S(1)}, bf16[640,384]{1,0:T(8,128)(2,1)}, u32[]{:S(2)}, u32[]{:S(2)}) collective-permute-start(bf16[640,384]{1,0:T(8,128)(2,1)S(1)} %collective-permute-done.10.refs_9_), channel_id=1, source_target_pairs={{0,2},{2,0},{4,6},{6,4},{8,10},{10,8},{12,14},{14,12},{16,18},{18,... | collective-permute-start | bytes 1474568 | tf_op jit(solution)/shard_map/ppermute | solution.py:19
  131.0 20.6 %collective-permute-start.19 = (bf16[640,384]{1,0:T(8,128)(2,1)}, bf16[640,384]{1,0:T(8,128)(2,1)}, u32[]{:S(2)}, u32[]{:S(2)}) collective-permute-start(bf16[640,384]{1,0:T(8,128)(2,1)} %collective-permute-done.18.refs_17_), channel_id=1, source_target_pairs={{0,2},{2,0},{4,6},{6,4},{8,10},{10,8},{12,14},{14,12},{16,18},{18,... | collective-permute-start | bytes 1474568 | tf_op jit(solution)/shard_map/ppermute | solution.py:19
  131.5 24.4 %collective-permute-start.32 = (bf16[64,3840]{1,0:T(8,128)(2,1)}, bf16[64,3840]{1,0:T(8,128)(2,1)}, u32[]{:S(2)}, u32[]{:S(2)}) collective-permute-start(bf16[64,3840]{1,0:T(8,128)(2,1)} %pad_maximum_fusion.15), channel_id=1, source_target_pairs={{0,2},{2,0},{4,6},{6,4},{8,10},{10,8},{12,14},{14,12},{16,18},{18,... | collective-permute-start | bytes 1474568 | tf_op jit(solution)/shard_map/ppermute | solution.py:19
  150.4 7.6 %collective-permute-start.15 = (bf16[640,384]{1,0:T(8,128)(2,1)S(1)}, bf16[640,384]{1,0:T(8,128)(2,1)S(1)}, u32[]{:S(2)}, u32[]{:S(2)}) collective-permute-start(bf16[640,384]{1,0:T(8,128)(2,1)S(1)} %collective-permute-done.14.refs_13_), channel_id=1, source_target_pairs={{0,2},{2,0},{4,6},{6,4},{8,10},{10,8},{12,14},{14,12},{16,18},{18,... | collective-permute-start | bytes 1474568 | tf_op jit(solution)/shard_map/ppermute | solution.py:19
  151.0 17.8 %collective-permute-start.8 = (bf16[320,384]{1,0:T(8,128)(2,1)S(1)}, bf16[320,384]{1,0:T(8,128)(2,1)S(1)}, u32[]{:S(2)}, u32[]{:S(2)}) collective-permute-start(bf16[320,384]{1,0:T(8,128)(2,1)S(1)} %get-tuple-element.43), channel_id=1, source_target_pairs={{0,24},{2,26},{4,28},{6,30},{8,16},{10,18},{12,20},{14,22},{16,8},... | collective-permute-start | bytes 737288 | tf_op jit(solution)/shard_map/ppermute | solution.py:19
  151.6 20.8 %collective-permute-start.7 = (bf16[320,384]{1,0:T(8,128)(2,1)S(1)}, bf16[320,384]{1,0:T(8,128)(2,1)S(1)}, u32[]{:S(2)}, u32[]{:S(2)}) collective-permute-start(bf16[320,384]{1,0:T(8,128)(2,1)S(1)} %get-tuple-element.44), channel_id=1, source_target_pairs={{0,16},{2,18},{4,20},{6,22},{8,24},{10,26},{12,28},{14,30},{16,0},... | collective-permute-start | bytes 737288 | tf_op jit(solution)/shard_map/ppermute | solution.py:19
  155.9 16.6 %collective-permute-start.6 = (bf16[320,384]{1,0:T(8,128)(2,1)S(1)}, bf16[320,384]{1,0:T(8,128)(2,1)S(1)}, u32[]{:S(2)}, u32[]{:S(2)}) collective-permute-start(bf16[320,384]{1,0:T(8,128)(2,1)S(1)} %get-tuple-element.45), channel_id=1, source_target_pairs={{0,8},{2,10},{4,12},{6,14},{8,0},{10,2},{12,4},{14,6},{16,24},{18,... | collective-permute-start | bytes 737288 | tf_op jit(solution)/shard_map/ppermute | solution.py:19
  225.2 17.0 %collective-permute-start.24 = (bf16[320,384]{1,0:T(8,128)(2,1)}, bf16[320,384]{1,0:T(8,128)(2,1)S(1)}, u32[]{:S(2)}, u32[]{:S(2)}) collective-permute-start(bf16[320,384]{1,0:T(8,128)(2,1)} %get-tuple-element.10), channel_id=1, source_target_pairs={{0,8},{2,10},{4,12},{6,14},{8,0},{10,2},{12,4},{14,6},{16,24},{18,... | collective-permute-start | bytes 737288 | tf_op jit(solution)/shard_map/ppermute | solution.py:19
  228.0 15.1 %collective-permute-start.25 = (bf16[320,384]{1,0:T(8,128)(2,1)}, bf16[320,384]{1,0:T(8,128)(2,1)S(1)}, u32[]{:S(2)}, u32[]{:S(2)}) collective-permute-start(bf16[320,384]{1,0:T(8,128)(2,1)} %get-tuple-element.11), channel_id=1, source_target_pairs={{0,16},{2,18},{4,20},{6,22},{8,24},{10,26},{12,28},{14,30},{16,0},... | collective-permute-start | bytes 737288 | tf_op jit(solution)/shard_map/ppermute | solution.py:19
  228.4 19.1 %collective-permute-start.26 = (bf16[320,384]{1,0:T(8,128)(2,1)S(1)}, bf16[320,384]{1,0:T(8,128)(2,1)S(1)}, u32[]{:S(2)}, u32[]{:S(2)}) collective-permute-start(bf16[320,384]{1,0:T(8,128)(2,1)S(1)} %get-tuple-element.12), channel_id=1, source_target_pairs={{0,24},{2,26},{4,28},{6,30},{8,16},{10,18},{12,20},{14,22},{16,8},... | collective-permute-start | bytes 737288 | tf_op jit(solution)/shard_map/ppermute | solution.py:19
  257.5 13.3 %collective-permute-start.33 = (bf16[320,768]{1,0:T(8,128)(2,1)S(1)}, bf16[320,768]{1,0:T(8,128)(2,1)S(1)}, u32[]{:S(2)}, u32[]{:S(2)}) collective-permute-start(bf16[320,768]{1,0:T(8,128)(2,1)S(1)} %fusion.20), channel_id=1, source_target_pairs={{0,1},{1,0},{2,3},{3,2},{4,5},{5,4},{6,7},{7,6},{8,9},{9,8},{10,11... | collective-permute-start | bytes 1474568 | tf_op jit(solution)/shard_map/ppermute | solution.py:259
  258.5 22.7 %collective-permute-start.34 = (bf16[320,768]{1,0:T(8,128)(2,1)S(1)}, bf16[320,768]{1,0:T(8,128)(2,1)S(1)}, u32[]{:S(2)}, u32[]{:S(2)}) collective-permute-start(bf16[320,768]{1,0:T(8,128)(2,1)S(1)} %fusion.23), channel_id=1, source_target_pairs={{0,1},{1,0},{2,3},{3,2},{4,5},{5,4},{6,7},{7,6},{8,9},{9,8},{10,11... | collective-permute-start | bytes 1474568 | tf_op jit(solution)/shard_map/ppermute | solution.py:259
  259.0 32.8 %collective-permute-start.35 = (bf16[320,768]{1,0:T(8,128)(2,1)S(1)}, bf16[320,768]{1,0:T(8,128)(2,1)S(1)}, u32[]{:S(2)}, u32[]{:S(2)}) collective-permute-start(bf16[320,768]{1,0:T(8,128)(2,1)S(1)} %fusion.26), channel_id=1, source_target_pairs={{0,1},{1,0},{2,3},{3,2},{4,5},{5,4},{6,7},{7,6},{8,9},{9,8},{10,11... | collective-permute-start | bytes 1474568 | tf_op jit(solution)/shard_map/ppermute | solution.py:259
  260.0 41.3 %collective-permute-start.36 = (bf16[320,768]{1,0:T(8,128)(2,1)S(1)}, bf16[320,768]{1,0:T(8,128)(2,1)S(1)}, u32[]{:S(2)}, u32[]{:S(2)}) collective-permute-start(bf16[320,768]{1,0:T(8,128)(2,1)S(1)} %fusion.29), channel_id=1, source_target_pairs={{0,1},{1,0},{2,3},{3,2},{4,5},{5,4},{6,7},{7,6},{8,9},{9,8},{10,11... | collective-permute-start | bytes 1474568 | tf_op jit(solution)/shard_map/ppermute | solution.py:259
  (15 other events, 102.1 us)
Sparse Core Ops, SparseCore 0:
  10.5 54.5 all-gather.1

commit v2 on v1

v2 whole, which is shorter than its diff:
```python
import functools

import jax
import jax.numpy as jnp
from jax import lax
from jax.experimental import pallas as pl
from jax.experimental.pallas import tpu as pltpu
from jax.sharding import PartitionSpec as P

HS = 128
FTOK = 64
norm_eps = 1e-06
masked_score = -1e30
LOG2E = 1.4426950408889634


def swap(x, bit):
    n = lax.axis_size("ctx")
    return lax.ppermute(x, "ctx", [(i, i ^ bit) for i in range(n)])


def fetch_pair(down, up, down_owner, up_owner, hold=None):
    n = lax.axis_size("ctx")
    me = lax.axis_index("ctx")
    cols = down.shape[0]
    buf = jnp.concatenate([down.T, up], axis=1)
    owner = jnp.where(jnp.arange(buf.shape[1]) < cols, down_owner, up_owner)[None, :]
    halved = []
    bit = 1
    while bit < n:
        high = (me & bit) != 0
        if bit <= 2:
            half = buf.shape[1] // 2
            low_part, high_part = buf[:, :half], buf[:, half:]
            received = swap(jnp.where(high, low_part, high_part), bit)
            kept = jnp.where(high, high_part, low_part)
            owner = jnp.where(high, owner[:, half:], owner[:, :half])
            halved.append(bit)
        else:
            if hold is not None:
                buf, _ = lax.optimization_barrier((buf, hold))
                hold = None
            received = swap(buf, bit)
            kept = buf
        buf = jnp.where((owner & bit) == (me & bit), kept, received)
        bit *= 2
    part = buf
    for bit in reversed(halved):
        high = (me & bit) != 0
        other = swap(buf, bit)
        buf = jnp.concatenate(
            [jnp.where(high, other, buf), jnp.where(high, buf, other)], axis=1
        )
    return buf[:, :cols], buf[:, cols:], part


def merge_weight(base, down_t, up):
    product = lax.dot_general(
        down_t, up, (((0,), (0,)), ((), ())), preferred_element_type=jnp.float32
    )
    return (base.astype(jnp.float32) + product).astype(jnp.bfloat16)


def attention_kernel(n, heads, rows, *refs):
    info, kid, qid, q_in = refs[:4]
    kv_in = refs[4 : 4 + n]
    out, kv_buf, top, total, acc, kv_sem = refs[4 + n :]
    for i in range(n):
        pltpu.make_async_copy(kv_in[i], kv_buf.at[i], kv_sem.at[i]).start()
    top[...] = jnp.full(top.shape, masked_score, jnp.float32)
    total[...] = jnp.zeros(total.shape, jnp.float32)
    acc[...] = jnp.zeros(acc.shape, jnp.float32)
    mine = info[2]
    rate = HS ** (-0.5) * LOG2E

    def slots_of(c):
        return (2 * c) ^ mine, (2 * c + 1) ^ mine

    def arrived(c):
        for s in slots_of(c):
            pltpu.make_async_copy(kv_buf.at[s], kv_buf.at[s], kv_sem.at[s]).wait()

    def chunk(c, masked):
        slots = slots_of(c)
        if masked:
            seen = kid[c] <= qid[...]

        def score(h):
            cut = slice(h * HS, (h + 1) * HS)
            k = jnp.concatenate([kv_buf[s, :rows, cut] for s in slots], axis=0)
            scores = lax.dot_general(
                q_in[:, cut], k, (((1,), (1,)), ((), ())), preferred_element_type=jnp.float32
            )
            return jnp.where(seen, scores, masked_score) if masked else scores

        following = score(0)
        for h in range(heads):
            scores = following
            if h + 1 < heads:
                following = score(h + 1)
            cut = slice(h * HS, (h + 1) * HS)
            v = jnp.concatenate([kv_buf[s, rows:, cut] for s in slots], axis=0)
            old = top[h]
            new = jnp.maximum(old, jnp.max(scores, axis=1, keepdims=True))
            weights = jnp.exp2((scores - new[:, :1]) * rate)
            factor = jnp.exp2((old - new) * rate)
            lanes = weights[:, :HS]
            for j in range(1, 2 * rows // HS):
                lanes = lanes + weights[:, j * HS : (j + 1) * HS]
            top[h] = new
            total[h] = total[h] * factor + lanes
            acc[h] = acc[h] * factor + jnp.dot(
                weights.astype(jnp.bfloat16), v, preferred_element_type=jnp.float32
            )

    def plain(c, carry):
        arrived(c)
        chunk(c, False)
        return carry

    def edge(c, carry):
        arrived(c)
        chunk(c, True)
        return carry

    def unused(c, carry):
        arrived(c)
        return carry

    lax.fori_loop(0, info[0], plain, 0)
    lax.fori_loop(info[0], info[1], edge, 0)
    lax.fori_loop(info[1], n // 2, unused, 0)
    for h in range(heads):
        out[:, h * HS : (h + 1) * HS] = (
            acc[h] / jnp.sum(total[h], axis=1, keepdims=True)
        ).astype(jnp.bfloat16)


def attend(q_part, kv_parts, q_rank, frame_block_number):
    rows, width = q_part.shape
    heads = width // HS
    n = len(kv_parts)
    frames = rows // FTOK
    chunk_frames = 2 * frames
    own = lax.dynamic_slice_in_dim(frame_block_number, q_rank * frames, frames, 0)
    full = jnp.sum(frame_block_number <= own[0]) // chunk_frames
    some = (jnp.sum(frame_block_number <= own[-1]) + chunk_frames - 1) // chunk_frames
    info = jnp.stack([full, some, lax.axis_index("ctx")]).astype(jnp.int32)
    kid = jnp.repeat(frame_block_number, FTOK).reshape(n // 2, 1, 2 * rows)
    qid = jnp.repeat(own, FTOK).reshape(rows, 1)
    bf16, f32 = jnp.bfloat16, jnp.float32
    vmem = pl.BlockSpec(memory_space=pltpu.VMEM)
    return pl.pallas_call(
        functools.partial(attention_kernel, n, heads, rows),
        out_shape=jax.ShapeDtypeStruct((rows, width), bf16),
        in_specs=[pl.BlockSpec(memory_space=pltpu.SMEM), vmem, vmem, vmem]
        + [pl.BlockSpec(memory_space=pl.ANY)] * n,
        out_specs=vmem,
        scratch_shapes=[
            pltpu.VMEM((n, 2 * rows, width), bf16),
            pltpu.VMEM((heads, rows, HS), f32),
            pltpu.VMEM((heads, rows, HS), f32),
            pltpu.VMEM((heads, rows, HS), f32),
            pltpu.SemaphoreType.DMA((n,)),
        ],
        compiler_params=pltpu.CompilerParams(vmem_limit_bytes=40 * 2**20),
        cost_estimate=pl.CostEstimate(
            flops=4 * rows * n * rows * width,
            bytes_accessed=(2 * n + 2) * rows * width * 2,
            transcendentals=rows * n * rows * heads // 2,
        ),
        name="block_attention",
    )(info, kid, qid, q_part, *kv_parts)


def shards(
    tokens,
    norm_gain_vector,
    keys,
    values,
    query_frozen_weight,
    output_frozen_weight,
    query_update_first,
    query_update_second,
    output_update_first,
    output_update_second,
    owners,
    frame_block_number,
):
    n, tp = lax.axis_size("ctx"), lax.axis_size("tp")
    me, mine = lax.axis_index("ctx"), lax.axis_index("tp")
    local_heads = keys.shape[1] // HS
    groups = next(g for g in (4, 2, 1) if local_heads % g == 0 and n % (2 * g) == 0)
    ranks = n // groups
    width = keys.shape[1] // groups
    my_group = me // ranks

    def columns(x, step):
        return lax.dynamic_slice_in_dim(x, (my_group ^ step) * width, width, 1)

    gain = lax.all_gather(norm_gain_vector, "tp", axis=0, tiled=True)
    query_down_t, query_up, fetched = fetch_pair(
        query_update_first[0], query_update_second[0], owners[0], owners[1]
    )
    whole = lax.all_gather(tokens, "tp", axis=1, tiled=True)

    held_keys, held_values, _ = lax.optimization_barrier((keys, values, fetched))
    kv_parts = []
    for step in range(groups):
        part = jnp.concatenate([columns(held_keys, step), columns(held_values, step)], axis=0)
        if step:
            part = swap(part, step * ranks)
        have = {0: part}
        bit = ranks // 2
        while bit:
            have.update({j | bit: swap(x, bit) for j, x in list(have.items())})
            bit //= 2
        kv_parts += [have[j] for j in range(ranks)]

    features = whole.astype(jnp.float32)
    mean_square = jnp.mean(features * features, axis=-1, keepdims=True)
    normed = (features * lax.rsqrt(mean_square + norm_eps) * gain.astype(jnp.float32)).astype(
        jnp.bfloat16
    )
    query_merged = merge_weight(query_frozen_weight, query_down_t, query_up)
    queries = jnp.dot(normed, query_merged, preferred_element_type=jnp.float32).astype(jnp.bfloat16)

    q_parts = []
    for step in range(groups):
        part = columns(queries, step)
        q_parts.append(swap(part, step * ranks) if step else part)

    out_down_t, out_up, _ = fetch_pair(
        output_update_first[0],
        output_update_second[0],
        owners[2],
        owners[3],
        hold=tuple(q_parts),
    )

    order = list(range(1, groups)) + [0]
    o_parts = [None] * groups
    gate = None
    for step in order:
        q_part = q_parts[step]
        if gate is not None:
            q_part, _ = lax.optimization_barrier((q_part, gate))
        gate = attend(q_part, kv_parts, (my_group ^ step) * ranks + me % ranks, frame_block_number)
        o_parts[step] = swap(gate, step * ranks) if step else gate
    out_merged = merge_weight(output_frozen_weight, out_down_t, out_up)
    stacked = jnp.stack(o_parts)
    attended = jnp.concatenate(
        [lax.dynamic_index_in_dim(stacked, my_group ^ g, 0, keepdims=False) for g in range(groups)],
        axis=1,
    )
    if tp != 2:
        partial_value = jnp.dot(attended, out_merged, preferred_element_type=jnp.float32)
        return lax.psum_scatter(
            partial_value.astype(jnp.bfloat16), "tp", scatter_dimension=1, tiled=True
        )
    half = out_merged.shape[1] // 2
    pieces = 4
    step = half // pieces
    received = []
    for i in range(pieces):
        theirs = lax.dynamic_slice_in_dim(out_merged, (1 - mine) * half + i * step, step, 1)
        product = jnp.dot(attended, theirs, preferred_element_type=jnp.float32)
        received.append(lax.ppermute(product.astype(jnp.bfloat16), "tp", [(0, 1), (1, 0)]))
    own = lax.dynamic_slice_in_dim(out_merged, mine * half, half, 1)
    product = jnp.dot(attended, own, preferred_element_type=jnp.float32)
    return jnp.concatenate(
        [
            (product[:, i * step : (i + 1) * step] + received[i].astype(jnp.float32)).astype(
                jnp.bfloat16
            )
            for i in range(pieces)
        ],
        axis=1,
    )


def solution(mesh):
    in_specs = (
        P("ctx", "tp"),
        P("tp"),
        P("ctx", "tp"),
        P("ctx", "tp"),
        P(None, "tp"),
        P("tp", None),
        P("ctx", None, None),
        P("ctx", None, "tp"),
        P("ctx", "tp", None),
        P("ctx", None, None),
        P(),
        P(),
    )
    out_specs = P("ctx", "tp")
    return jax.shard_map(shards, mesh=mesh, in_specs=in_specs, out_specs=out_specs, check_vma=False)
```

time: 311 us -> 286 us (0.920)
  the two profiles are of different devices: /device:TPU:13 before, /device:TPU:28 now
where the time goes in v2:
time: 286 us; the launch traced here: 283 us
  waiting for transfers between devices  91.7 us (32%)
  Pallas kernels  50.9 us (18%)
  matrix products  43.7 us (15%)
  starting transfers between devices  35.1 us (12%)
  other arithmetic  25.6 us (9%)
  between operations  24.3 us (8%)
  local copies, waits for them, and re-layouts  7.14 us (2%)
  blocking collectives  4.45 us (2%)
    pallas_call x4, Pallas kernels, attend(): pl.pallas_call(functools.partial(attention_kernel, n, heads, rows), out_s...  50.9 us
    ppermute x33, waiting for transfers between devices, swap(): return lax.ppermute(x, 'ctx', [(i, i ^ bit) for i in range(n)])  43.9 us
    ppermute x4, waiting for transfers between devices, shards(): lax.ppermute(product.astype(jnp.bfloat16), 'tp', [(0, 1), (1, 0)])  37.5 us
    ppermute x33, starting transfers between devices, swap(): return lax.ppermute(x, 'ctx', [(i, i ^ bit) for i in range(n)])  30.9 us
    dot_general x1, matrix products, shards(): jnp.dot(normed, query_merged, preferred_element_type=jnp.float32)  17.3 us
    dot_general x1, matrix products, merge_weight(): lax.dot_general(down_t, up, (((0,), (0,)), ((), ())), preferred_element_t...  12.8 us
    dot_general x4, matrix products, shards(): product = jnp.dot(attended, theirs, preferred_element_type=jnp.float32)  10.3 us
    all_gather x1, waiting for transfers between devices, shards(): whole = lax.all_gather(tokens, 'tp', axis=1, tiled=True)  9.64 us
  transfers between devices with their start and end apart: 38, of which 12 were waited for; matrix products, arithmetic and copies ran while one was open for 17% of the time, Pallas kernels for 18%

profile of v2, /device:TPU:28, one launch (start us, length us, event | category | flops | bytes accessed | tf_op | source)
XLA Modules:
  0.0 282.8 jit_solution(16151720063835581587)
XLA Ops:
  7.7 1.8 broadcast_select_fusion.2
  14.4 6.0 %collective-permute-done.1 = bf16[64,1920]{1,0:T(8,128)(2,1)S(1)} collective-permute-done((bf16[64,1920]{1,0:T(8,128)(2,1)S(1)}, bf16[64,1920]{1,0:T(8,128)(2,1)S(1)}, u32[]{:S(2)}, u32[]{:S(2)}) %collective-permute-start.1) | collective-permute-done | bytes 245792 | tf_op jit(solution)/shard_map/ppermute | solution.py:19
  21.9 4.4 %all_gather.7 = bf16[6144]{0:T(1024)(128)(2,1)S(1)} all-gather(bf16[3072]{0:T(1024)(128)(2,1)S(1)} %copy-done.14), channel_id=1, replica_groups=mesh['ctx'=16,'tp'=2] {'tp'}, dimensions={0}, use_global_device_ids=true | all-gather | bytes 18432 | tf_op jit(solution)/shard_map/all_gather | solution.py:201
  29.3 10.7 %collective-permute-done.3 = bf16[64,1920]{1,0:T(8,128)(2,1)S(1)} collective-permute-done((bf16[64,1920]{1,0:T(8,128)(2,1)S(1)}, bf16[64,1920]{1,0:T(8,128)(2,1)S(1)}, u32[]{:S(2)}, u32[]{:S(2)}) %collective-permute-start.3) | collective-permute-done | bytes 245792 | tf_op jit(solution)/shard_map/ppermute | solution.py:19
  43.0 5.8 %collective-permute-done.4 = bf16[64,1920]{1,0:T(8,128)(2,1)S(1)} collective-permute-done((bf16[64,1920]{1,0:T(8,128)(2,1)S(1)}, bf16[64,1920]{1,0:T(8,128)(2,1)S(1)}, u32[]{:S(2)}, u32[]{:S(2)}) %collective-permute-start.4) | collective-permute-done | bytes 245792 | tf_op jit(solution)/shard_map/ppermute | solution.py:19
  54.2 9.6 %all-gather.2.cloned.1.call-done = bf16[320,6144]{1,0:T(8,128)(2,1)} async-done(((bf16[320,3072]{1,0:T(8,128)(2,1)}), bf16[320,6144]{1,0:T(8,128)(2,1)}) %all-gather.2.cloned.1.call-update) | async-done | bytes 3932176 | tf_op jit(solution)/shard_map/all_gather | solution.py:205
  63.8 3.0 %fusion.2 = f32[320]{0:T(512)S(1)} fusion(bf16[320,6144]{1,0:T(8,128)(2,1)} %all-gather.2.cloned.1.call-done), kind=kLoop, calls=%fused_computation.6 | loop fusion | flops 5897920 | bytes 3933440 | tf_op jit(solution)/shard_map/reduce_sum | solution.py:221
  67.4 17.3 %fusion.9 = bf16[320,1536]{1,0:T(8,128)(2,1)} fusion(bf16[6144,1536]{1,0:T(8,128)(2,1)} %param.16, bf16[320,6144]{1,0:T(8,128)(2,1)} %all-gather.2.cloned.1.call-done, f32[6144]{0:T(1024)S(1)} %convert_element_type.87, f32[320]{0:T(512)S(1)} %add_rsqrt_fusion, bf16[64,3840]{1,0:T(8,128)(2,1)} %get-tuple-element.58, bf16[64,3840]{1,0:T(8,128)(2,1)} %get-tuple-element.57), kind=kOutput, calls=%fused_computation.12 | convolution fusion | flops 7285997568 | bytes 24995072 | tf_op jit(solution)/shard_map/dot_general | solution.py:226
  84.7 2.2 constant_dynamic-slice_fusion.10
  86.9 3.3 %collective-permute-start.6 = (bf16[320,384]{1,0:T(8,128)(2,1)}, bf16[320,384]{1,0:T(8,128)(2,1)}, u32[]{:S(2)}, u32[]{:S(2)}) collective-permute-start(bf16[320,384]{1,0:T(8,128)(2,1)} %get-tuple-element.53), channel_id=1, source_target_pairs={{0,24},{2,26},{4,28},{6,30},{8,16},{10,18},{12,20},{14,22},{16,8},... | collective-permute-start | bytes 737288 | tf_op jit(solution)/shard_map/ppermute | solution.py:19
  92.6 5.8 %fusion.47 = (s32[]{:T(128)}, s32[]{:T(128)}, s32[]{:T(128)}, s32[]{:T(128)}, s32[]{:T(128)}, /*index=5*/s32[]{:T(128)}, s32[]{:T(128)}, s32[]{:T(128)}) fusion(s32[80]{0:T(128)S(1)} %copy-done.12, s32[]{:T(128)} %bitcast, s32[]{:T(128)} %bitcast.17, s32[]{:T(128)} %bitcast.15, s32[]{:T(128)} %bitcast.13, s32[]{:T(128)} %bitcast.11, s32[]{:T(128)} %bitcast.2, ...), kind=kLoop, calls=%fused_computation.114 | loop fusion | flops 1912 | bytes 384 | tf_op jit(solution)/shard_map/reduce_sum | solution.py:146
  103.1 15.9 %collective-permute-done.7.refs_3_ = bf16[320,384]{1,0:T(8,128)(2,1)} collective-permute-done((bf16[320,384]{1,0:T(8,128)(2,1)}, bf16[320,384]{1,0:T(8,128)(2,1)}, u32[]{:S(2)}, u32[]{:S(2)}) %collective-permute-start.7) | collective-permute-done | bytes 245792 | tf_op jit(solution)/shard_map/ppermute | solution.py:19
  130.3 1.7 collective-permute-done.22.refs_18_
  132.4 1.7 broadcast_select_fusion.6
  134.1 5.6 %collective-permute-start.30 = (bf16[64,1920]{1,0:T(8,128)(2,1)}, bf16[64,1920]{1,0:T(8,128)(2,1)}, u32[]{:S(2)}, u32[]{:S(2)}) collective-permute-start(bf16[64,1920]{1,0:T(8,128)(2,1)} %broadcast_select_fusion.6), channel_id=1, source_target_pairs={{0,16},{2,18},{4,20},{6,22},{8,24},{10,26},{12,28},{14,30},{16,0},... | collective-permute-start | bytes 737288 | tf_op jit(solution)/shard_map/ppermute | solution.py:19
  142.1 14.2 %block_attention.4 = bf16[320,384]{1,0:T(8,128)(2,1)S(1)} custom-call(s32[3]{0:T(128)S(1)} %add_add_fusion.3.refs_0_, s32[8,1,640]{2,1,0:T(1,128)S(1)} %broadcast_in_dim.129.refs_1_, s32[320,1]{1,0:T(8,128)S(1)} %reshape_reshape.23.refs_2_, bf16[320,384]{1,0:T(8,128)(2,1)} %collective-permute-done.8.refs_3_, ...), custom_call_target="tpu_custom_call" | custom-call | flops 2516582400 | bytes 8355840 | tf_op jit(solution)/shard_map/block_attention/pallas_call | solution.py:153
  157.5 11.3 %block_attention.5 = bf16[320,384]{1,0:T(8,128)(2,1)S(1)} custom-call(s32[3]{0:T(128)S(1)} %add_add_fusion.2.refs_0_, s32[8,1,640]{2,1,0:T(1,128)S(1)} %broadcast_in_dim.129.refs_1_, s32[320,1]{1,0:T(8,128)S(1)} %reshape_reshape.22.refs_2_, bf16[320,384]{1,0:T(8,128)(2,1)} %collective-permute-done.7.refs_3_, ...), custom_call_target="tpu_custom_call" | custom-call | flops 2516582400 | bytes 8355840 | tf_op jit(solution)/shard_map/block_attention/pallas_call | solution.py:153
  168.9 8.3 %block_attention.6 = bf16[320,384]{1,0:T(8,128)(2,1)S(1)} custom-call(s32[3]{0:T(128)S(1)} %add_add_fusion.1.refs_0_, s32[8,1,640]{2,1,0:T(1,128)S(1)} %broadcast_in_dim.129.refs_1_, s32[320,1]{1,0:T(8,128)S(1)} %reshape_reshape.21.refs_2_, bf16[320,384]{1,0:T(8,128)(2,1)} %collective-permute-done.6.refs_3_, ...), custom_call_target="tpu_custom_call" | custom-call | flops 2516582400 | bytes 8355840 | tf_op jit(solution)/shard_map/block_attention/pallas_call | solution.py:153
  177.2 7.0 %collective-permute-start.26 = (bf16[320,384]{1,0:T(8,128)(2,1)S(1)}, bf16[320,384]{1,0:T(8,128)(2,1)S(1)}, u32[]{:S(2)}, u32[]{:S(2)}) collective-permute-start(bf16[320,384]{1,0:T(8,128)(2,1)S(1)} %block_attention.6), channel_id=1, source_target_pairs={{0,24},{2,26},{4,28},{6,30},{8,16},{10,18},{12,20},{14,22},{16,8},... | collective-permute-start | bytes 737288 | tf_op jit(solution)/shard_map/ppermute | solution.py:19
  186.1 17.0 %block_attention.7 = bf16[320,384]{1,0:T(8,128)(2,1)S(1)} custom-call(s32[3]{0:T(128)S(1)} %add_add_fusion.refs_0_, s32[8,1,640]{2,1,0:T(1,128)S(1)} %broadcast_in_dim.129.refs_1_, s32[320,1]{1,0:T(8,128)S(1)} %reshape_reshape.20.refs_2_, bf16[320,384]{1,0:T(8,128)(2,1)S(1)} %get-tuple-element.15.refs_3_, bf16[640,384]{1,0:T(8,128)(2,1)S(1)} %pad_maximum_fusion.11.refs_4_, ...), custom_call_target="tpu_custom_call" | custom-call | flops 2516582400 | bytes 8355840 | tf_op jit(solution)/shard_map/block_attention/pallas_call | solution.py:153
  203.1 2.4 collective-permute-done.25
  206.0 12.8 %add_convert_fusion = bf16[1536,6144]{1,0:T(8,128)(2,1)} fusion(bf16[1536,6144]{1,0:T(8,128)(2,1)} %param.17, bf16[64,3840]{1,0:T(8,128)(2,1)S(1)} %get-tuple-element.52, bf16[64,3840]{1,0:T(8,128)(2,1)S(1)} %get-tuple-element.51), kind=kOutput, calls=%fused_computation | convolution fusion | flops 1237843968 | bytes 38928384 | tf_op jit(solution)/shard_map/dot_general | solution.py:58
  218.7 2.7 fusion.29
  221.5 3.2 %fusion.26 = bf16[320,768]{1,0:T(8,128)(2,1)S(1)} fusion(bf16[1536,6144]{1,0:T(8,128)(2,1)} %add_convert_fusion, s32[]{:T(128)S(6)} %select_n.303, bf16[320,384]{1,0:T(8,128)(2,1)S(1)} %get-tuple-element.40, bf16[320,384]{1,0:T(8,128)(2,1)S(1)} %get-tuple-element.41, bf16[320,384]{1,0:T(8,128)(2,1)S(1)} %get-tuple-element.42, ...), kind=kOutput, calls=%fused_computation.24 | convolution fusion | flops 759152640 | bytes 3833860 | tf_op jit(solution)/shard_map/dot_general | solution.py:267
  224.7 3.3 %fusion.23 = bf16[320,768]{1,0:T(8,128)(2,1)S(1)} fusion(bf16[1536,6144]{1,0:T(8,128)(2,1)} %add_convert_fusion, s32[]{:T(128)S(6)} %select_n.302, bf16[320,384]{1,0:T(8,128)(2,1)S(1)} %get-tuple-element.40, bf16[320,384]{1,0:T(8,128)(2,1)S(1)} %get-tuple-element.41, bf16[320,384]{1,0:T(8,128)(2,1)S(1)} %get-tuple-element.42, ...), kind=kOutput, calls=%fused_computation.23 | convolution fusion | flops 759152640 | bytes 3833860 | tf_op jit(solution)/shard_map/dot_general | solution.py:267
  229.1 1.7 collective-permute-start.33
  231.2 1.7 collective-permute-start.35
  233.2 3.3 %fusion = f32[320,3072]{1,0:T(8,128)S(1)} fusion(bf16[1536,6144]{1,0:T(8,128)(2,1)S(1)} %copy-done.3, s32[]{:T(128)S(6)} %select_n.300, bf16[320,384]{1,0:T(8,128)(2,1)S(1)} %get-tuple-element.40, bf16[320,384]{1,0:T(8,128)(2,1)S(1)} %get-tuple-element.41, bf16[320,384]{1,0:T(8,128)(2,1)S(1)} %get-tuple-element.42, bf16[320,384]{1,0:T(8,128)(2,1)S(1)} %get-tuple-element.39), kind=kOutput, calls=%fused_computation.4 | convolution fusion | flops 3023831040 | bytes 14352388 | tf_op jit(solution)/shard_map/dot_general | solution.py:270
  236.5 6.7 %collective-permute-done.33 = bf16[320,768]{1,0:T(8,128)(2,1)S(1)} collective-permute-done((bf16[320,768]{1,0:T(8,128)(2,1)S(1)}, bf16[320,768]{1,0:T(8,128)(2,1)S(1)}, u32[]{:S(2)}, u32[]{:S(2)}) %collective-permute-start.33) | collective-permute-done | bytes 491552 | tf_op jit(solution)/shard_map/ppermute | solution.py:268
  243.2 10.5 %collective-permute-done.34 = bf16[320,768]{1,0:T(8,128)(2,1)S(1)} collective-permute-done((bf16[320,768]{1,0:T(8,128)(2,1)S(1)}, bf16[320,768]{1,0:T(8,128)(2,1)S(1)}, u32[]{:S(2)}, u32[]{:S(2)}) %collective-permute-start.34) | collective-permute-done | bytes 491552 | tf_op jit(solution)/shard_map/ppermute | solution.py:268
  253.7 10.5 %collective-permute-done.35 = bf16[320,768]{1,0:T(8,128)(2,1)S(1)} collective-permute-done((bf16[320,768]{1,0:T(8,128)(2,1)S(1)}, bf16[320,768]{1,0:T(8,128)(2,1)S(1)}, u32[]{:S(2)}, u32[]{:S(2)}) %collective-permute-start.35) | collective-permute-done | bytes 491552 | tf_op jit(solution)/shard_map/ppermute | solution.py:268
  264.3 9.7 %collective-permute-done.36 = bf16[320,768]{1,0:T(8,128)(2,1)S(1)} collective-permute-done((bf16[320,768]{1,0:T(8,128)(2,1)S(1)}, bf16[320,768]{1,0:T(8,128)(2,1)S(1)}, u32[]{:S(2)}, u32[]{:S(2)}) %collective-permute-start.36) | collective-permute-done | bytes 491552 | tf_op jit(solution)/shard_map/ppermute | solution.py:268
  (144 shorter events, 37.0 us)
Async XLA Ops:
  6.5 57.3 %all-gather.2.cloned.1.call-start = ((), (), s32[]{:S(2)}) async-start(), calls=%async_computation | async-start | bytes 5898240 | tf_op jit(solution)/shard_map/all_gather | solution.py:205
  9.5 18.5 %collective-permute-start.27 = (bf16[64,3840]{1,0:T(8,128)(2,1)}, bf16[64,3840]{1,0:T(8,128)(2,1)}, u32[]{:S(2)}, u32[]{:S(2)}) collective-permute-start(bf16[64,3840]{1,0:T(8,128)(2,1)} %broadcast_select_fusion.2), channel_id=1, source_target_pairs={{0,2},{2,0},{4,6},{6,4},{8,10},{10,8},{12,14},{14,12},{16,18},{18,... | collective-permute-start | bytes 1474568 | tf_op jit(solution)/shard_map/ppermute | solution.py:19
  27.6 12.3 %collective-permute-start.3 = (bf16[64,1920]{1,0:T(8,128)(2,1)S(1)}, bf16[64,1920]{1,0:T(8,128)(2,1)S(1)}, u32[]{:S(2)}, u32[]{:S(2)}) collective-permute-start(bf16[64,1920]{1,0:T(8,128)(2,1)S(1)} %broadcast_select_fusion.8), channel_id=1, source_target_pairs={{0,16},{2,18},{4,20},{6,22},{8,24},{10,26},{12,28},{14,30},{16,0},... | collective-permute-start | bytes 737288 | tf_op jit(solution)/shard_map/ppermute | solution.py:19
  41.3 25.5 %collective-permute-start.28 = (bf16[64,1920]{1,0:T(8,128)(2,1)}, bf16[64,1920]{1,0:T(8,128)(2,1)S(1)}, u32[]{:S(2)}, u32[]{:S(2)}) collective-permute-start(bf16[64,1920]{1,0:T(8,128)(2,1)} %broadcast_select_fusion.12), channel_id=1, source_target_pairs={{0,4},{2,6},{4,0},{6,2},{8,12},{10,14},{12,8},{14,10},{16,20},{18,... | collective-permute-start | bytes 737288 | tf_op jit(solution)/shard_map/ppermute | solution.py:19
  49.1 41.1 %collective-permute-start.10 = (bf16[640,384]{1,0:T(8,128)(2,1)S(1)}, bf16[640,384]{1,0:T(8,128)(2,1)S(1)}, u32[]{:S(2)}, u32[]{:S(2)}) collective-permute-start(bf16[640,384]{1,0:T(8,128)(2,1)S(1)} %pad_maximum_fusion.11.refs_4_), channel_id=1, source_target_pairs={{0,4},{2,6},{4,0},{6,2},{8,12},{10,14},{12,8},{14,10},{16,20},{18,... | collective-permute-start | bytes 1474568 | tf_op jit(solution)/shard_map/ppermute | solution.py:19
  49.7 42.3 %collective-permute-start.9 = (bf16[640,384]{1,0:T(8,128)(2,1)S(1)}, bf16[640,384]{1,0:T(8,128)(2,1)S(1)}, u32[]{:S(2)}, u32[]{:S(2)}) collective-permute-start(bf16[640,384]{1,0:T(8,128)(2,1)S(1)} %pad_maximum_fusion.11.refs_4_), channel_id=1, source_target_pairs={{0,2},{2,0},{4,6},{6,4},{8,10},{10,8},{12,14},{14,12},{16,18},{18,... | collective-permute-start | bytes 1474568 | tf_op jit(solution)/shard_map/ppermute | solution.py:19
  50.7 36.2 %collective-permute-start.12 = (bf16[640,384]{1,0:T(8,128)(2,1)}, bf16[640,384]{1,0:T(8,128)(2,1)S(1)}, u32[]{:S(2)}, u32[]{:S(2)}) collective-permute-start(bf16[640,384]{1,0:T(8,128)(2,1)} %pad_maximum_fusion.12), channel_id=1, source_target_pairs={{0,8},{2,10},{4,12},{6,14},{8,0},{10,2},{12,4},{14,6},{16,24},{18,... | collective-permute-start | bytes 1474568 | tf_op jit(solution)/shard_map/ppermute | solution.py:19
  51.6 38.6 %collective-permute-start.16 = (bf16[640,384]{1,0:T(8,128)(2,1)}, bf16[640,384]{1,0:T(8,128)(2,1)S(1)}, u32[]{:S(2)}, u32[]{:S(2)}) collective-permute-start(bf16[640,384]{1,0:T(8,128)(2,1)} %pad_maximum_fusion.13), channel_id=1, source_target_pairs={{0,16},{2,18},{4,20},{6,22},{8,24},{10,26},{12,28},{14,30},{16,0},... | collective-permute-start | bytes 1474568 | tf_op jit(solution)/shard_map/ppermute | solution.py:19
  66.8 34.5 %collective-permute-start.20 = (bf16[640,384]{1,0:T(8,128)(2,1)S(1)}, bf16[640,384]{1,0:T(8,128)(2,1)}, u32[]{:S(2)}, u32[]{:S(2)}) collective-permute-start(bf16[640,384]{1,0:T(8,128)(2,1)S(1)} %pad_maximum_fusion.14), channel_id=1, source_target_pairs={{0,24},{2,26},{4,28},{6,30},{8,16},{10,18},{12,20},{14,22},{16,8},... | collective-permute-start | bytes 1474568 | tf_op jit(solution)/shard_map/ppermute | solution.py:19
  86.9 14.4 %collective-permute-start.6 = (bf16[320,384]{1,0:T(8,128)(2,1)}, bf16[320,384]{1,0:T(8,128)(2,1)}, u32[]{:S(2)}, u32[]{:S(2)}) collective-permute-start(bf16[320,384]{1,0:T(8,128)(2,1)} %get-tuple-element.53), channel_id=1, source_target_pairs={{0,24},{2,26},{4,28},{6,30},{8,16},{10,18},{12,20},{14,22},{16,8},... | collective-permute-start | bytes 737288 | tf_op jit(solution)/shard_map/ppermute | solution.py:19
  90.2 12.7 %collective-permute-start.8 = (bf16[320,384]{1,0:T(8,128)(2,1)}, bf16[320,384]{1,0:T(8,128)(2,1)}, u32[]{:S(2)}, u32[]{:S(2)}) collective-permute-start(bf16[320,384]{1,0:T(8,128)(2,1)} %get-tuple-element.54), channel_id=1, source_target_pairs={{0,8},{2,10},{4,12},{6,14},{8,0},{10,2},{12,4},{14,6},{16,24},{18,... | collective-permute-start | bytes 737288 | tf_op jit(solution)/shard_map/ppermute | solution.py:19
  90.3 28.7 %collective-permute-start.7 = (bf16[320,384]{1,0:T(8,128)(2,1)}, bf16[320,384]{1,0:T(8,128)(2,1)}, u32[]{:S(2)}, u32[]{:S(2)}) collective-permute-start(bf16[320,384]{1,0:T(8,128)(2,1)} %get-tuple-element.55), channel_id=1, source_target_pairs={{0,16},{2,18},{4,20},{6,22},{8,24},{10,26},{12,28},{14,30},{16,0},... | collective-permute-start | bytes 737288 | tf_op jit(solution)/shard_map/ppermute | solution.py:19
  92.0 29.7 %collective-permute-start.14 = (bf16[640,384]{1,0:T(8,128)(2,1)S(1)}, bf16[640,384]{1,0:T(8,128)(2,1)}, u32[]{:S(2)}, u32[]{:S(2)}) collective-permute-start(bf16[640,384]{1,0:T(8,128)(2,1)S(1)} %collective-permute-done.12.refs_8_), channel_id=1, source_target_pairs={{0,4},{2,6},{4,0},{6,2},{8,12},{10,14},{12,8},{14,10},{16,20},{18,... | collective-permute-start | bytes 1474568 | tf_op jit(solution)/shard_map/ppermute | solution.py:19
  101.3 25.9 %collective-permute-start.13 = (bf16[640,384]{1,0:T(8,128)(2,1)S(1)}, bf16[640,384]{1,0:T(8,128)(2,1)S(1)}, u32[]{:S(2)}, u32[]{:S(2)}) collective-permute-start(bf16[640,384]{1,0:T(8,128)(2,1)S(1)} %collective-permute-done.12.refs_8_), channel_id=1, source_target_pairs={{0,2},{2,0},{4,6},{6,4},{8,10},{10,8},{12,14},{14,12},{16,18},{18,... | collective-permute-start | bytes 1474568 | tf_op jit(solution)/shard_map/ppermute | solution.py:19
  101.4 28.2 %collective-permute-start.18 = (bf16[640,384]{1,0:T(8,128)(2,1)S(1)}, bf16[640,384]{1,0:T(8,128)(2,1)}, u32[]{:S(2)}, u32[]{:S(2)}) collective-permute-start(bf16[640,384]{1,0:T(8,128)(2,1)S(1)} %collective-permute-done.16.refs_12_), channel_id=1, source_target_pairs={{0,4},{2,6},{4,0},{6,2},{8,12},{10,14},{12,8},{14,10},{16,20},{18,... | collective-permute-start | bytes 1474568 | tf_op jit(solution)/shard_map/ppermute | solution.py:19
  102.9 27.3 %collective-permute-start.17 = (bf16[640,384]{1,0:T(8,128)(2,1)S(1)}, bf16[640,384]{1,0:T(8,128)(2,1)}, u32[]{:S(2)}, u32[]{:S(2)}) collective-permute-start(bf16[640,384]{1,0:T(8,128)(2,1)S(1)} %collective-permute-done.16.refs_12_), channel_id=1, source_target_pairs={{0,2},{2,0},{4,6},{6,4},{8,10},{10,8},{12,14},{14,12},{16,18},{18,... | collective-permute-start | bytes 1474568 | tf_op jit(solution)/shard_map/ppermute | solution.py:19
  119.0 12.9 %collective-permute-start.22 = (bf16[640,384]{1,0:T(8,128)(2,1)}, bf16[640,384]{1,0:T(8,128)(2,1)}, u32[]{:S(2)}, u32[]{:S(2)}) collective-permute-start(bf16[640,384]{1,0:T(8,128)(2,1)} %collective-permute-done.20.refs_16_), channel_id=1, source_target_pairs={{0,4},{2,6},{4,0},{6,2},{8,12},{10,14},{12,8},{14,10},{16,20},{18,... | collective-permute-start | bytes 1474568 | tf_op jit(solution)/shard_map/ppermute | solution.py:19
  121.8 10.2 %collective-permute-start.29 = (bf16[64,1920]{1,0:T(8,128)(2,1)S(1)}, bf16[64,1920]{1,0:T(8,128)(2,1)}, u32[]{:S(2)}, u32[]{:S(2)}) collective-permute-start(bf16[64,1920]{1,0:T(8,128)(2,1)S(1)} %select_select_fusion.2), channel_id=1, source_target_pairs={{0,8},{2,10},{4,12},{6,14},{8,0},{10,2},{12,4},{14,6},{16,24},{18,... | collective-permute-start | bytes 737288 | tf_op jit(solution)/shard_map/ppermute | solution.py:19
  129.6 11.4 %collective-permute-start.21 = (bf16[640,384]{1,0:T(8,128)(2,1)}, bf16[640,384]{1,0:T(8,128)(2,1)}, u32[]{:S(2)}, u32[]{:S(2)}) collective-permute-start(bf16[640,384]{1,0:T(8,128)(2,1)} %collective-permute-done.20.refs_16_), channel_id=1, source_target_pairs={{0,2},{2,0},{4,6},{6,4},{8,10},{10,8},{12,14},{14,12},{16,18},{18,... | collective-permute-start | bytes 1474568 | tf_op jit(solution)/shard_map/ppermute | solution.py:19
  130.2 10.9 %collective-permute-start.15 = (bf16[640,384]{1,0:T(8,128)(2,1)}, bf16[640,384]{1,0:T(8,128)(2,1)}, u32[]{:S(2)}, u32[]{:S(2)}) collective-permute-start(bf16[640,384]{1,0:T(8,128)(2,1)} %collective-permute-done.14.refs_10_), channel_id=1, source_target_pairs={{0,2},{2,0},{4,6},{6,4},{8,10},{10,8},{12,14},{14,12},{16,18},{18,... | collective-permute-start | bytes 1474568 | tf_op jit(solution)/shard_map/ppermute | solution.py:19
  131.9 9.1 %collective-permute-start.19 = (bf16[640,384]{1,0:T(8,128)(2,1)}, bf16[640,384]{1,0:T(8,128)(2,1)}, u32[]{:S(2)}, u32[]{:S(2)}) collective-permute-start(bf16[640,384]{1,0:T(8,128)(2,1)} %collective-permute-done.18.refs_14_), channel_id=1, source_target_pairs={{0,2},{2,0},{4,6},{6,4},{8,10},{10,8},{12,14},{14,12},{16,18},{18,... | collective-permute-start | bytes 1474568 | tf_op jit(solution)/shard_map/ppermute | solution.py:19
  131.9 9.1 %collective-permute-start.23 = (bf16[640,384]{1,0:T(8,128)(2,1)}, bf16[640,384]{1,0:T(8,128)(2,1)}, u32[]{:S(2)}, u32[]{:S(2)}) collective-permute-start(bf16[640,384]{1,0:T(8,128)(2,1)} %collective-permute-done.22.refs_18_), channel_id=1, source_target_pairs={{0,2},{2,0},{4,6},{6,4},{8,10},{10,8},{12,14},{14,12},{16,18},{18,... | collective-permute-start | bytes 1474568 | tf_op jit(solution)/shard_map/ppermute | solution.py:19
  134.1 22.2 %collective-permute-start.30 = (bf16[64,1920]{1,0:T(8,128)(2,1)}, bf16[64,1920]{1,0:T(8,128)(2,1)}, u32[]{:S(2)}, u32[]{:S(2)}) collective-permute-start(bf16[64,1920]{1,0:T(8,128)(2,1)} %broadcast_select_fusion.6), channel_id=1, source_target_pairs={{0,16},{2,18},{4,20},{6,22},{8,24},{10,26},{12,28},{14,30},{16,0},... | collective-permute-start | bytes 737288 | tf_op jit(solution)/shard_map/ppermute | solution.py:19
  157.5 27.4 %collective-permute-start.31 = (bf16[64,1920]{1,0:T(8,128)(2,1)S(1)}, bf16[64,1920]{1,0:T(8,128)(2,1)S(1)}, u32[]{:S(2)}, u32[]{:S(2)}) collective-permute-start(bf16[64,1920]{1,0:T(8,128)(2,1)S(1)} %broadcast_select_fusion.7), channel_id=1, source_target_pairs={{0,4},{2,6},{4,0},{6,2},{8,12},{10,14},{12,8},{14,10},{16,20},{18,... | collective-permute-start | bytes 737288 | tf_op jit(solution)/shard_map/ppermute | solution.py:19
  177.2 25.9 %collective-permute-start.26 = (bf16[320,384]{1,0:T(8,128)(2,1)S(1)}, bf16[320,384]{1,0:T(8,128)(2,1)S(1)}, u32[]{:S(2)}, u32[]{:S(2)}) collective-permute-start(bf16[320,384]{1,0:T(8,128)(2,1)S(1)} %block_attention.6), channel_id=1, source_target_pairs={{0,24},{2,26},{4,28},{6,30},{8,16},{10,18},{12,20},{14,22},{16,8},... | collective-permute-start | bytes 737288 | tf_op jit(solution)/shard_map/ppermute | solution.py:19
  184.2 21.3 %collective-permute-start.25 = (bf16[320,384]{1,0:T(8,128)(2,1)S(1)}, bf16[320,384]{1,0:T(8,128)(2,1)S(1)}, u32[]{:S(2)}, u32[]{:S(2)}) collective-permute-start(bf16[320,384]{1,0:T(8,128)(2,1)S(1)} %block_attention.5), channel_id=1, source_target_pairs={{0,16},{2,18},{4,20},{6,22},{8,24},{10,26},{12,28},{14,30},{16,0},... | collective-permute-start | bytes 737288 | tf_op jit(solution)/shard_map/ppermute | solution.py:19
  184.2 21.3 %collective-permute-start.24 = (bf16[320,384]{1,0:T(8,128)(2,1)S(1)}, bf16[320,384]{1,0:T(8,128)(2,1)S(1)}, u32[]{:S(2)}, u32[]{:S(2)}) collective-permute-start(bf16[320,384]{1,0:T(8,128)(2,1)S(1)} %block_attention.4), channel_id=1, source_target_pairs={{0,8},{2,10},{4,12},{6,14},{8,0},{10,2},{12,4},{14,6},{16,24},{18,... | collective-permute-start | bytes 737288 | tf_op jit(solution)/shard_map/ppermute | solution.py:19
  185.0 20.8 %collective-permute-start.32 = (bf16[64,3840]{1,0:T(8,128)(2,1)S(1)}, bf16[64,3840]{1,0:T(8,128)(2,1)S(1)}, u32[]{:S(2)}, u32[]{:S(2)}) collective-permute-start(bf16[64,3840]{1,0:T(8,128)(2,1)S(1)} %pad_maximum_fusion.15), channel_id=1, source_target_pairs={{0,2},{2,0},{4,6},{6,4},{8,10},{10,8},{12,14},{14,12},{16,18},{18,... | collective-permute-start | bytes 1474568 | tf_op jit(solution)/shard_map/ppermute | solution.py:19
  229.1 14.1 %collective-permute-start.33 = (bf16[320,768]{1,0:T(8,128)(2,1)S(1)}, bf16[320,768]{1,0:T(8,128)(2,1)S(1)}, u32[]{:S(2)}, u32[]{:S(2)}) collective-permute-start(bf16[320,768]{1,0:T(8,128)(2,1)S(1)} %fusion.20), channel_id=1, source_target_pairs={{0,1},{1,0},{2,3},{3,2},{4,5},{5,4},{6,7},{7,6},{8,9},{9,8},{10,11... | collective-permute-start | bytes 1474568 | tf_op jit(solution)/shard_map/ppermute | solution.py:268
  230.8 22.9 %collective-permute-start.34 = (bf16[320,768]{1,0:T(8,128)(2,1)S(1)}, bf16[320,768]{1,0:T(8,128)(2,1)S(1)}, u32[]{:S(2)}, u32[]{:S(2)}) collective-permute-start(bf16[320,768]{1,0:T(8,128)(2,1)S(1)} %fusion.23), channel_id=1, source_target_pairs={{0,1},{1,0},{2,3},{3,2},{4,5},{5,4},{6,7},{7,6},{8,9},{9,8},{10,11... | collective-permute-start | bytes 1474568 | tf_op jit(solution)/shard_map/ppermute | solution.py:268
  231.2 33.1 %collective-permute-start.35 = (bf16[320,768]{1,0:T(8,128)(2,1)S(1)}, bf16[320,768]{1,0:T(8,128)(2,1)S(1)}, u32[]{:S(2)}, u32[]{:S(2)}) collective-permute-start(bf16[320,768]{1,0:T(8,128)(2,1)S(1)} %fusion.26), channel_id=1, source_target_pairs={{0,1},{1,0},{2,3},{3,2},{4,5},{5,4},{6,7},{7,6},{8,9},{9,8},{10,11... | collective-permute-start | bytes 1474568 | tf_op jit(solution)/shard_map/ppermute | solution.py:268
  232.8 41.2 %collective-permute-start.36 = (bf16[320,768]{1,0:T(8,128)(2,1)S(1)}, bf16[320,768]{1,0:T(8,128)(2,1)S(1)}, u32[]{:S(2)}, u32[]{:S(2)}) collective-permute-start(bf16[320,768]{1,0:T(8,128)(2,1)S(1)} %fusion.29), channel_id=1, source_target_pairs={{0,1},{1,0},{2,3},{3,2},{4,5},{5,4},{6,7},{7,6},{8,9},{9,8},{10,11... | collective-permute-start | bytes 1474568 | tf_op jit(solution)/shard_map/ppermute | solution.py:268
  (21 other events, 182.8 us)
Sparse Core Ops, SparseCore 0:
  8.9 54.8 all-gather.1

commit v3 on v2

--- a/solution.py
+++ b/solution.py
@@ -24,6 +24,8 @@
     me = lax.axis_index("ctx")
     cols = down.shape[0]
     buf = jnp.concatenate([down.T, up], axis=1)
+    if hold is not None:
+        buf, _ = lax.optimization_barrier((buf, hold))
     owner = jnp.where(jnp.arange(buf.shape[1]) < cols, down_owner, up_owner)[None, :]
     halved = []
     bit = 1
@@ -37,12 +39,11 @@
             owner = jnp.where(high, owner[:, half:], owner[:, :half])
             halved.append(bit)
         else:
-            if hold is not None:
-                buf, _ = lax.optimization_barrier((buf, hold))
-                hold = None
             received = swap(buf, bit)
             kept = buf
         buf = jnp.where((owner & bit) == (me & bit), kept, received)
+        if bit <= 2:
+            after_halving = buf
         bit *= 2
     part = buf
     for bit in reversed(halved):
@@ -51,7 +52,7 @@
         buf = jnp.concatenate(
             [jnp.where(high, other, buf), jnp.where(high, buf, other)], axis=1
         )
-    return buf[:, :cols], buf[:, cols:], part
+    return buf[:, :cols], buf[:, cols:], after_halving, part
 
 
 def merge_weight(base, down_t, up):
@@ -199,15 +200,24 @@
         return lax.dynamic_slice_in_dim(x, (my_group ^ step) * width, width, 1)
 
     gain = lax.all_gather(norm_gain_vector, "tp", axis=0, tiled=True)
-    query_down_t, query_up, fetched = fetch_pair(
+    query_down_t, query_up, after_halving, fetched = fetch_pair(
         query_update_first[0], query_update_second[0], owners[0], owners[1]
     )
-    whole = lax.all_gather(tokens, "tp", axis=1, tiled=True)
-
-    held_keys, held_values, _ = lax.optimization_barrier((keys, values, fetched))
+    if tp == 2:
+        other = lax.ppermute(tokens, "tp", [(0, 1), (1, 0)])
+        whole = jnp.concatenate(
+            [jnp.where(mine == 0, tokens, other), jnp.where(mine == 0, other, tokens)], axis=1
+        )
+    else:
+        whole = lax.all_gather(tokens, "tp", axis=1, tiled=True)
+
     kv_parts = []
     for step in range(groups):
-        part = jnp.concatenate([columns(held_keys, step), columns(held_values, step)], axis=0)
+        part = jnp.concatenate([columns(keys, step), columns(values, step)], axis=0)
+        if step == 0:
+            part, _ = lax.optimization_barrier((part, after_halving))
+        elif step < groups - 1:
+            part, _ = lax.optimization_barrier((part, fetched))
         if step:
             part = swap(part, step * ranks)
         have = {0: part}
@@ -230,24 +240,19 @@
         part = columns(queries, step)
         q_parts.append(swap(part, step * ranks) if step else part)
 
-    out_down_t, out_up, _ = fetch_pair(
-        output_update_first[0],
-        output_update_second[0],
-        owners[2],
-        owners[3],
-        hold=tuple(q_parts),
-    )
+    out_down_t, out_up, _, _ = fetch_pair(
+        output_update_first[0], output_update_second[0], owners[2], owners[3], hold=fetched
+    )
+    out_merged = merge_weight(output_frozen_weight, out_down_t, out_up)
 
     order = list(range(1, groups)) + [0]
     o_parts = [None] * groups
-    gate = None
+    gate = out_merged
     for step in order:
         q_part = q_parts[step]
-        if gate is not None:
-            q_part, _ = lax.optimization_barrier((q_part, gate))
+        q_part, _ = lax.optimization_barrier((q_part, gate))
         gate = attend(q_part, kv_parts, (my_group ^ step) * ranks + me % ranks, frame_block_number)
         o_parts[step] = swap(gate, step * ranks) if step else gate
-    out_merged = merge_weight(output_frozen_weight, out_down_t, out_up)
     stacked = jnp.stack(o_parts)
     attended = jnp.concatenate(
         [lax.dynamic_index_in_dim(stacked, my_group ^ g, 0, keepdims=False) for g in range(groups)],

time: 286 us -> 280 us (0.979)
  between operations: 24.3 us -> 10.7 us
  other arithmetic: 25.6 us -> 36.2 us
  waiting for transfers between devices: 91.7 us -> 82.6 us
  local copies, waits for them, and re-layouts: 7.14 us -> 15.6 us
  Pallas kernels: 50.9 us -> 45 us
  starting transfers between devices: 35.1 us -> 40.9 us
    all_gather x1 -> x0, waiting for transfers between devices: 9.64 us -> none  [shards(): whole = lax.all_gather(tokens, 'tp', axis=1, tiled=True)]
    ppermute x33, waiting for transfers between devices: 43.9 us -> 51.9 us  [swap(): return lax.ppermute(x, 'ctx', [(i, i ^ bit) for i in range(n)])]
    unnamed x30 -> x80, local copies, waits for them, and re-layouts: 1.48 us -> 8.89 us
    ppermute x4, waiting for transfers between devices: 37.5 us -> 30.7 us  [shards(): lax.ppermute(product.astype(jnp.bfloat16), 'tp', [(0, 1), (1, 0)])]
    pallas_call x4, Pallas kernels: 50.9 us -> 45 us  [attend(): pl.pallas_call(functools.partial(attention_kernel, n, heads, rows), out_s...]
    ppermute x33, starting transfers between devices: 30.9 us -> 35.3 us  [swap(): return lax.ppermute(x, 'ctx', [(i, i ^ bit) for i in range(n)])]
    select_n x4, other arithmetic: 1.39 us -> 4.63 us  [fetch_pair(): jnp.where(high, other, buf)]
    concatenate x4 -> x5, other arithmetic: 1.79 us -> 4.73 us  [the longest x4 3.5 us: shards(): part = jnp.concatenate([columns(keys, step), columns(values, step)], axis=0)]
  transfers between devices with their start and end apart: 38 -> 38, of which waited for: 12 -> 13; matrix products, arithmetic and copies ran while one was open for 17% -> 28% of each run, Pallas kernels for 18% -> 16%
where the time goes in v3:
time: 280 us; the launch traced here: 278 us
  waiting for transfers between devices  82.6 us (30%)
  Pallas kernels  45 us (16%)
  matrix products  42.9 us (15%)
  starting transfers between devices  40.9 us (15%)
  other arithmetic  36.2 us (13%)
  local copies, waits for them, and re-layouts  15.6 us (6%)
  between operations  10.7 us (4%)
  blocking collectives  4.36 us (2%)
    ppermute x33, waiting for transfers between devices, swap(): return lax.ppermute(x, 'ctx', [(i, i ^ bit) for i in range(n)])  51.9 us
    pallas_call x4, Pallas kernels, attend(): pl.pallas_call(functools.partial(attention_kernel, n, heads, rows), out_s...  45 us
    ppermute x33, starting transfers between devices, swap(): return lax.ppermute(x, 'ctx', [(i, i ^ bit) for i in range(n)])  35.3 us
    ppermute x4, waiting for transfers between devices, shards(): lax.ppermute(product.astype(jnp.bfloat16), 'tp', [(0, 1), (1, 0)])  30.7 us
    dot_general x1, matrix products, shards(): jnp.dot(normed, query_merged, preferred_element_type=jnp.float32)  17.6 us
    dot_general x1, matrix products, merge_weight(): lax.dot_general(down_t, up, (((0,), (0,)), ((), ())), preferred_element_t...  13 us
    dot_general x4, matrix products, shards(): product = jnp.dot(attended, theirs, preferred_element_type=jnp.float32)  9.09 us
    unnamed x80, local copies, waits for them, and re-layouts  8.89 us
  transfers between devices with their start and end apart: 38, of which 13 were waited for; matrix products, arithmetic and copies ran while one was open for 28% of the time, Pallas kernels for 16%

profile of v3, /device:TPU:28, one launch (start us, length us, event | category | flops | bytes accessed | tf_op | source)
XLA Modules:
  0.0 278.1 jit_solution(18092476639221795645)
XLA Ops:
  15.1 5.8 %fusion.47 = (s32[]{:T(128)}, s32[]{:T(128)}, s32[]{:T(128)}, s32[]{:T(128)}, s32[]{:T(128)}, /*index=5*/s32[]{:T(128)}, s32[]{:T(128)}, s32[]{:T(128)}) fusion(s32[80]{0:T(128)S(1)} %copy-done.23, s32[]{:T(128)} %bitcast, s32[]{:T(128)} %bitcast.17, s32[]{:T(128)} %bitcast.15, s32[]{:T(128)} %bitcast.13, s32[]{:T(128)} %bitcast.11, s32[]{:T(128)} %bitcast.2, ...), kind=kLoop, calls=%fused_computation.117 | loop fusion | flops 1912 | bytes 384 | tf_op jit(solution)/shard_map/reduce_sum | solution.py:147
  30.4 2.5 collective-permute-done.3
  33.0 2.4 collective-permute-start.4
  36.3 9.7 %collective-permute-done.4 = bf16[64,1920]{1,0:T(8,128)(2,1)S(1)} collective-permute-done((bf16[64,1920]{1,0:T(8,128)(2,1)S(1)}, bf16[64,1920]{1,0:T(8,128)(2,1)S(1)}, u32[]{:S(2)}, u32[]{:S(2)}) %collective-permute-start.4) | collective-permute-done | bytes 245792 | tf_op jit(solution)/shard_map/ppermute | solution.py:19
  60.8 4.4 %all_gather.3 = bf16[6144]{0:T(1024)(128)(2,1)S(1)} all-gather(bf16[3072]{0:T(1024)(128)(2,1)S(1)} %copy-done.34), channel_id=1, replica_groups=mesh['ctx'=16,'tp'=2] {'tp'}, dimensions={0}, use_global_device_ids=true | all-gather | bytes 18432 | tf_op jit(solution)/shard_map/all_gather | solution.py:202
  70.8 2.3 broadcast_select_fusion.6
  73.2 4.2 %collective-permute-done.12 = bf16[64,1920]{1,0:T(8,128)(2,1)S(1)} collective-permute-done((bf16[64,1920]{1,0:T(8,128)(2,1)S(1)}, bf16[64,1920]{1,0:T(8,128)(2,1)S(1)}, u32[]{:S(2)}, u32[]{:S(2)}) %collective-permute-start.12) | collective-permute-done | bytes 245792 | tf_op jit(solution)/shard_map/ppermute | solution.py:19
  77.4 3.2 %collective-permute-start.13 = (bf16[64,1920]{1,0:T(8,128)(2,1)S(1)}, bf16[64,1920]{1,0:T(8,128)(2,1)S(1)}, u32[]{:S(2)}, u32[]{:S(2)}) collective-permute-start(bf16[64,1920]{1,0:T(8,128)(2,1)S(1)} %broadcast_select_fusion.8), channel_id=1, source_target_pairs={{0,16},{2,18},{4,20},{6,22},{8,24},{10,26},{12,28},{14,30},{16,0},... | collective-permute-start | bytes 737288 | tf_op jit(solution)/shard_map/ppermute | solution.py:19
  80.7 2.4 broadcast_select_fusion.1
  83.1 9.5 %collective-permute-done.13 = bf16[64,1920]{1,0:T(8,128)(2,1)S(1)} collective-permute-done((bf16[64,1920]{1,0:T(8,128)(2,1)S(1)}, bf16[64,1920]{1,0:T(8,128)(2,1)S(1)}, u32[]{:S(2)}, u32[]{:S(2)}) %collective-permute-start.13) | collective-permute-done | bytes 245792 | tf_op jit(solution)/shard_map/ppermute | solution.py:19
  94.1 6.4 %collective-permute-done.14 = bf16[64,1920]{1,0:T(8,128)(2,1)S(1)} collective-permute-done((bf16[64,1920]{1,0:T(8,128)(2,1)S(1)}, bf16[64,1920]{1,0:T(8,128)(2,1)S(1)}, u32[]{:S(2)}, u32[]{:S(2)}) %collective-permute-start.14) | collective-permute-done | bytes 245792 | tf_op jit(solution)/shard_map/ppermute | solution.py:19
  102.3 3.4 %collective-permute-start.23 = (bf16[640,384]{1,0:T(8,128)(2,1)}, bf16[640,384]{1,0:T(8,128)(2,1)}, u32[]{:S(2)}, u32[]{:S(2)}) collective-permute-start(bf16[640,384]{1,0:T(8,128)(2,1)} %pad_maximum_fusion.16), channel_id=1, source_target_pairs={{0,16},{2,18},{4,20},{6,22},{8,24},{10,26},{12,28},{14,30},{16,0},... | collective-permute-start | bytes 1474568 | tf_op jit(solution)/shard_map/ppermute | solution.py:19
  105.6 17.6 %fusion.9 = bf16[320,1536]{1,0:T(8,128)(2,1)} fusion(bf16[6144,1536]{1,0:T(8,128)(2,1)} %param.16, f32[6144]{0:T(1024)S(1)} %convert_element_type.87, f32[320]{0:T(512)S(1)} %add_rsqrt_fusion, bf16[320,3072]{1,0:T(8,128)(2,1)} %copy-done.11, bf16[320,3072]{1,0:T(8,128)(2,1)} %copy-done.10, bf16[64,3840]{1,0:T(8,128)(2,1)} %get-tuple-element.62, ...), kind=kOutput, calls=%fused_computation.13 | convolution fusion | flops 7291895808 | bytes 24995072 | tf_op jit(solution)/shard_map/dot_general | solution.py:236
  123.3 2.3 constant_dynamic-slice_fusion.11
  132.4 3.3 %collective-permute-done.9.refs_3_ = bf16[320,384]{1,0:T(8,128)(2,1)S(1)} collective-permute-done((bf16[320,384]{1,0:T(8,128)(2,1)S(1)}, bf16[320,384]{1,0:T(8,128)(2,1)S(1)}, u32[]{:S(2)}, u32[]{:S(2)}) %collective-permute-start.9) | collective-permute-done | bytes 245792 | tf_op jit(solution)/shard_map/ppermute | solution.py:19
  136.5 3.9 %collective-permute-done.21.refs_10_ = bf16[640,384]{1,0:T(8,128)(2,1)} collective-permute-done((bf16[640,384]{1,0:T(8,128)(2,1)}, bf16[640,384]{1,0:T(8,128)(2,1)}, u32[]{:S(2)}, u32[]{:S(2)}) %collective-permute-start.21) | collective-permute-done | bytes 491552 | tf_op jit(solution)/shard_map/ppermute | solution.py:19
  140.4 9.9 %collective-permute-done.25.refs_14_ = bf16[640,384]{1,0:T(8,128)(2,1)} collective-permute-done((bf16[640,384]{1,0:T(8,128)(2,1)}, bf16[640,384]{1,0:T(8,128)(2,1)}, u32[]{:S(2)}, u32[]{:S(2)}) %collective-permute-start.25) | collective-permute-done | bytes 491552 | tf_op jit(solution)/shard_map/ppermute | solution.py:19
  150.4 13.0 %add_convert_fusion = bf16[1536,6144]{1,0:T(8,128)(2,1)} fusion(bf16[1536,6144]{1,0:T(8,128)(2,1)} %param.17, bf16[64,3840]{1,0:T(8,128)(2,1)} %get-tuple-element.64, bf16[64,3840]{1,0:T(8,128)(2,1)} %get-tuple-element.63), kind=kOutput, calls=%fused_computation | convolution fusion | flops 1237843968 | bytes 38928384 | tf_op jit(solution)/shard_map/dot_general | solution.py:59
  166.5 12.6 %block_attention.4 = bf16[320,384]{1,0:T(8,128)(2,1)S(1)} custom-call(s32[3]{0:T(128)S(1)} %add_add_fusion.3.refs_0_, s32[8,1,640]{2,1,0:T(1,128)S(1)} %broadcast_in_dim.129.refs_1_, s32[320,1]{1,0:T(8,128)S(1)} %reshape_reshape.23.refs_2_, bf16[320,384]{1,0:T(8,128)(2,1)S(1)} %copy-done.8, bf16[640,384]{1,0:T(8,128)(2,1)S(1)} %pad_maximum_fusion.14.refs_4_, ...), custom_call_target="tpu_custom_call" | custom-call | flops 2516582400 | bytes 8355840 | tf_op jit(solution)/shard_map/block_attention/pallas_call | solution.py:154
  179.1 4.3 %collective-permute-start.31 = (bf16[320,384]{1,0:T(8,128)(2,1)S(1)}, bf16[320,384]{1,0:T(8,128)(2,1)}, u32[]{:S(2)}, u32[]{:S(2)}) collective-permute-start(bf16[320,384]{1,0:T(8,128)(2,1)S(1)} %block_attention.4), channel_id=1, source_target_pairs={{0,8},{2,10},{4,12},{6,14},{8,0},{10,2},{12,4},{14,6},{16,24},{18,... | collective-permute-start | bytes 737288 | tf_op jit(solution)/shard_map/ppermute | solution.py:19
  183.4 10.4 %block_attention.5 = bf16[320,384]{1,0:T(8,128)(2,1)} custom-call(s32[3]{0:T(128)S(1)} %add_add_fusion.2.refs_0_, s32[8,1,640]{2,1,0:T(1,128)S(1)} %broadcast_in_dim.129.refs_1_, s32[320,1]{1,0:T(8,128)S(1)} %reshape_reshape.22.refs_2_, bf16[320,384]{1,0:T(8,128)(2,1)} %collective-permute-done.8.refs_3_, bf16[640,384]{1,0:T(8,128)(2,1)S(1)} %pad_maximum_fusion.14.refs_4_, ...), custom_call_target="tpu_custom_call" | custom-call | flops 2516582400 | bytes 8355840 | tf_op jit(solution)/shard_map/block_attention/pallas_call | solution.py:154
  193.9 3.2 %collective-permute-start.32 = (bf16[320,384]{1,0:T(8,128)(2,1)}, bf16[320,384]{1,0:T(8,128)(2,1)}, u32[]{:S(2)}, u32[]{:S(2)}) collective-permute-start(bf16[320,384]{1,0:T(8,128)(2,1)} %block_attention.5), channel_id=1, source_target_pairs={{0,16},{2,18},{4,20},{6,22},{8,24},{10,26},{12,28},{14,30},{16,0},... | collective-permute-start | bytes 737288 | tf_op jit(solution)/shard_map/ppermute | solution.py:19
  197.1 6.4 %block_attention.6 = bf16[320,384]{1,0:T(8,128)(2,1)S(1)} custom-call(s32[3]{0:T(128)S(1)} %add_add_fusion.1.refs_0_, s32[8,1,640]{2,1,0:T(1,128)S(1)} %broadcast_in_dim.129.refs_1_, s32[320,1]{1,0:T(8,128)S(1)} %reshape_reshape.21.refs_2_, bf16[320,384]{1,0:T(8,128)(2,1)S(1)} %collective-permute-done.7.refs_3_, ...), custom_call_target="tpu_custom_call" | custom-call | flops 2516582400 | bytes 8355840 | tf_op jit(solution)/shard_map/block_attention/pallas_call | solution.py:154
  203.5 6.1 %collective-permute-start.33 = (bf16[320,384]{1,0:T(8,128)(2,1)S(1)}, bf16[320,384]{1,0:T(8,128)(2,1)}, u32[]{:S(2)}, u32[]{:S(2)}) collective-permute-start(bf16[320,384]{1,0:T(8,128)(2,1)S(1)} %block_attention.6), channel_id=1, source_target_pairs={{0,24},{2,26},{4,28},{6,30},{8,16},{10,18},{12,20},{14,22},{16,8},... | collective-permute-start | bytes 737288 | tf_op jit(solution)/shard_map/ppermute | solution.py:19
  211.9 15.6 %block_attention.7 = bf16[320,384]{1,0:T(8,128)(2,1)S(1)} custom-call(s32[3]{0:T(128)S(1)} %add_add_fusion.refs_0_, s32[8,1,640]{2,1,0:T(1,128)S(1)} %broadcast_in_dim.129.refs_1_, s32[320,1]{1,0:T(8,128)S(1)} %reshape_reshape.20.refs_2_, bf16[320,384]{1,0:T(8,128)(2,1)S(1)} %get-tuple-element.20.refs_3_, bf16[640,384]{1,0:T(8,128)(2,1)S(1)} %pad_maximum_fusion.14.refs_4_, ...), custom_call_target="tpu_custom_call" | custom-call | flops 2516582400 | bytes 8355840 | tf_op jit(solution)/shard_map/block_attention/pallas_call | solution.py:154
  229.1 2.7 fusion.23
  232.4 2.8 %fusion.26 = bf16[320,768]{1,0:T(8,128)(2,1)S(1)} fusion(bf16[1536,6144]{1,0:T(8,128)(2,1)} %add_convert_fusion, s32[]{:T(128)S(6)} %select_n.318, bf16[320,384]{1,0:T(8,128)(2,1)S(1)} %get-tuple-element.46, bf16[320,384]{1,0:T(8,128)(2,1)S(1)} %get-tuple-element.47, bf16[320,384]{1,0:T(8,128)(2,1)S(1)} %get-tuple-element.48, ...), kind=kOutput, calls=%fused_computation.27 | convolution fusion | flops 759152640 | bytes 3833860 | tf_op jit(solution)/shard_map/dot_general | solution.py:272
  236.6 2.6 fusion.29
  242.3 3.2 %fusion = f32[320,3072]{1,0:T(8,128)S(1)} fusion(bf16[1536,6144]{1,0:T(8,128)(2,1)S(1)} %bitcast.43, s32[]{:T(128)S(6)} %select_n.315, bf16[320,384]{1,0:T(8,128)(2,1)S(1)} %get-tuple-element.46, bf16[320,384]{1,0:T(8,128)(2,1)S(1)} %get-tuple-element.47, bf16[320,384]{1,0:T(8,128)(2,1)S(1)} %get-tuple-element.48, bf16[320,384]{1,0:T(8,128)(2,1)S(1)} %get-tuple-element.45), kind=kOutput, calls=%fused_computation.4 | convolution fusion | flops 3023831040 | bytes 14352388 | tf_op jit(solution)/shard_map/dot_general | solution.py:275
  245.5 9.6 %collective-permute-done.36 = bf16[320,768]{1,0:T(8,128)(2,1)S(1)} collective-permute-done((bf16[320,768]{1,0:T(8,128)(2,1)S(1)}, bf16[320,768]{1,0:T(8,128)(2,1)S(1)}, u32[]{:S(2)}, u32[]{:S(2)}) %collective-permute-start.36) | collective-permute-done | bytes 491552 | tf_op jit(solution)/shard_map/ppermute | solution.py:273
  255.1 10.5 %collective-permute-done.37 = bf16[320,768]{1,0:T(8,128)(2,1)S(1)} collective-permute-done((bf16[320,768]{1,0:T(8,128)(2,1)S(1)}, bf16[320,768]{1,0:T(8,128)(2,1)S(1)}, u32[]{:S(2)}, u32[]{:S(2)}) %collective-permute-start.37) | collective-permute-done | bytes 491552 | tf_op jit(solution)/shard_map/ppermute | solution.py:273
  265.7 10.5 %collective-permute-done.34 = bf16[320,768]{1,0:T(8,128)(2,1)S(1)} collective-permute-done((bf16[320,768]{1,0:T(8,128)(2,1)S(1)}, bf16[320,768]{1,0:T(8,128)(2,1)S(1)}, u32[]{:S(2)}, u32[]{:S(2)}) %collective-permute-start.34) | collective-permute-done | bytes 491552 | tf_op jit(solution)/shard_map/ppermute | solution.py:273
  (196 shorter events, 60.6 us)
Async XLA Ops:
  2.2 10.4 %collective-permute-start.1 = (bf16[64,3840]{1,0:T(8,128)(2,1)}, bf16[64,3840]{1,0:T(8,128)(2,1)}, u32[]{:S(2)}, u32[]{:S(2)}) collective-permute-start(bf16[64,3840]{1,0:T(8,128)(2,1)} %broadcast_select_fusion.7), channel_id=1, source_target_pairs={{0,2},{2,0},{4,6},{6,4},{8,10},{10,8},{12,14},{14,12},{16,18},{18,... | collective-permute-start | bytes 1474568 | tf_op jit(solution)/shard_map/ppermute | solution.py:19
  2.2 75.2 %collective-permute-start = (bf16[320,3072]{1,0:T(8,128)(2,1)}, bf16[320,3072]{1,0:T(8,128)(2,1)}, u32[]{:S(2)}, u32[]{:S(2)}) collective-permute-start(bf16[320,3072]{1,0:T(8,128)(2,1)} %param.12), channel_id=1, source_target_pairs={{0,1},{1,0},{2,3},{3,2},{4,5},{5,4},{6,7},{7,6},{8,9},{9,8},{10,11... | collective-permute-start | bytes 5898248 | tf_op jit(solution)/shard_map/ppermute | solution.py:207
  5.7 60.5 %collective-permute-start.27 = (bf16[640,384]{1,0:T(8,128)(2,1)}, bf16[640,384]{1,0:T(8,128)(2,1)S(1)}, u32[]{:S(2)}, u32[]{:S(2)}) collective-permute-start(bf16[640,384]{1,0:T(8,128)(2,1)} %pad_maximum_fusion.17), channel_id=1, source_target_pairs={{0,24},{2,26},{4,28},{6,30},{8,16},{10,18},{12,20},{14,22},{16,8},... | collective-permute-start | bytes 1474568 | tf_op jit(solution)/shard_map/ppermute | solution.py:19
  14.6 9.0 %collective-permute-start.2 = (bf16[64,1920]{1,0:T(8,128)(2,1)}, bf16[64,1920]{1,0:T(8,128)(2,1)S(1)}, u32[]{:S(2)}, u32[]{:S(2)}) collective-permute-start(bf16[64,1920]{1,0:T(8,128)(2,1)} %broadcast_select_fusion.17), channel_id=1, source_target_pairs={{0,4},{2,6},{4,0},{6,2},{8,12},{10,14},{12,8},{14,10},{16,20},{18,... | collective-permute-start | bytes 737288 | tf_op jit(solution)/shard_map/ppermute | solution.py:19
  33.0 13.0 %collective-permute-start.4 = (bf16[64,1920]{1,0:T(8,128)(2,1)S(1)}, bf16[64,1920]{1,0:T(8,128)(2,1)S(1)}, u32[]{:S(2)}, u32[]{:S(2)}) collective-permute-start(bf16[64,1920]{1,0:T(8,128)(2,1)S(1)} %broadcast_select_fusion.10), channel_id=1, source_target_pairs={{0,16},{2,18},{4,20},{6,22},{8,24},{10,26},{12,28},{14,30},{16,0},... | collective-permute-start | bytes 737288 | tf_op jit(solution)/shard_map/ppermute | solution.py:19
  55.8 10.9 %collective-permute-start.11 = (bf16[64,1920]{1,0:T(8,128)(2,1)}, bf16[64,1920]{1,0:T(8,128)(2,1)}, u32[]{:S(2)}, u32[]{:S(2)}) collective-permute-start(bf16[64,1920]{1,0:T(8,128)(2,1)} %broadcast_select_fusion.14), channel_id=1, source_target_pairs={{0,4},{2,6},{4,0},{6,2},{8,12},{10,14},{12,8},{14,10},{16,20},{18,... | collective-permute-start | bytes 737288 | tf_op jit(solution)/shard_map/ppermute | solution.py:19
  58.2 11.1 %collective-permute-start.6 = (bf16[64,3840]{1,0:T(8,128)(2,1)}, bf16[64,3840]{1,0:T(8,128)(2,1)}, u32[]{:S(2)}, u32[]{:S(2)}) collective-permute-start(bf16[64,3840]{1,0:T(8,128)(2,1)} %pad_maximum_fusion.12), channel_id=1, source_target_pairs={{0,2},{2,0},{4,6},{6,4},{8,10},{10,8},{12,14},{14,12},{16,18},{18,... | collective-permute-start | bytes 1474568 | tf_op jit(solution)/shard_map/ppermute | solution.py:19
  66.1 36.1 %collective-permute-start.29 = (bf16[640,384]{1,0:T(8,128)(2,1)S(1)}, bf16[640,384]{1,0:T(8,128)(2,1)S(1)}, u32[]{:S(2)}, u32[]{:S(2)}) collective-permute-start(bf16[640,384]{1,0:T(8,128)(2,1)S(1)} %collective-permute-done.27.refs_16_), channel_id=1, source_target_pairs={{0,4},{2,6},{4,0},{6,2},{8,12},{10,14},{12,8},{14,10},{16,20},{18,... | collective-permute-start | bytes 1474568 | tf_op jit(solution)/shard_map/ppermute | solution.py:19
  66.7 38.9 %collective-permute-start.28 = (bf16[640,384]{1,0:T(8,128)(2,1)S(1)}, bf16[640,384]{1,0:T(8,128)(2,1)S(1)}, u32[]{:S(2)}, u32[]{:S(2)}) collective-permute-start(bf16[640,384]{1,0:T(8,128)(2,1)S(1)} %collective-permute-done.27.refs_16_), channel_id=1, source_target_pairs={{0,2},{2,0},{4,6},{6,4},{8,10},{10,8},{12,14},{14,12},{16,18},{18,... | collective-permute-start | bytes 1474568 | tf_op jit(solution)/shard_map/ppermute | solution.py:19
  66.7 58.9 %collective-permute-start.17 = (bf16[640,384]{1,0:T(8,128)(2,1)S(1)}, bf16[640,384]{1,0:T(8,128)(2,1)S(1)}, u32[]{:S(2)}, u32[]{:S(2)}) collective-permute-start(bf16[640,384]{1,0:T(8,128)(2,1)S(1)} %pad_maximum_fusion.14.refs_4_), channel_id=1, source_target_pairs={{0,4},{2,6},{4,0},{6,2},{8,12},{10,14},{12,8},{14,10},{16,20},{18,... | collective-permute-start | bytes 1474568 | tf_op jit(solution)/shard_map/ppermute | solution.py:19
  69.2 8.2 %collective-permute-start.12 = (bf16[64,1920]{1,0:T(8,128)(2,1)S(1)}, bf16[64,1920]{1,0:T(8,128)(2,1)S(1)}, u32[]{:S(2)}, u32[]{:S(2)}) collective-permute-start(bf16[64,1920]{1,0:T(8,128)(2,1)S(1)} %select_select_fusion.2), channel_id=1, source_target_pairs={{0,8},{2,10},{4,12},{6,14},{8,0},{10,2},{12,4},{14,6},{16,24},{18,... | collective-permute-start | bytes 737288 | tf_op jit(solution)/shard_map/ppermute | solution.py:19
  77.4 48.5 %collective-permute-start.16 = (bf16[640,384]{1,0:T(8,128)(2,1)S(1)}, bf16[640,384]{1,0:T(8,128)(2,1)}, u32[]{:S(2)}, u32[]{:S(2)}) collective-permute-start(bf16[640,384]{1,0:T(8,128)(2,1)S(1)} %pad_maximum_fusion.14.refs_4_), channel_id=1, source_target_pairs={{0,2},{2,0},{4,6},{6,4},{8,10},{10,8},{12,14},{14,12},{16,18},{18,... | collective-permute-start | bytes 1474568 | tf_op jit(solution)/shard_map/ppermute | solution.py:19
  77.4 15.1 %collective-permute-start.13 = (bf16[64,1920]{1,0:T(8,128)(2,1)S(1)}, bf16[64,1920]{1,0:T(8,128)(2,1)S(1)}, u32[]{:S(2)}, u32[]{:S(2)}) collective-permute-start(bf16[64,1920]{1,0:T(8,128)(2,1)S(1)} %broadcast_select_fusion.8), channel_id=1, source_target_pairs={{0,16},{2,18},{4,20},{6,22},{8,24},{10,26},{12,28},{14,30},{16,0},... | collective-permute-start | bytes 737288 | tf_op jit(solution)/shard_map/ppermute | solution.py:19
  92.6 7.9 %collective-permute-start.14 = (bf16[64,1920]{1,0:T(8,128)(2,1)S(1)}, bf16[64,1920]{1,0:T(8,128)(2,1)S(1)}, u32[]{:S(2)}, u32[]{:S(2)}) collective-permute-start(bf16[64,1920]{1,0:T(8,128)(2,1)S(1)} %broadcast_select_fusion.9), channel_id=1, source_target_pairs={{0,4},{2,6},{4,0},{6,2},{8,12},{10,14},{12,8},{14,10},{16,20},{18,... | collective-permute-start | bytes 737288 | tf_op jit(solution)/shard_map/ppermute | solution.py:19
  100.4 25.6 %collective-permute-start.19 = (bf16[640,384]{1,0:T(8,128)(2,1)}, bf16[640,384]{1,0:T(8,128)(2,1)}, u32[]{:S(2)}, u32[]{:S(2)}) collective-permute-start(bf16[640,384]{1,0:T(8,128)(2,1)} %pad_maximum_fusion.15), channel_id=1, source_target_pairs={{0,8},{2,10},{4,12},{6,14},{8,0},{10,2},{12,4},{14,6},{16,24},{18,... | collective-permute-start | bytes 1474568 | tf_op jit(solution)/shard_map/ppermute | solution.py:19
  102.3 24.6 %collective-permute-start.23 = (bf16[640,384]{1,0:T(8,128)(2,1)}, bf16[640,384]{1,0:T(8,128)(2,1)}, u32[]{:S(2)}, u32[]{:S(2)}) collective-permute-start(bf16[640,384]{1,0:T(8,128)(2,1)} %pad_maximum_fusion.16), channel_id=1, source_target_pairs={{0,16},{2,18},{4,20},{6,22},{8,24},{10,26},{12,28},{14,30},{16,0},... | collective-permute-start | bytes 1474568 | tf_op jit(solution)/shard_map/ppermute | solution.py:19
  105.6 22.5 %collective-permute-start.15 = (bf16[64,3840]{1,0:T(8,128)(2,1)}, bf16[64,3840]{1,0:T(8,128)(2,1)}, u32[]{:S(2)}, u32[]{:S(2)}) collective-permute-start(bf16[64,3840]{1,0:T(8,128)(2,1)} %pad_maximum_fusion.13), channel_id=1, source_target_pairs={{0,2},{2,0},{4,6},{6,4},{8,10},{10,8},{12,14},{14,12},{16,18},{18,... | collective-permute-start | bytes 1474568 | tf_op jit(solution)/shard_map/ppermute | solution.py:19
  126.1 14.4 %collective-permute-start.21 = (bf16[640,384]{1,0:T(8,128)(2,1)}, bf16[640,384]{1,0:T(8,128)(2,1)}, u32[]{:S(2)}, u32[]{:S(2)}) collective-permute-start(bf16[640,384]{1,0:T(8,128)(2,1)} %collective-permute-done.19.refs_8_), channel_id=1, source_target_pairs={{0,4},{2,6},{4,0},{6,2},{8,12},{10,14},{12,8},{14,10},{16,20},{18,... | collective-permute-start | bytes 1474568 | tf_op jit(solution)/shard_map/ppermute | solution.py:19
  126.9 23.5 %collective-permute-start.25 = (bf16[640,384]{1,0:T(8,128)(2,1)}, bf16[640,384]{1,0:T(8,128)(2,1)}, u32[]{:S(2)}, u32[]{:S(2)}) collective-permute-start(bf16[640,384]{1,0:T(8,128)(2,1)} %collective-permute-done.23.refs_12_), channel_id=1, source_target_pairs={{0,4},{2,6},{4,0},{6,2},{8,12},{10,14},{12,8},{14,10},{16,20},{18,... | collective-permute-start | bytes 1474568 | tf_op jit(solution)/shard_map/ppermute | solution.py:19
  131.1 32.3 %collective-permute-start.20 = (bf16[640,384]{1,0:T(8,128)(2,1)}, bf16[640,384]{1,0:T(8,128)(2,1)}, u32[]{:S(2)}, u32[]{:S(2)}) collective-permute-start(bf16[640,384]{1,0:T(8,128)(2,1)} %collective-permute-done.19.refs_8_), channel_id=1, source_target_pairs={{0,2},{2,0},{4,6},{6,4},{8,10},{10,8},{12,14},{14,12},{16,18},{18,... | collective-permute-start | bytes 1474568 | tf_op jit(solution)/shard_map/ppermute | solution.py:19
  131.9 31.6 %collective-permute-start.24 = (bf16[640,384]{1,0:T(8,128)(2,1)}, bf16[640,384]{1,0:T(8,128)(2,1)}, u32[]{:S(2)}, u32[]{:S(2)}) collective-permute-start(bf16[640,384]{1,0:T(8,128)(2,1)} %collective-permute-done.23.refs_12_), channel_id=1, source_target_pairs={{0,2},{2,0},{4,6},{6,4},{8,10},{10,8},{12,14},{14,12},{16,18},{18,... | collective-permute-start | bytes 1474568 | tf_op jit(solution)/shard_map/ppermute | solution.py:19
  136.4 47.0 %collective-permute-start.8 = (bf16[320,384]{1,0:T(8,128)(2,1)}, bf16[320,384]{1,0:T(8,128)(2,1)}, u32[]{:S(2)}, u32[]{:S(2)}) collective-permute-start(bf16[320,384]{1,0:T(8,128)(2,1)} %get-tuple-element.51), channel_id=1, source_target_pairs={{0,16},{2,18},{4,20},{6,22},{8,24},{10,26},{12,28},{14,30},{16,0},... | collective-permute-start | bytes 737288 | tf_op jit(solution)/shard_map/ppermute | solution.py:19
  140.4 23.1 %collective-permute-start.22 = (bf16[640,384]{1,0:T(8,128)(2,1)}, bf16[640,384]{1,0:T(8,128)(2,1)}, u32[]{:S(2)}, u32[]{:S(2)}) collective-permute-start(bf16[640,384]{1,0:T(8,128)(2,1)} %collective-permute-done.21.refs_10_), channel_id=1, source_target_pairs={{0,2},{2,0},{4,6},{6,4},{8,10},{10,8},{12,14},{14,12},{16,18},{18,... | collective-permute-start | bytes 1474568 | tf_op jit(solution)/shard_map/ppermute | solution.py:19
  150.4 13.1 %collective-permute-start.26 = (bf16[640,384]{1,0:T(8,128)(2,1)}, bf16[640,384]{1,0:T(8,128)(2,1)}, u32[]{:S(2)}, u32[]{:S(2)}) collective-permute-start(bf16[640,384]{1,0:T(8,128)(2,1)} %collective-permute-done.25.refs_14_), channel_id=1, source_target_pairs={{0,2},{2,0},{4,6},{6,4},{8,10},{10,8},{12,14},{14,12},{16,18},{18,... | collective-permute-start | bytes 1474568 | tf_op jit(solution)/shard_map/ppermute | solution.py:19
  163.4 33.7 %collective-permute-start.7 = (bf16[320,384]{1,0:T(8,128)(2,1)}, bf16[320,384]{1,0:T(8,128)(2,1)S(1)}, u32[]{:S(2)}, u32[]{:S(2)}) collective-permute-start(bf16[320,384]{1,0:T(8,128)(2,1)} %get-tuple-element.52), channel_id=1, source_target_pairs={{0,24},{2,26},{4,28},{6,30},{8,16},{10,18},{12,20},{14,22},{16,8},... | collective-permute-start | bytes 737288 | tf_op jit(solution)/shard_map/ppermute | solution.py:19
  179.1 48.5 %collective-permute-start.31 = (bf16[320,384]{1,0:T(8,128)(2,1)S(1)}, bf16[320,384]{1,0:T(8,128)(2,1)}, u32[]{:S(2)}, u32[]{:S(2)}) collective-permute-start(bf16[320,384]{1,0:T(8,128)(2,1)S(1)} %block_attention.4), channel_id=1, source_target_pairs={{0,8},{2,10},{4,12},{6,14},{8,0},{10,2},{12,4},{14,6},{16,24},{18,... | collective-permute-start | bytes 737288 | tf_op jit(solution)/shard_map/ppermute | solution.py:19
  193.9 33.7 %collective-permute-start.32 = (bf16[320,384]{1,0:T(8,128)(2,1)}, bf16[320,384]{1,0:T(8,128)(2,1)}, u32[]{:S(2)}, u32[]{:S(2)}) collective-permute-start(bf16[320,384]{1,0:T(8,128)(2,1)} %block_attention.5), channel_id=1, source_target_pairs={{0,16},{2,18},{4,20},{6,22},{8,24},{10,26},{12,28},{14,30},{16,0},... | collective-permute-start | bytes 737288 | tf_op jit(solution)/shard_map/ppermute | solution.py:19
  203.5 24.1 %collective-permute-start.33 = (bf16[320,384]{1,0:T(8,128)(2,1)S(1)}, bf16[320,384]{1,0:T(8,128)(2,1)}, u32[]{:S(2)}, u32[]{:S(2)}) collective-permute-start(bf16[320,384]{1,0:T(8,128)(2,1)S(1)} %block_attention.6), channel_id=1, source_target_pairs={{0,24},{2,26},{4,28},{6,30},{8,16},{10,18},{12,20},{14,22},{16,8},... | collective-permute-start | bytes 737288 | tf_op jit(solution)/shard_map/ppermute | solution.py:19
  231.8 13.7 %collective-permute-start.35 = (bf16[320,768]{1,0:T(8,128)(2,1)S(1)}, bf16[320,768]{1,0:T(8,128)(2,1)S(1)}, u32[]{:S(2)}, u32[]{:S(2)}) collective-permute-start(bf16[320,768]{1,0:T(8,128)(2,1)S(1)} %fusion.23), channel_id=1, source_target_pairs={{0,1},{1,0},{2,3},{3,2},{4,5},{5,4},{6,7},{7,6},{8,9},{9,8},{10,11... | collective-permute-start | bytes 1474568 | tf_op jit(solution)/shard_map/ppermute | solution.py:273
  235.2 19.9 %collective-permute-start.36 = (bf16[320,768]{1,0:T(8,128)(2,1)S(1)}, bf16[320,768]{1,0:T(8,128)(2,1)S(1)}, u32[]{:S(2)}, u32[]{:S(2)}) collective-permute-start(bf16[320,768]{1,0:T(8,128)(2,1)S(1)} %fusion.26), channel_id=1, source_target_pairs={{0,1},{1,0},{2,3},{3,2},{4,5},{5,4},{6,7},{7,6},{8,9},{9,8},{10,11... | collective-permute-start | bytes 1474568 | tf_op jit(solution)/shard_map/ppermute | solution.py:273
  239.2 26.5 %collective-permute-start.37 = (bf16[320,768]{1,0:T(8,128)(2,1)S(1)}, bf16[320,768]{1,0:T(8,128)(2,1)S(1)}, u32[]{:S(2)}, u32[]{:S(2)}) collective-permute-start(bf16[320,768]{1,0:T(8,128)(2,1)S(1)} %fusion.29), channel_id=1, source_target_pairs={{0,1},{1,0},{2,3},{3,2},{4,5},{5,4},{6,7},{7,6},{8,9},{9,8},{10,11... | collective-permute-start | bytes 1474568 | tf_op jit(solution)/shard_map/ppermute | solution.py:273
  241.4 34.8 %collective-permute-start.34 = (bf16[320,768]{1,0:T(8,128)(2,1)S(1)}, bf16[320,768]{1,0:T(8,128)(2,1)S(1)}, u32[]{:S(2)}, u32[]{:S(2)}) collective-permute-start(bf16[320,768]{1,0:T(8,128)(2,1)S(1)} %fusion.20), channel_id=1, source_target_pairs={{0,1},{1,0},{2,3},{3,2},{4,5},{5,4},{6,7},{7,6},{8,9},{9,8},{10,11... | collective-permute-start | bytes 1474568 | tf_op jit(solution)/shard_map/ppermute | solution.py:273
  (46 other events, 370.0 us)

commit v4 on v3

--- a/solution.py
+++ b/solution.py
@@ -24,8 +24,6 @@
     me = lax.axis_index("ctx")
     cols = down.shape[0]
     buf = jnp.concatenate([down.T, up], axis=1)
-    if hold is not None:
-        buf, _ = lax.optimization_barrier((buf, hold))
     owner = jnp.where(jnp.arange(buf.shape[1]) < cols, down_owner, up_owner)[None, :]
     halved = []
     bit = 1
@@ -39,6 +37,9 @@
             owner = jnp.where(high, owner[:, half:], owner[:, :half])
             halved.append(bit)
         else:
+            if hold is not None:
+                buf, _ = lax.optimization_barrier((buf, hold))
+                hold = None
             received = swap(buf, bit)
             kept = buf
         buf = jnp.where((owner & bit) == (me & bit), kept, received)
@@ -199,19 +200,24 @@
     def columns(x, step):
         return lax.dynamic_slice_in_dim(x, (my_group ^ step) * width, width, 1)
 
-    gain = lax.all_gather(norm_gain_vector, "tp", axis=0, tiled=True)
     query_down_t, query_up, after_halving, fetched = fetch_pair(
         query_update_first[0], query_update_second[0], owners[0], owners[1]
     )
     if tp == 2:
-        other = lax.ppermute(tokens, "tp", [(0, 1), (1, 0)])
-        whole = jnp.concatenate(
-            [jnp.where(mine == 0, tokens, other), jnp.where(mine == 0, other, tokens)], axis=1
-        )
+
+        def both(x):
+            other = lax.ppermute(x, "tp", [(0, 1), (1, 0)])
+            return jnp.concatenate(
+                [jnp.where(mine == 0, x, other), jnp.where(mine == 0, other, x)], axis=1
+            )
+
+        whole, gain = both(tokens), both(norm_gain_vector[None, :])
     else:
+        gain = lax.all_gather(norm_gain_vector[None, :], "tp", axis=1, tiled=True)
         whole = lax.all_gather(tokens, "tp", axis=1, tiled=True)
 
     kv_parts = []
+    early = []
     for step in range(groups):
         part = jnp.concatenate([columns(keys, step), columns(values, step)], axis=0)
         if step == 0:
@@ -226,7 +232,12 @@
             have.update({j | bit: swap(x, bit) for j, x in list(have.items())})
             bit //= 2
         kv_parts += [have[j] for j in range(ranks)]
-
+        if step in (0, groups - 1):
+            early.append(have[ranks // 2])
+        else:
+            early.append(part)
+
+    query_down_t, _ = lax.optimization_barrier((query_down_t, early))
     features = whole.astype(jnp.float32)
     mean_square = jnp.mean(features * features, axis=-1, keepdims=True)
     normed = (features * lax.rsqrt(mean_square + norm_eps) * gain.astype(jnp.float32)).astype(
@@ -241,16 +252,17 @@
         q_parts.append(swap(part, step * ranks) if step else part)
 
     out_down_t, out_up, _, _ = fetch_pair(
-        output_update_first[0], output_update_second[0], owners[2], owners[3], hold=fetched
+        output_update_first[0], output_update_second[0], owners[2], owners[3], hold=queries
     )
     out_merged = merge_weight(output_frozen_weight, out_down_t, out_up)
 
     order = list(range(1, groups)) + [0]
     o_parts = [None] * groups
-    gate = out_merged
+    gate = None
     for step in order:
         q_part = q_parts[step]
-        q_part, _ = lax.optimization_barrier((q_part, gate))
+        if gate is not None:
+            q_part, _ = lax.optimization_barrier((q_part, (gate, out_merged) if step == 0 else gate))
         gate = attend(q_part, kv_parts, (my_group ^ step) * ranks + me % ranks, frame_block_number)
         o_parts[step] = swap(gate, step * ranks) if step else gate
     stacked = jnp.stack(o_parts)
@@ -264,7 +276,7 @@
             partial_value.astype(jnp.bfloat16), "tp", scatter_dimension=1, tiled=True
         )
     half = out_merged.shape[1] // 2
-    pieces = 4
+    pieces = 6
     step = half // pieces
     received = []
     for i in range(pieces):

time: 280 us -> 298 us (1.064)
  waiting for transfers between devices: 82.6 us -> 96.5 us
  other arithmetic: 36.2 us -> 27.8 us
  Pallas kernels: 45 us -> 53.1 us
  matrix products: 42.9 us -> 48.5 us
  starting transfers between devices: 40.9 us -> 46 us
  blocking collectives: 4.36 us -> 0 us
    ppermute x33, waiting for transfers between devices: 51.9 us -> 71.7 us  [swap(): return lax.ppermute(x, 'ctx', [(i, i ^ bit) for i in range(n)])]
    pallas_call x4, Pallas kernels: 45 us -> 53.1 us  [attend(): pl.pallas_call(functools.partial(attention_kernel, n, heads, rows), out_s...]
    ppermute x4 -> x6, waiting for transfers between devices: 30.7 us -> 24.9 us  [shards(): lax.ppermute(product.astype(jnp.bfloat16), 'tp', [(0, 1), (1, 0)])]
    all_gather x1 -> x0, blocking collectives: 4.36 us -> none  [shards(): gain = lax.all_gather(norm_gain_vector, 'tp', axis=0, tiled=True)]
    dot_general x4 -> x6, matrix products: 9.09 us -> 12.4 us  [shards(): product = jnp.dot(attended, theirs, preferred_element_type=jnp.float32)]
    select_n x4, other arithmetic: 4.63 us -> 1.42 us  [fetch_pair(): jnp.where(high, other, buf)]
    ppermute x4 -> x6, starting transfers between devices: 4.07 us -> 6.49 us  [shards(): lax.ppermute(product.astype(jnp.bfloat16), 'tp', [(0, 1), (1, 0)])]
    unnamed x80 -> x66, local copies, waits for them, and re-layouts: 8.89 us -> 9.36 us
  transfers between devices with their start and end apart: 38 -> 41, of which waited for: 13 -> 17; matrix products, arithmetic and copies ran while one was open for 28% -> 18% of each run, Pallas kernels for 16% -> 18%
where the time goes in v4:
time: 298 us
  waiting for transfers between devices  96.5 us (32%)
  Pallas kernels  53.1 us (18%)
  matrix products  48.5 us (16%)
  starting transfers between devices  46 us (15%)
  other arithmetic  27.8 us (9%)
  local copies, waits for them, and re-layouts  15.1 us (5%)
  between operations  10.8 us (4%)
    ppermute x33, waiting for transfers between devices, swap(): return lax.ppermute(x, 'ctx', [(i, i ^ bit) for i in range(n)])  71.7 us
    pallas_call x4, Pallas kernels, attend(): pl.pallas_call(functools.partial(attention_kernel, n, heads, rows), out_s...  53.1 us
    ppermute x33, starting transfers between devices, swap(): return lax.ppermute(x, 'ctx', [(i, i ^ bit) for i in range(n)])  37.4 us
    ppermute x6, waiting for transfers between devices, shards(): lax.ppermute(product.astype(jnp.bfloat16), 'tp', [(0, 1), (1, 0)])  24.9 us
    dot_general x1, matrix products, shards(): jnp.dot(normed, query_merged, preferred_element_type=jnp.float32)  17.4 us
    dot_general x1, matrix products, merge_weight(): lax.dot_general(down_t, up, (((0,), (0,)), ((), ())), preferred_element_t...  12.9 us
    dot_general x6, matrix products, shards(): product = jnp.dot(attended, theirs, preferred_element_type=jnp.float32)  12.4 us
    unnamed x66, local copies, waits for them, and re-layouts  9.36 us
  transfers between devices with their start and end apart: 41, of which 17 were waited for; matrix products, arithmetic and copies ran while one was open for 18% of the time, Pallas kernels for 18%

profile of v4, /device:TPU:28, one launch (start us, length us, event | category | flops | bytes accessed | tf_op | source)
XLA Modules:
  0.0 297.9 jit_solution(17109986560419166819)
XLA Ops:
  0.0 2.2 broadcast_select_fusion.4
  14.6 6.7 %collective-permute-done.3 = bf16[64,1920]{1,0:T(8,128)(2,1)S(1)} collective-permute-done((bf16[64,1920]{1,0:T(8,128)(2,1)S(1)}, bf16[64,1920]{1,0:T(8,128)(2,1)S(1)}, u32[]{:S(2)}, u32[]{:S(2)}) %collective-permute-start.3) | collective-permute-done | bytes 245792 | tf_op jit(solution)/shard_map/ppermute | solution.py:19
  22.3 5.4 %collective-permute-done.4 = bf16[64,1920]{1,0:T(8,128)(2,1)S(1)} collective-permute-done((bf16[64,1920]{1,0:T(8,128)(2,1)S(1)}, bf16[64,1920]{1,0:T(8,128)(2,1)S(1)}, u32[]{:S(2)}, u32[]{:S(2)}) %collective-permute-start.4) | collective-permute-done | bytes 245792 | tf_op jit(solution)/shard_map/ppermute | solution.py:19
  27.7 2.4 collective-permute-start.5
  31.3 8.5 %collective-permute-done.5 = bf16[64,1920]{1,0:T(8,128)(2,1)S(1)} collective-permute-done((bf16[64,1920]{1,0:T(8,128)(2,1)S(1)}, bf16[64,1920]{1,0:T(8,128)(2,1)S(1)}, u32[]{:S(2)}, u32[]{:S(2)}) %collective-permute-start.5) | collective-permute-done | bytes 245792 | tf_op jit(solution)/shard_map/ppermute | solution.py:19
  42.0 6.8 %collective-permute-done.6 = bf16[64,1920]{1,0:T(8,128)(2,1)S(1)} collective-permute-done((bf16[64,1920]{1,0:T(8,128)(2,1)S(1)}, bf16[64,1920]{1,0:T(8,128)(2,1)S(1)}, u32[]{:S(2)}, u32[]{:S(2)}) %collective-permute-start.6) | collective-permute-done | bytes 245792 | tf_op jit(solution)/shard_map/ppermute | solution.py:19
  53.4 3.4 %collective-permute-start.10 = (bf16[640,384]{1,0:T(8,128)(2,1)S(1)}, bf16[640,384]{1,0:T(8,128)(2,1)}, u32[]{:S(2)}, u32[]{:S(2)}) collective-permute-start(bf16[640,384]{1,0:T(8,128)(2,1)S(1)} %copy-done.28), channel_id=1, source_target_pairs={{0,16},{2,18},{4,20},{6,22},{8,24},{10,26},{12,28},{14,30},{16,0},... | collective-permute-start | bytes 1474568 | tf_op jit(solution)/shard_map/ppermute | solution.py:19
  57.8 5.6 %collective-permute-done.12.refs_18_ = bf16[640,384]{1,0:T(8,128)(2,1)S(1)} collective-permute-done((bf16[640,384]{1,0:T(8,128)(2,1)S(1)}, bf16[640,384]{1,0:T(8,128)(2,1)S(1)}, u32[]{:S(2)}, u32[]{:S(2)}) %collective-permute-start.12) | collective-permute-done | bytes 491552 | tf_op jit(solution)/shard_map/ppermute | solution.py:19
  63.5 10.1 %collective-permute-done.8.refs_6_ = bf16[640,384]{1,0:T(8,128)(2,1)S(1)} collective-permute-done((bf16[640,384]{1,0:T(8,128)(2,1)S(1)}, bf16[640,384]{1,0:T(8,128)(2,1)S(1)}, u32[]{:S(2)}, u32[]{:S(2)}) %collective-permute-start.8) | collective-permute-done | bytes 491552 | tf_op jit(solution)/shard_map/ppermute | solution.py:19
  76.8 2.4 broadcast_select_fusion.1
  81.2 17.4 %fusion.9 = bf16[320,1536]{1,0:T(8,128)(2,1)} fusion(bf16[6144,1536]{1,0:T(8,128)(2,1)} %param.16, bf16[64,6144]{1,0:T(8,128)(2,1)} %pad_maximum_fusion.6, f32[6144]{0:T(1024)S(1)} %maximum_convert_fusion, f32[320]{0:T(512)S(1)} %add_rsqrt_fusion, bf16[320,3072]{1,0:T(8,128)(2,1)} %copy-done.19, bf16[320,3072]{1,0:T(8,128)(2,1)} %copy-done.18, ...), kind=kOutput, calls=%fused_computation.13 | convolution fusion | flops 7290322944 | bytes 24799232 | tf_op jit(solution)/shard_map/dot_general | solution.py:247
  100.2 5.9 %fusion.67 = (s32[]{:T(128)}, s32[]{:T(128)}, s32[]{:T(128)}, s32[]{:T(128)}, s32[]{:T(128)}, /*index=5*/s32[]{:T(128)}, s32[]{:T(128)}, s32[]{:T(128)}) fusion(s32[80]{0:T(128)S(1)} %copy-done.31, s32[]{:T(128)} %bitcast, s32[]{:T(128)} %bitcast.17, s32[]{:T(128)} %bitcast.15, s32[]{:T(128)} %bitcast.13, s32[]{:T(128)} %bitcast.11, s32[]{:T(128)} %bitcast.2, ...), kind=kLoop, calls=%fused_computation.138 | loop fusion | flops 1912 | bytes 384 | tf_op jit(solution)/shard_map/reduce_sum | solution.py:148
  109.7 2.7 collective-permute-start.29
  129.6 6.6 %collective-permute-done.19.refs_10_ = bf16[640,384]{1,0:T(8,128)(2,1)S(1)} collective-permute-done((bf16[640,384]{1,0:T(8,128)(2,1)S(1)}, bf16[640,384]{1,0:T(8,128)(2,1)S(1)}, u32[]{:S(2)}, u32[]{:S(2)}) %collective-permute-start.19) | collective-permute-done | bytes 491552 | tf_op jit(solution)/shard_map/ppermute | solution.py:19
  136.3 10.5 %collective-permute-done.22.refs_14_ = bf16[640,384]{1,0:T(8,128)(2,1)S(1)} collective-permute-done((bf16[640,384]{1,0:T(8,128)(2,1)}, bf16[640,384]{1,0:T(8,128)(2,1)S(1)}, u32[]{:S(2)}, u32[]{:S(2)}) %collective-permute-start.22) | collective-permute-done | bytes 491552 | tf_op jit(solution)/shard_map/ppermute | solution.py:19
  146.8 4.6 %collective-permute-done.30 = bf16[64,1920]{1,0:T(8,128)(2,1)S(1)} collective-permute-done((bf16[64,1920]{1,0:T(8,128)(2,1)S(1)}, bf16[64,1920]{1,0:T(8,128)(2,1)S(1)}, u32[]{:S(2)}, u32[]{:S(2)}) %collective-permute-start.30) | collective-permute-done | bytes 245792 | tf_op jit(solution)/shard_map/ppermute | solution.py:19
  151.9 2.2 collective-permute-start.13
  154.1 14.8 %block_attention.4 = bf16[320,384]{1,0:T(8,128)(2,1)} custom-call(s32[3]{0:T(128)S(1)} %add_add_fusion.3.refs_0_, s32[8,1,640]{2,1,0:T(1,128)S(1)} %broadcast_in_dim.132.refs_1_, s32[320,1]{1,0:T(8,128)S(1)} %reshape_reshape.23.refs_2_, bf16[320,384]{1,0:T(8,128)(2,1)S(1)} %collective-permute-done.15.refs_3_, ...), custom_call_target="tpu_custom_call" | custom-call | flops 2516582400 | bytes 8355840 | tf_op jit(solution)/shard_map/block_attention/pallas_call | solution.py:155
  168.9 4.1 %collective-permute-start.32 = (bf16[320,384]{1,0:T(8,128)(2,1)}, bf16[320,384]{1,0:T(8,128)(2,1)}, u32[]{:S(2)}, u32[]{:S(2)}) collective-permute-start(bf16[320,384]{1,0:T(8,128)(2,1)} %block_attention.4), channel_id=1, source_target_pairs={{0,8},{2,10},{4,12},{6,14},{8,0},{10,2},{12,4},{14,6},{16,24},{18,... | collective-permute-start | bytes 737288 | tf_op jit(solution)/shard_map/ppermute | solution.py:19
  173.1 12.1 %block_attention.5 = bf16[320,384]{1,0:T(8,128)(2,1)} custom-call(s32[3]{0:T(128)S(1)} %add_add_fusion.2.refs_0_, s32[8,1,640]{2,1,0:T(1,128)S(1)} %broadcast_in_dim.132.refs_1_, s32[320,1]{1,0:T(8,128)S(1)} %reshape_reshape.22.refs_2_, bf16[320,384]{1,0:T(8,128)(2,1)S(1)} %collective-permute-done.14.refs_3_, ...), custom_call_target="tpu_custom_call" | custom-call | flops 2516582400 | bytes 8355840 | tf_op jit(solution)/shard_map/block_attention/pallas_call | solution.py:155
  185.2 3.3 %collective-permute-start.33 = (bf16[320,384]{1,0:T(8,128)(2,1)}, bf16[320,384]{1,0:T(8,128)(2,1)}, u32[]{:S(2)}, u32[]{:S(2)}) collective-permute-start(bf16[320,384]{1,0:T(8,128)(2,1)} %block_attention.5), channel_id=1, source_target_pairs={{0,16},{2,18},{4,20},{6,22},{8,24},{10,26},{12,28},{14,30},{16,0},... | collective-permute-start | bytes 737288 | tf_op jit(solution)/shard_map/ppermute | solution.py:19
  188.5 8.9 %block_attention.6 = bf16[320,384]{1,0:T(8,128)(2,1)} custom-call(s32[3]{0:T(128)S(1)} %add_add_fusion.1.refs_0_, s32[8,1,640]{2,1,0:T(1,128)S(1)} %broadcast_in_dim.132.refs_1_, s32[320,1]{1,0:T(8,128)S(1)} %reshape_reshape.21.refs_2_, bf16[320,384]{1,0:T(8,128)(2,1)S(1)} %collective-permute-done.13.refs_3_, ...), custom_call_target="tpu_custom_call" | custom-call | flops 2516582400 | bytes 8355840 | tf_op jit(solution)/shard_map/block_attention/pallas_call | solution.py:155
  197.4 8.3 %collective-permute-start.34 = (bf16[320,384]{1,0:T(8,128)(2,1)}, bf16[320,384]{1,0:T(8,128)(2,1)}, u32[]{:S(2)}, u32[]{:S(2)}) collective-permute-start(bf16[320,384]{1,0:T(8,128)(2,1)} %block_attention.6), channel_id=1, source_target_pairs={{0,24},{2,26},{4,28},{6,30},{8,16},{10,18},{12,20},{14,22},{16,8},... | collective-permute-start | bytes 737288 | tf_op jit(solution)/shard_map/ppermute | solution.py:19
  206.8 12.9 %add_convert_fusion = bf16[1536,6144]{1,0:T(8,128)(2,1)} fusion(bf16[1536,6144]{1,0:T(8,128)(2,1)} %param.17, bf16[64,3840]{1,0:T(8,128)(2,1)} %get-tuple-element.52, bf16[64,3840]{1,0:T(8,128)(2,1)} %get-tuple-element.51), kind=kOutput, calls=%fused_computation | convolution fusion | flops 1237843968 | bytes 38928384 | tf_op jit(solution)/shard_map/dot_general | solution.py:60
  228.0 17.4 %block_attention.7 = bf16[320,384]{1,0:T(8,128)(2,1)S(1)} custom-call(s32[3]{0:T(128)S(1)} %add_add_fusion.refs_0_, s32[8,1,640]{2,1,0:T(1,128)S(1)} %broadcast_in_dim.132.refs_1_, s32[320,1]{1,0:T(8,128)S(1)} %reshape_reshape.20.refs_2_, bf16[320,384]{1,0:T(8,128)(2,1)S(1)} %get-tuple-element.20.refs_3_, bf16[640,384]{1,0:T(8,128)(2,1)S(1)} %pad_maximum_fusion.10.refs_4_, ...), custom_call_target="tpu_custom_call" | custom-call | flops 2516582400 | bytes 8355840 | tf_op jit(solution)/shard_map/block_attention/pallas_call | solution.py:155
  246.9 2.1 fusion.24
  250.5 5.8 %fusion = f32[320,3072]{1,0:T(8,128)S(1)} fusion(bf16[1536,6144]{1,0:T(8,128)(2,1)} %add_convert_fusion, s32[]{:T(128)S(6)} %select_n.336, bf16[320,384]{1,0:T(8,128)(2,1)S(1)} %get-tuple-element.44, bf16[320,384]{1,0:T(8,128)(2,1)S(1)} %get-tuple-element.45, bf16[320,384]{1,0:T(8,128)(2,1)S(1)} %get-tuple-element.46, bf16[320,384]{1,0:T(8,128)(2,1)S(1)} %get-tuple-element.43), kind=kOutput, calls=%fused_computation.4 | convolution fusion | flops 3023831040 | bytes 14352388 | tf_op jit(solution)/shard_map/dot_general | solution.py:287
  256.3 2.1 fusion.27
  271.9 4.2 %collective-permute-done.37 = bf16[320,512]{1,0:T(8,128)(2,1)S(1)} collective-permute-done((bf16[320,512]{1,0:T(8,128)(2,1)S(1)}, bf16[320,512]{1,0:T(8,128)(2,1)S(1)}, u32[]{:S(2)}, u32[]{:S(2)}) %collective-permute-start.37) | collective-permute-done | bytes 327712 | tf_op jit(solution)/shard_map/ppermute | solution.py:285
  276.1 6.9 %collective-permute-done.38 = bf16[320,512]{1,0:T(8,128)(2,1)S(1)} collective-permute-done((bf16[320,512]{1,0:T(8,128)(2,1)S(1)}, bf16[320,512]{1,0:T(8,128)(2,1)S(1)}, u32[]{:S(2)}, u32[]{:S(2)}) %collective-permute-start.38) | collective-permute-done | bytes 327712 | tf_op jit(solution)/shard_map/ppermute | solution.py:285
  283.2 6.9 %collective-permute-done.39 = bf16[320,512]{1,0:T(8,128)(2,1)S(1)} collective-permute-done((bf16[320,512]{1,0:T(8,128)(2,1)S(1)}, bf16[320,512]{1,0:T(8,128)(2,1)S(1)}, u32[]{:S(2)}, u32[]{:S(2)}) %collective-permute-start.39) | collective-permute-done | bytes 327712 | tf_op jit(solution)/shard_map/ppermute | solution.py:285
  290.2 6.9 %collective-permute-done.40 = bf16[320,512]{1,0:T(8,128)(2,1)S(1)} collective-permute-done((bf16[320,512]{1,0:T(8,128)(2,1)S(1)}, bf16[320,512]{1,0:T(8,128)(2,1)S(1)}, u32[]{:S(2)}, u32[]{:S(2)}) %collective-permute-start.40) | collective-permute-done | bytes 327712 | tf_op jit(solution)/shard_map/ppermute | solution.py:285
  (194 shorter events, 67.2 us)
Async XLA Ops:
  2.2 27.9 %collective-permute-start.26 = (bf16[64,3840]{1,0:T(8,128)(2,1)}, bf16[64,3840]{1,0:T(8,128)(2,1)}, u32[]{:S(2)}, u32[]{:S(2)}) collective-permute-start(bf16[64,3840]{1,0:T(8,128)(2,1)} %broadcast_select_fusion.4), channel_id=1, source_target_pairs={{0,2},{2,0},{4,6},{6,4},{8,10},{10,8},{12,14},{14,12},{16,18},{18,... | collective-permute-start | bytes 1474568 | tf_op jit(solution)/shard_map/ppermute | solution.py:19
  3.1 9.6 %collective-permute-start.2 = (bf16[64,3840]{1,0:T(8,128)(2,1)}, bf16[64,3840]{1,0:T(8,128)(2,1)}, u32[]{:S(2)}, u32[]{:S(2)}) collective-permute-start(bf16[64,3840]{1,0:T(8,128)(2,1)} %broadcast_select_fusion.7), channel_id=1, source_target_pairs={{0,2},{2,0},{4,6},{6,4},{8,10},{10,8},{12,14},{14,12},{16,18},{18,... | collective-permute-start | bytes 1474568 | tf_op jit(solution)/shard_map/ppermute | solution.py:19
  5.5 43.5 %collective-permute-start.11 = (bf16[640,384]{1,0:T(8,128)(2,1)}, bf16[640,384]{1,0:T(8,128)(2,1)S(1)}, u32[]{:S(2)}, u32[]{:S(2)}) collective-permute-start(bf16[640,384]{1,0:T(8,128)(2,1)} %pad_maximum_fusion.13), channel_id=1, source_target_pairs={{0,24},{2,26},{4,28},{6,30},{8,16},{10,18},{12,20},{14,22},{16,8},... | collective-permute-start | bytes 1474568 | tf_op jit(solution)/shard_map/ppermute | solution.py:19
  5.7 16.5 %collective-permute-start.1 = (bf16[1,3072]{1,0:T(2,128)(2,1)S(1)}, bf16[1,3072]{1,0:T(2,128)(2,1)S(1)}, u32[]{:S(2)}, u32[]{:S(2)}) collective-permute-start(bf16[1,3072]{1,0:T(2,128)(2,1)S(1)} %broadcast_in_dim.108), channel_id=1, source_target_pairs={{0,1},{1,0},{2,3},{3,2},{4,5},{5,4},{6,7},{7,6},{8,9},{9,8},{10,11... | collective-permute-start | bytes 18440 | tf_op jit(solution)/shard_map/ppermute | solution.py:209
  7.3 69.6 %collective-permute-start = (bf16[320,3072]{1,0:T(8,128)(2,1)}, bf16[320,3072]{1,0:T(8,128)(2,1)}, u32[]{:S(2)}, u32[]{:S(2)}) collective-permute-start(bf16[320,3072]{1,0:T(8,128)(2,1)} %param.12), channel_id=1, source_target_pairs={{0,1},{1,0},{2,3},{3,2},{4,5},{5,4},{6,7},{7,6},{8,9},{9,8},{10,11... | collective-permute-start | bytes 5898248 | tf_op jit(solution)/shard_map/ppermute | solution.py:209
  27.7 12.1 %collective-permute-start.5 = (bf16[64,1920]{1,0:T(8,128)(2,1)S(1)}, bf16[64,1920]{1,0:T(8,128)(2,1)S(1)}, u32[]{:S(2)}, u32[]{:S(2)}) collective-permute-start(bf16[64,1920]{1,0:T(8,128)(2,1)S(1)} %broadcast_select_fusion.10), channel_id=1, source_target_pairs={{0,16},{2,18},{4,20},{6,22},{8,24},{10,26},{12,28},{14,30},{16,0},... | collective-permute-start | bytes 737288 | tf_op jit(solution)/shard_map/ppermute | solution.py:19
  40.5 12.4 %collective-permute-start.27 = (bf16[64,1920]{1,0:T(8,128)(2,1)S(1)}, bf16[64,1920]{1,0:T(8,128)(2,1)S(1)}, u32[]{:S(2)}, u32[]{:S(2)}) collective-permute-start(bf16[64,1920]{1,0:T(8,128)(2,1)S(1)} %broadcast_select_fusion.14), channel_id=1, source_target_pairs={{0,4},{2,6},{4,0},{6,2},{8,12},{10,14},{12,8},{14,10},{16,20},{18,... | collective-permute-start | bytes 737288 | tf_op jit(solution)/shard_map/ppermute | solution.py:19
  49.0 14.5 %collective-permute-start.12 = (bf16[640,384]{1,0:T(8,128)(2,1)S(1)}, bf16[640,384]{1,0:T(8,128)(2,1)S(1)}, u32[]{:S(2)}, u32[]{:S(2)}) collective-permute-start(bf16[640,384]{1,0:T(8,128)(2,1)S(1)} %collective-permute-done.11.refs_16_), channel_id=1, source_target_pairs={{0,4},{2,6},{4,0},{6,2},{8,12},{10,14},{12,8},{14,10},{16,20},{18,... | collective-permute-start | bytes 1474568 | tf_op jit(solution)/shard_map/ppermute | solution.py:19
  49.6 24.0 %collective-permute-start.8 = (bf16[640,384]{1,0:T(8,128)(2,1)S(1)}, bf16[640,384]{1,0:T(8,128)(2,1)S(1)}, u32[]{:S(2)}, u32[]{:S(2)}) collective-permute-start(bf16[640,384]{1,0:T(8,128)(2,1)S(1)} %pad_maximum_fusion.10.refs_4_), channel_id=1, source_target_pairs={{0,4},{2,6},{4,0},{6,2},{8,12},{10,14},{12,8},{14,10},{16,20},{18,... | collective-permute-start | bytes 1474568 | tf_op jit(solution)/shard_map/ppermute | solution.py:19
  53.0 21.8 %collective-permute-start.9 = (bf16[640,384]{1,0:T(8,128)(2,1)S(1)}, bf16[640,384]{1,0:T(8,128)(2,1)S(1)}, u32[]{:S(2)}, u32[]{:S(2)}) collective-permute-start(bf16[640,384]{1,0:T(8,128)(2,1)S(1)} %copy-done.27), channel_id=1, source_target_pairs={{0,8},{2,10},{4,12},{6,14},{8,0},{10,2},{12,4},{14,6},{16,24},{18,... | collective-permute-start | bytes 1474568 | tf_op jit(solution)/shard_map/ppermute | solution.py:19
  53.4 23.5 %collective-permute-start.10 = (bf16[640,384]{1,0:T(8,128)(2,1)S(1)}, bf16[640,384]{1,0:T(8,128)(2,1)}, u32[]{:S(2)}, u32[]{:S(2)}) collective-permute-start(bf16[640,384]{1,0:T(8,128)(2,1)S(1)} %copy-done.28), channel_id=1, source_target_pairs={{0,16},{2,18},{4,20},{6,22},{8,24},{10,26},{12,28},{14,30},{16,0},... | collective-permute-start | bytes 1474568 | tf_op jit(solution)/shard_map/ppermute | solution.py:19
  98.5 10.2 %collective-permute-start.28 = (bf16[64,1920]{1,0:T(8,128)(2,1)S(1)}, bf16[64,1920]{1,0:T(8,128)(2,1)S(1)}, u32[]{:S(2)}, u32[]{:S(2)}) collective-permute-start(bf16[64,1920]{1,0:T(8,128)(2,1)S(1)} %select_select_fusion.2), channel_id=1, source_target_pairs={{0,8},{2,10},{4,12},{6,14},{8,0},{10,2},{12,4},{14,6},{16,24},{18,... | collective-permute-start | bytes 737288 | tf_op jit(solution)/shard_map/ppermute | solution.py:19
  108.7 13.5 %collective-permute-start.24 = (bf16[640,384]{1,0:T(8,128)(2,1)S(1)}, bf16[640,384]{1,0:T(8,128)(2,1)}, u32[]{:S(2)}, u32[]{:S(2)}) collective-permute-start(bf16[640,384]{1,0:T(8,128)(2,1)S(1)} %collective-permute-done.11.refs_16_), channel_id=1, source_target_pairs={{0,2},{2,0},{4,6},{6,4},{8,10},{10,8},{12,14},{14,12},{16,18},{18,... | collective-permute-start | bytes 1474568 | tf_op jit(solution)/shard_map/ppermute | solution.py:19
  109.7 14.7 %collective-permute-start.29 = (bf16[64,1920]{1,0:T(8,128)(2,1)S(1)}, bf16[64,1920]{1,0:T(8,128)(2,1)}, u32[]{:S(2)}, u32[]{:S(2)}) collective-permute-start(bf16[64,1920]{1,0:T(8,128)(2,1)S(1)} %broadcast_select_fusion.8), channel_id=1, source_target_pairs={{0,16},{2,18},{4,20},{6,22},{8,24},{10,26},{12,28},{14,30},{16,0},... | collective-permute-start | bytes 737288 | tf_op jit(solution)/shard_map/ppermute | solution.py:19
  122.2 14.0 %collective-permute-start.19 = (bf16[640,384]{1,0:T(8,128)(2,1)S(1)}, bf16[640,384]{1,0:T(8,128)(2,1)S(1)}, u32[]{:S(2)}, u32[]{:S(2)}) collective-permute-start(bf16[640,384]{1,0:T(8,128)(2,1)S(1)} %collective-permute-done.9.refs_8_), channel_id=1, source_target_pairs={{0,4},{2,6},{4,0},{6,2},{8,12},{10,14},{12,8},{14,10},{16,20},{18,... | collective-permute-start | bytes 1474568 | tf_op jit(solution)/shard_map/ppermute | solution.py:19
  124.5 22.3 %collective-permute-start.22 = (bf16[640,384]{1,0:T(8,128)(2,1)}, bf16[640,384]{1,0:T(8,128)(2,1)S(1)}, u32[]{:S(2)}, u32[]{:S(2)}) collective-permute-start(bf16[640,384]{1,0:T(8,128)(2,1)} %collective-permute-done.10.refs_12_), channel_id=1, source_target_pairs={{0,4},{2,6},{4,0},{6,2},{8,12},{10,14},{12,8},{14,10},{16,20},{18,... | collective-permute-start | bytes 1474568 | tf_op jit(solution)/shard_map/ppermute | solution.py:19
  126.0 25.5 %collective-permute-start.30 = (bf16[64,1920]{1,0:T(8,128)(2,1)S(1)}, bf16[64,1920]{1,0:T(8,128)(2,1)S(1)}, u32[]{:S(2)}, u32[]{:S(2)}) collective-permute-start(bf16[64,1920]{1,0:T(8,128)(2,1)S(1)} %broadcast_select_fusion.9), channel_id=1, source_target_pairs={{0,4},{2,6},{4,0},{6,2},{8,12},{10,14},{12,8},{14,10},{16,20},{18,... | collective-permute-start | bytes 737288 | tf_op jit(solution)/shard_map/ppermute | solution.py:19
  129.1 22.8 %collective-permute-start.18 = (bf16[640,384]{1,0:T(8,128)(2,1)S(1)}, bf16[640,384]{1,0:T(8,128)(2,1)S(1)}, u32[]{:S(2)}, u32[]{:S(2)}) collective-permute-start(bf16[640,384]{1,0:T(8,128)(2,1)S(1)} %collective-permute-done.9.refs_8_), channel_id=1, source_target_pairs={{0,2},{2,0},{4,6},{6,4},{8,10},{10,8},{12,14},{14,12},{16,18},{18,... | collective-permute-start | bytes 1474568 | tf_op jit(solution)/shard_map/ppermute | solution.py:19
  129.2 24.9 %collective-permute-start.21 = (bf16[640,384]{1,0:T(8,128)(2,1)}, bf16[640,384]{1,0:T(8,128)(2,1)S(1)}, u32[]{:S(2)}, u32[]{:S(2)}) collective-permute-start(bf16[640,384]{1,0:T(8,128)(2,1)} %collective-permute-done.10.refs_12_), channel_id=1, source_target_pairs={{0,2},{2,0},{4,6},{6,4},{8,10},{10,8},{12,14},{14,12},{16,18},{18,... | collective-permute-start | bytes 1474568 | tf_op jit(solution)/shard_map/ppermute | solution.py:19
  136.2 15.2 %collective-permute-start.15 = (bf16[320,384]{1,0:T(8,128)(2,1)S(1)}, bf16[320,384]{1,0:T(8,128)(2,1)S(1)}, u32[]{:S(2)}, u32[]{:S(2)}) collective-permute-start(bf16[320,384]{1,0:T(8,128)(2,1)S(1)} %get-tuple-element.48), channel_id=1, source_target_pairs={{0,8},{2,10},{4,12},{6,14},{8,0},{10,2},{12,4},{14,6},{16,24},{18,... | collective-permute-start | bytes 737288 | tf_op jit(solution)/shard_map/ppermute | solution.py:19
  151.5 21.6 %collective-permute-start.14 = (bf16[320,384]{1,0:T(8,128)(2,1)S(1)}, bf16[320,384]{1,0:T(8,128)(2,1)S(1)}, u32[]{:S(2)}, u32[]{:S(2)}) collective-permute-start(bf16[320,384]{1,0:T(8,128)(2,1)S(1)} %get-tuple-element.49), channel_id=1, source_target_pairs={{0,16},{2,18},{4,20},{6,22},{8,24},{10,26},{12,28},{14,30},{16,0},... | collective-permute-start | bytes 737288 | tf_op jit(solution)/shard_map/ppermute | solution.py:19
  151.9 36.6 %collective-permute-start.13 = (bf16[320,384]{1,0:T(8,128)(2,1)S(1)}, bf16[320,384]{1,0:T(8,128)(2,1)S(1)}, u32[]{:S(2)}, u32[]{:S(2)}) collective-permute-start(bf16[320,384]{1,0:T(8,128)(2,1)S(1)} %get-tuple-element.50), channel_id=1, source_target_pairs={{0,24},{2,26},{4,28},{6,30},{8,16},{10,18},{12,20},{14,22},{16,8},... | collective-permute-start | bytes 737288 | tf_op jit(solution)/shard_map/ppermute | solution.py:19
  154.1 51.6 %collective-permute-start.31 = (bf16[64,3840]{1,0:T(8,128)(2,1)S(1)}, bf16[64,3840]{1,0:T(8,128)(2,1)S(1)}, u32[]{:S(2)}, u32[]{:S(2)}) collective-permute-start(bf16[64,3840]{1,0:T(8,128)(2,1)S(1)} %pad_maximum_fusion.14), channel_id=1, source_target_pairs={{0,2},{2,0},{4,6},{6,4},{8,10},{10,8},{12,14},{14,12},{16,18},{18,... | collective-permute-start | bytes 1474568 | tf_op jit(solution)/shard_map/ppermute | solution.py:19
  168.9 76.4 %collective-permute-start.32 = (bf16[320,384]{1,0:T(8,128)(2,1)}, bf16[320,384]{1,0:T(8,128)(2,1)}, u32[]{:S(2)}, u32[]{:S(2)}) collective-permute-start(bf16[320,384]{1,0:T(8,128)(2,1)} %block_attention.4), channel_id=1, source_target_pairs={{0,8},{2,10},{4,12},{6,14},{8,0},{10,2},{12,4},{14,6},{16,24},{18,... | collective-permute-start | bytes 737288 | tf_op jit(solution)/shard_map/ppermute | solution.py:19
  185.2 60.2 %collective-permute-start.33 = (bf16[320,384]{1,0:T(8,128)(2,1)}, bf16[320,384]{1,0:T(8,128)(2,1)}, u32[]{:S(2)}, u32[]{:S(2)}) collective-permute-start(bf16[320,384]{1,0:T(8,128)(2,1)} %block_attention.5), channel_id=1, source_target_pairs={{0,16},{2,18},{4,20},{6,22},{8,24},{10,26},{12,28},{14,30},{16,0},... | collective-permute-start | bytes 737288 | tf_op jit(solution)/shard_map/ppermute | solution.py:19
  197.4 48.0 %collective-permute-start.34 = (bf16[320,384]{1,0:T(8,128)(2,1)}, bf16[320,384]{1,0:T(8,128)(2,1)}, u32[]{:S(2)}, u32[]{:S(2)}) collective-permute-start(bf16[320,384]{1,0:T(8,128)(2,1)} %block_attention.6), channel_id=1, source_target_pairs={{0,24},{2,26},{4,28},{6,30},{8,16},{10,18},{12,20},{14,22},{16,8},... | collective-permute-start | bytes 737288 | tf_op jit(solution)/shard_map/ppermute | solution.py:19
  248.9 22.1 %collective-permute-start.35 = (bf16[320,512]{1,0:T(8,128)(2,1)S(1)}, bf16[320,512]{1,0:T(8,128)(2,1)S(1)}, u32[]{:S(2)}, u32[]{:S(2)}) collective-permute-start(bf16[320,512]{1,0:T(8,128)(2,1)S(1)} %fusion.24), channel_id=1, source_target_pairs={{0,1},{1,0},{2,3},{3,2},{4,5},{5,4},{6,7},{7,6},{8,9},{9,8},{10,11... | collective-permute-start | bytes 983048 | tf_op jit(solution)/shard_map/ppermute | solution.py:285
  258.4 13.4 %collective-permute-start.36 = (bf16[320,512]{1,0:T(8,128)(2,1)S(1)}, bf16[320,512]{1,0:T(8,128)(2,1)S(1)}, u32[]{:S(2)}, u32[]{:S(2)}) collective-permute-start(bf16[320,512]{1,0:T(8,128)(2,1)S(1)} %fusion.27), channel_id=1, source_target_pairs={{0,1},{1,0},{2,3},{3,2},{4,5},{5,4},{6,7},{7,6},{8,9},{9,8},{10,11... | collective-permute-start | bytes 983048 | tf_op jit(solution)/shard_map/ppermute | solution.py:285
  261.0 15.0 %collective-permute-start.37 = (bf16[320,512]{1,0:T(8,128)(2,1)S(1)}, bf16[320,512]{1,0:T(8,128)(2,1)S(1)}, u32[]{:S(2)}, u32[]{:S(2)}) collective-permute-start(bf16[320,512]{1,0:T(8,128)(2,1)S(1)} %fusion.30), channel_id=1, source_target_pairs={{0,1},{1,0},{2,3},{3,2},{4,5},{5,4},{6,7},{7,6},{8,9},{9,8},{10,11... | collective-permute-start | bytes 983048 | tf_op jit(solution)/shard_map/ppermute | solution.py:285
  264.7 18.4 %collective-permute-start.38 = (bf16[320,512]{1,0:T(8,128)(2,1)S(1)}, bf16[320,512]{1,0:T(8,128)(2,1)S(1)}, u32[]{:S(2)}, u32[]{:S(2)}) collective-permute-start(bf16[320,512]{1,0:T(8,128)(2,1)S(1)} %fusion.33), channel_id=1, source_target_pairs={{0,1},{1,0},{2,3},{3,2},{4,5},{5,4},{6,7},{7,6},{8,9},{9,8},{10,11... | collective-permute-start | bytes 983048 | tf_op jit(solution)/shard_map/ppermute | solution.py:285
  267.4 22.7 %collective-permute-start.39 = (bf16[320,512]{1,0:T(8,128)(2,1)S(1)}, bf16[320,512]{1,0:T(8,128)(2,1)S(1)}, u32[]{:S(2)}, u32[]{:S(2)}) collective-permute-start(bf16[320,512]{1,0:T(8,128)(2,1)S(1)} %fusion.36), channel_id=1, source_target_pairs={{0,1},{1,0},{2,3},{3,2},{4,5},{5,4},{6,7},{7,6},{8,9},{9,8},{10,11... | collective-permute-start | bytes 983048 | tf_op jit(solution)/shard_map/ppermute | solution.py:285
  271.0 26.1 %collective-permute-start.40 = (bf16[320,512]{1,0:T(8,128)(2,1)S(1)}, bf16[320,512]{1,0:T(8,128)(2,1)S(1)}, u32[]{:S(2)}, u32[]{:S(2)}) collective-permute-start(bf16[320,512]{1,0:T(8,128)(2,1)S(1)} %fusion.39), channel_id=1, source_target_pairs={{0,1},{1,0},{2,3},{3,2},{4,5},{5,4},{6,7},{7,6},{8,9},{9,8},{10,11... | collective-permute-start | bytes 983048 | tf_op jit(solution)/shard_map/ppermute | solution.py:285
  (42 other events, 577.4 us)

commit v5 on v4

--- a/solution.py
+++ b/solution.py
@@ -217,7 +217,6 @@
         whole = lax.all_gather(tokens, "tp", axis=1, tiled=True)
 
     kv_parts = []
-    early = []
     for step in range(groups):
         part = jnp.concatenate([columns(keys, step), columns(values, step)], axis=0)
         if step == 0:
@@ -232,12 +231,7 @@
             have.update({j | bit: swap(x, bit) for j, x in list(have.items())})
             bit //= 2
         kv_parts += [have[j] for j in range(ranks)]
-        if step in (0, groups - 1):
-            early.append(have[ranks // 2])
-        else:
-            early.append(part)
-
-    query_down_t, _ = lax.optimization_barrier((query_down_t, early))
+
     features = whole.astype(jnp.float32)
     mean_square = jnp.mean(features * features, axis=-1, keepdims=True)
     normed = (features * lax.rsqrt(mean_square + norm_eps) * gain.astype(jnp.float32)).astype(
@@ -262,7 +256,7 @@
     for step in order:
         q_part = q_parts[step]
         if gate is not None:
-            q_part, _ = lax.optimization_barrier((q_part, (gate, out_merged) if step == 0 else gate))
+            q_part, _ = lax.optimization_barrier((q_part, gate))
         gate = attend(q_part, kv_parts, (my_group ^ step) * ranks + me % ranks, frame_block_number)
         o_parts[step] = swap(gate, step * ranks) if step else gate
     stacked = jnp.stack(o_parts)
@@ -276,7 +270,7 @@
             partial_value.astype(jnp.bfloat16), "tp", scatter_dimension=1, tiled=True
         )
     half = out_merged.shape[1] // 2
-    pieces = 6
+    pieces = 4
     step = half // pieces
     received = []
     for i in range(pieces):

time: 298 us -> 284 us (0.953)
  Pallas kernels: 53.1 us -> 45.5 us
  waiting for transfers between devices: 96.5 us -> 102 us
  starting transfers between devices: 46 us -> 40.6 us
  matrix products: 48.5 us -> 43.5 us
  local copies, waits for them, and re-layouts: 15.1 us -> 10.9 us
  other arithmetic: 27.8 us -> 31.3 us
    ppermute x6 -> x4, waiting for transfers between devices: 24.9 us -> 37.8 us  [shards(): lax.ppermute(product.astype(jnp.bfloat16), 'tp', [(0, 1), (1, 0)])]
    pallas_call x4, Pallas kernels: 53.1 us -> 45.5 us  [attend(): pl.pallas_call(functools.partial(attention_kernel, n, heads, rows), out_s...]
    ppermute x33, waiting for transfers between devices: 71.7 us -> 64.1 us  [swap(): return lax.ppermute(x, 'ctx', [(i, i ^ bit) for i in range(n)])]
    unnamed x66 -> x48, local copies, waits for them, and re-layouts: 9.36 us -> 2.94 us
    ppermute x33, starting transfers between devices: 37.4 us -> 34.4 us  [swap(): return lax.ppermute(x, 'ctx', [(i, i ^ bit) for i in range(n)])]
    ppermute x6 -> x4, starting transfers between devices: 6.49 us -> 4.12 us  [shards(): lax.ppermute(product.astype(jnp.bfloat16), 'tp', [(0, 1), (1, 0)])]
    dot_general x6 -> x4, matrix products: 12.4 us -> 10.3 us  [shards(): product = jnp.dot(attended, theirs, preferred_element_type=jnp.float32)]
  transfers between devices with their start and end apart: 41 -> 39, of which waited for: 17 -> 13; matrix products, arithmetic and copies ran while one was open for 18% -> 20% of each run, Pallas kernels for 18% -> 16%
where the time goes in v5:
time: 284 us
  waiting for transfers between devices  102 us (36%)
  Pallas kernels  45.5 us (16%)
  matrix products  43.5 us (15%)
  starting transfers between devices  40.6 us (14%)
  other arithmetic  31.3 us (11%)
  local copies, waits for them, and re-layouts  10.9 us (4%)
  between operations  10.4 us (4%)
    ppermute x33, waiting for transfers between devices, swap(): return lax.ppermute(x, 'ctx', [(i, i ^ bit) for i in range(n)])  64.1 us
    pallas_call x4, Pallas kernels, attend(): pl.pallas_call(functools.partial(attention_kernel, n, heads, rows), out_s...  45.5 us
    ppermute x4, waiting for transfers between devices, shards(): lax.ppermute(product.astype(jnp.bfloat16), 'tp', [(0, 1), (1, 0)])  37.8 us
    ppermute x33, starting transfers between devices, swap(): return lax.ppermute(x, 'ctx', [(i, i ^ bit) for i in range(n)])  34.4 us
    dot_general x1, matrix products, shards(): jnp.dot(normed, query_merged, preferred_element_type=jnp.float32)  17 us
    dot_general x1, matrix products, merge_weight(): lax.dot_general(down_t, up, (((0,), (0,)), ((), ())), preferred_element_t...  12.8 us
    dot_general x4, matrix products, shards(): product = jnp.dot(attended, theirs, preferred_element_type=jnp.float32)  10.3 us
    reduce_sum x1, other arithmetic, attend(): full = jnp.sum(frame_block_number <= own[0]) // chunk_frames  5.83 us
  transfers between devices with their start and end apart: 39, of which 13 were waited for; matrix products, arithmetic and copies ran while one was open for 20% of the time, Pallas kernels for 16%

profile of v5, /device:TPU:28, one launch (start us, length us, event | category | flops | bytes accessed | tf_op | source)
XLA Modules:
  0.0 284.2 jit_solution(13986505810852713841)
XLA Ops:
  2.4 2.1 broadcast_select_fusion.4
  18.6 6.3 %collective-permute-done.3 = bf16[64,1920]{1,0:T(8,128)(2,1)S(1)} collective-permute-done((bf16[64,1920]{1,0:T(8,128)(2,1)S(1)}, bf16[64,1920]{1,0:T(8,128)(2,1)S(1)}, u32[]{:S(2)}, u32[]{:S(2)}) %collective-permute-start.3) | collective-permute-done | bytes 245792 | tf_op jit(solution)/shard_map/ppermute | solution.py:19
  26.9 4.7 %collective-permute-done.4 = bf16[64,1920]{1,0:T(8,128)(2,1)S(1)} collective-permute-done((bf16[64,1920]{1,0:T(8,128)(2,1)S(1)}, bf16[64,1920]{1,0:T(8,128)(2,1)S(1)}, u32[]{:S(2)}, u32[]{:S(2)}) %collective-permute-start.4) | collective-permute-done | bytes 245792 | tf_op jit(solution)/shard_map/ppermute | solution.py:19
  31.7 2.4 collective-permute-start.5
  36.2 7.5 %collective-permute-done.5 = bf16[64,1920]{1,0:T(8,128)(2,1)S(1)} collective-permute-done((bf16[64,1920]{1,0:T(8,128)(2,1)S(1)}, bf16[64,1920]{1,0:T(8,128)(2,1)S(1)}, u32[]{:S(2)}, u32[]{:S(2)}) %collective-permute-start.5) | collective-permute-done | bytes 245792 | tf_op jit(solution)/shard_map/ppermute | solution.py:19
  45.6 10.1 %collective-permute-done.6 = bf16[64,1920]{1,0:T(8,128)(2,1)S(1)} collective-permute-done((bf16[64,1920]{1,0:T(8,128)(2,1)S(1)}, bf16[64,1920]{1,0:T(8,128)(2,1)S(1)}, u32[]{:S(2)}, u32[]{:S(2)}) %collective-permute-start.6) | collective-permute-done | bytes 245792 | tf_op jit(solution)/shard_map/ppermute | solution.py:19
  55.8 2.4 broadcast_select_fusion.1
  60.3 17.0 %fusion.9 = bf16[320,1536]{1,0:T(8,128)(2,1)} fusion(bf16[6144,1536]{1,0:T(8,128)(2,1)} %param.16, f32[6144]{0:T(1024)S(1)} %maximum_convert_fusion, f32[320]{0:T(512)S(1)} %add_rsqrt_fusion, bf16[320,3072]{1,0:T(8,128)(2,1)} %copy-done.9, bf16[320,3072]{1,0:T(8,128)(2,1)S(1)} %get-tuple-element.43, bf16[64,3840]{1,0:T(8,128)(2,1)} %get-tuple-element.64, ...), kind=kOutput, calls=%fused_computation.13 | convolution fusion | flops 7291895808 | bytes 24995072 | tf_op jit(solution)/shard_map/dot_general | solution.py:241
  79.4 1.9 pad_maximum_fusion.15
  81.6 5.8 %fusion.49 = (s32[]{:T(128)}, s32[]{:T(128)}, s32[]{:T(128)}, s32[]{:T(128)}, s32[]{:T(128)}, /*index=5*/s32[]{:T(128)}, s32[]{:T(128)}, s32[]{:T(128)}) fusion(s32[80]{0:T(128)S(1)} %copy-done.15, s32[]{:T(128)} %bitcast, s32[]{:T(128)} %bitcast.17, s32[]{:T(128)} %bitcast.15, s32[]{:T(128)} %bitcast.13, s32[]{:T(128)} %bitcast.11, s32[]{:T(128)} %bitcast.2, ...), kind=kLoop, calls=%fused_computation.122 | loop fusion | flops 1912 | bytes 384 | tf_op jit(solution)/shard_map/reduce_sum | solution.py:148
  95.6 2.1 collective-permute-start.32
  97.7 8.3 %collective-permute-done.12.refs_6_ = bf16[640,384]{1,0:T(8,128)(2,1)S(1)} collective-permute-done((bf16[640,384]{1,0:T(8,128)(2,1)S(1)}, bf16[640,384]{1,0:T(8,128)(2,1)S(1)}, u32[]{:S(2)}, u32[]{:S(2)}) %collective-permute-start.12) | collective-permute-done | bytes 491552 | tf_op jit(solution)/shard_map/ppermute | solution.py:19
  106.0 2.2 constant_dynamic-slice_fusion.11
  108.7 10.2 %collective-permute-done.18.refs_12_ = bf16[640,384]{1,0:T(8,128)(2,1)} collective-permute-done((bf16[640,384]{1,0:T(8,128)(2,1)}, bf16[640,384]{1,0:T(8,128)(2,1)}, u32[]{:S(2)}, u32[]{:S(2)}) %collective-permute-start.18) | collective-permute-done | bytes 491552 | tf_op jit(solution)/shard_map/ppermute | solution.py:19
  121.0 7.9 %collective-permute-done.32 = bf16[64,1920]{1,0:T(8,128)(2,1)S(1)} collective-permute-done((bf16[64,1920]{1,0:T(8,128)(2,1)S(1)}, bf16[64,1920]{1,0:T(8,128)(2,1)S(1)}, u32[]{:S(2)}, u32[]{:S(2)}) %collective-permute-start.32) | collective-permute-done | bytes 245792 | tf_op jit(solution)/shard_map/ppermute | solution.py:19
  137.5 6.4 %collective-permute-done.16.refs_10_ = bf16[640,384]{1,0:T(8,128)(2,1)} collective-permute-done((bf16[640,384]{1,0:T(8,128)(2,1)}, bf16[640,384]{1,0:T(8,128)(2,1)}, u32[]{:S(2)}, u32[]{:S(2)}) %collective-permute-start.16) | collective-permute-done | bytes 491552 | tf_op jit(solution)/shard_map/ppermute | solution.py:19
  145.2 2.7 collective-permute-done.33
  151.6 12.6 %block_attention.4 = bf16[320,384]{1,0:T(8,128)(2,1)S(1)} custom-call(s32[3]{0:T(128)S(1)} %add_add_fusion.3.refs_0_, s32[8,1,640]{2,1,0:T(1,128)S(1)} %broadcast_in_dim.132.refs_1_, s32[320,1]{1,0:T(8,128)S(1)} %reshape_reshape.23.refs_2_, bf16[320,384]{1,0:T(8,128)(2,1)} %collective-permute-done.10.refs_3_, ...), custom_call_target="tpu_custom_call" | custom-call | flops 2516582400 | bytes 8355840 | tf_op jit(solution)/shard_map/block_attention/pallas_call | solution.py:155
  164.3 6.9 %collective-permute-start.26 = (bf16[320,384]{1,0:T(8,128)(2,1)S(1)}, bf16[320,384]{1,0:T(8,128)(2,1)S(1)}, u32[]{:S(2)}, u32[]{:S(2)}) collective-permute-start(bf16[320,384]{1,0:T(8,128)(2,1)S(1)} %block_attention.4), channel_id=1, source_target_pairs={{0,8},{2,10},{4,12},{6,14},{8,0},{10,2},{12,4},{14,6},{16,24},{18,... | collective-permute-start | bytes 737288 | tf_op jit(solution)/shard_map/ppermute | solution.py:19
  171.2 9.5 %block_attention.5 = bf16[320,384]{1,0:T(8,128)(2,1)S(1)} custom-call(s32[3]{0:T(128)S(1)} %add_add_fusion.2.refs_0_, s32[8,1,640]{2,1,0:T(1,128)S(1)} %broadcast_in_dim.132.refs_1_, s32[320,1]{1,0:T(8,128)S(1)} %reshape_reshape.22.refs_2_, bf16[320,384]{1,0:T(8,128)(2,1)S(1)} %collective-permute-done.9.refs_3_, ...), custom_call_target="tpu_custom_call" | custom-call | flops 2516582400 | bytes 8355840 | tf_op jit(solution)/shard_map/block_attention/pallas_call | solution.py:155
  180.9 7.9 %block_attention.6 = bf16[320,384]{1,0:T(8,128)(2,1)S(1)} custom-call(s32[3]{0:T(128)S(1)} %add_add_fusion.1.refs_0_, s32[8,1,640]{2,1,0:T(1,128)S(1)} %broadcast_in_dim.132.refs_1_, s32[320,1]{1,0:T(8,128)S(1)} %reshape_reshape.21.refs_2_, bf16[320,384]{1,0:T(8,128)(2,1)S(1)} %collective-permute-done.8.refs_3_, ...), custom_call_target="tpu_custom_call" | custom-call | flops 2516582400 | bytes 8355840 | tf_op jit(solution)/shard_map/block_attention/pallas_call | solution.py:155
  188.8 8.9 %collective-permute-start.28 = (bf16[320,384]{1,0:T(8,128)(2,1)S(1)}, bf16[320,384]{1,0:T(8,128)(2,1)S(1)}, u32[]{:S(2)}, u32[]{:S(2)}) collective-permute-start(bf16[320,384]{1,0:T(8,128)(2,1)S(1)} %block_attention.6), channel_id=1, source_target_pairs={{0,24},{2,26},{4,28},{6,30},{8,16},{10,18},{12,20},{14,22},{16,8},... | collective-permute-start | bytes 737288 | tf_op jit(solution)/shard_map/ppermute | solution.py:19
  197.8 15.5 %block_attention.7 = bf16[320,384]{1,0:T(8,128)(2,1)S(1)} custom-call(s32[3]{0:T(128)S(1)} %add_add_fusion.refs_0_, s32[8,1,640]{2,1,0:T(1,128)S(1)} %broadcast_in_dim.132.refs_1_, s32[320,1]{1,0:T(8,128)S(1)} %reshape_reshape.20.refs_2_, bf16[320,384]{1,0:T(8,128)(2,1)S(1)} %get-tuple-element.17.refs_3_, bf16[640,384]{1,0:T(8,128)(2,1)S(1)} %pad_maximum_fusion.13.refs_4_, ...), custom_call_target="tpu_custom_call" | custom-call | flops 2516582400 | bytes 8355840 | tf_op jit(solution)/shard_map/block_attention/pallas_call | solution.py:155
  213.8 12.8 %add_convert_fusion = bf16[1536,6144]{1,0:T(8,128)(2,1)} fusion(bf16[1536,6144]{1,0:T(8,128)(2,1)} %param.17, bf16[64,3840]{1,0:T(8,128)(2,1)S(1)} %get-tuple-element.62, bf16[64,3840]{1,0:T(8,128)(2,1)S(1)} %get-tuple-element.61), kind=kOutput, calls=%fused_computation | convolution fusion | flops 1237843968 | bytes 38928384 | tf_op jit(solution)/shard_map/dot_general | solution.py:60
  226.7 2.7 fusion.29
  229.4 3.2 %fusion.26 = bf16[320,768]{1,0:T(8,128)(2,1)S(1)} fusion(bf16[1536,6144]{1,0:T(8,128)(2,1)} %add_convert_fusion, s32[]{:T(128)S(6)} %select_n.333, bf16[320,384]{1,0:T(8,128)(2,1)S(1)} %get-tuple-element.46, bf16[320,384]{1,0:T(8,128)(2,1)S(1)} %get-tuple-element.47, bf16[320,384]{1,0:T(8,128)(2,1)S(1)} %get-tuple-element.48, ...), kind=kOutput, calls=%fused_computation.27 | convolution fusion | flops 759152640 | bytes 3833860 | tf_op jit(solution)/shard_map/dot_general | solution.py:278
  232.6 3.3 %fusion.23 = bf16[320,768]{1,0:T(8,128)(2,1)S(1)} fusion(bf16[1536,6144]{1,0:T(8,128)(2,1)} %add_convert_fusion, s32[]{:T(128)S(6)} %select_n.332, bf16[320,384]{1,0:T(8,128)(2,1)S(1)} %get-tuple-element.46, bf16[320,384]{1,0:T(8,128)(2,1)S(1)} %get-tuple-element.47, bf16[320,384]{1,0:T(8,128)(2,1)S(1)} %get-tuple-element.48, ...), kind=kOutput, calls=%fused_computation.26 | convolution fusion | flops 759152640 | bytes 3833860 | tf_op jit(solution)/shard_map/dot_general | solution.py:278
  241.1 3.3 %fusion = f32[320,3072]{1,0:T(8,128)S(1)} fusion(bf16[1536,6144]{1,0:T(8,128)(2,1)S(1)} %copy-done.6, s32[]{:T(128)S(6)} %select_n.330, bf16[320,384]{1,0:T(8,128)(2,1)S(1)} %get-tuple-element.46, bf16[320,384]{1,0:T(8,128)(2,1)S(1)} %get-tuple-element.47, bf16[320,384]{1,0:T(8,128)(2,1)S(1)} %get-tuple-element.48, bf16[320,384]{1,0:T(8,128)(2,1)S(1)} %get-tuple-element.45), kind=kOutput, calls=%fused_computation.4 | convolution fusion | flops 3023831040 | bytes 14352388 | tf_op jit(solution)/shard_map/dot_general | solution.py:281
  244.4 6.6 %collective-permute-done.35 = bf16[320,768]{1,0:T(8,128)(2,1)S(1)} collective-permute-done((bf16[320,768]{1,0:T(8,128)(2,1)S(1)}, bf16[320,768]{1,0:T(8,128)(2,1)S(1)}, u32[]{:S(2)}, u32[]{:S(2)}) %collective-permute-start.35) | collective-permute-done | bytes 491552 | tf_op jit(solution)/shard_map/ppermute | solution.py:279
  251.1 10.5 %collective-permute-done.36 = bf16[320,768]{1,0:T(8,128)(2,1)S(1)} collective-permute-done((bf16[320,768]{1,0:T(8,128)(2,1)S(1)}, bf16[320,768]{1,0:T(8,128)(2,1)S(1)}, u32[]{:S(2)}, u32[]{:S(2)}) %collective-permute-start.36) | collective-permute-done | bytes 491552 | tf_op jit(solution)/shard_map/ppermute | solution.py:279
  261.6 10.5 %collective-permute-done.37 = bf16[320,768]{1,0:T(8,128)(2,1)S(1)} collective-permute-done((bf16[320,768]{1,0:T(8,128)(2,1)S(1)}, bf16[320,768]{1,0:T(8,128)(2,1)S(1)}, u32[]{:S(2)}, u32[]{:S(2)}) %collective-permute-start.37) | collective-permute-done | bytes 491552 | tf_op jit(solution)/shard_map/ppermute | solution.py:279
  272.1 10.1 %collective-permute-done.38 = bf16[320,768]{1,0:T(8,128)(2,1)S(1)} collective-permute-done((bf16[320,768]{1,0:T(8,128)(2,1)S(1)}, bf16[320,768]{1,0:T(8,128)(2,1)S(1)}, u32[]{:S(2)}, u32[]{:S(2)}) %collective-permute-start.38) | collective-permute-done | bytes 491552 | tf_op jit(solution)/shard_map/ppermute | solution.py:279
  (165 shorter events, 49.3 us)
Async XLA Ops:
  0.9 17.7 %collective-permute-start.1 = (bf16[1,3072]{1,0:T(2,128)(2,1)S(1)}, bf16[1,3072]{1,0:T(2,128)(2,1)S(1)}, u32[]{:S(2)}, u32[]{:S(2)}) collective-permute-start(bf16[1,3072]{1,0:T(2,128)(2,1)S(1)} %broadcast_in_dim.108), channel_id=1, source_target_pairs={{0,1},{1,0},{2,3},{3,2},{4,5},{5,4},{6,7},{7,6},{8,9},{9,8},{10,11... | collective-permute-start | bytes 18440 | tf_op jit(solution)/shard_map/ppermute | solution.py:209
  4.5 21.2 %collective-permute-start.29 = (bf16[64,3840]{1,0:T(8,128)(2,1)}, bf16[64,3840]{1,0:T(8,128)(2,1)}, u32[]{:S(2)}, u32[]{:S(2)}) collective-permute-start(bf16[64,3840]{1,0:T(8,128)(2,1)} %broadcast_select_fusion.4), channel_id=1, source_target_pairs={{0,2},{2,0},{4,6},{6,4},{8,10},{10,8},{12,14},{14,12},{16,18},{18,... | collective-permute-start | bytes 1474568 | tf_op jit(solution)/shard_map/ppermute | solution.py:19
  8.7 25.9 %collective-permute-start.22 = (bf16[640,384]{1,0:T(8,128)(2,1)}, bf16[640,384]{1,0:T(8,128)(2,1)S(1)}, u32[]{:S(2)}, u32[]{:S(2)}) collective-permute-start(bf16[640,384]{1,0:T(8,128)(2,1)} %pad_maximum_fusion.16), channel_id=1, source_target_pairs={{0,24},{2,26},{4,28},{6,30},{8,16},{10,18},{12,20},{14,22},{16,8},... | collective-permute-start | bytes 1474568 | tf_op jit(solution)/shard_map/ppermute | solution.py:19
  8.9 46.9 %collective-permute-start = (bf16[320,3072]{1,0:T(8,128)(2,1)}, bf16[320,3072]{1,0:T(8,128)(2,1)}, u32[]{:S(2)}, u32[]{:S(2)}) collective-permute-start(bf16[320,3072]{1,0:T(8,128)(2,1)} %param.12), channel_id=1, source_target_pairs={{0,1},{1,0},{2,3},{3,2},{4,5},{5,4},{6,7},{7,6},{8,9},{9,8},{10,11... | collective-permute-start | bytes 5898248 | tf_op jit(solution)/shard_map/ppermute | solution.py:209
  31.7 12.0 %collective-permute-start.5 = (bf16[64,1920]{1,0:T(8,128)(2,1)S(1)}, bf16[64,1920]{1,0:T(8,128)(2,1)S(1)}, u32[]{:S(2)}, u32[]{:S(2)}) collective-permute-start(bf16[64,1920]{1,0:T(8,128)(2,1)S(1)} %broadcast_select_fusion.10), channel_id=1, source_target_pairs={{0,16},{2,18},{4,20},{6,22},{8,24},{10,26},{12,28},{14,30},{16,0},... | collective-permute-start | bytes 737288 | tf_op jit(solution)/shard_map/ppermute | solution.py:19
  34.7 58.4 %collective-permute-start.24 = (bf16[640,384]{1,0:T(8,128)(2,1)S(1)}, bf16[640,384]{1,0:T(8,128)(2,1)S(1)}, u32[]{:S(2)}, u32[]{:S(2)}) collective-permute-start(bf16[640,384]{1,0:T(8,128)(2,1)S(1)} %collective-permute-done.22.refs_16_), channel_id=1, source_target_pairs={{0,4},{2,6},{4,0},{6,2},{8,12},{10,14},{12,8},{14,10},{16,20},{18,... | collective-permute-start | bytes 1474568 | tf_op jit(solution)/shard_map/ppermute | solution.py:19
  43.7 11.9 %collective-permute-start.6 = (bf16[64,1920]{1,0:T(8,128)(2,1)S(1)}, bf16[64,1920]{1,0:T(8,128)(2,1)S(1)}, u32[]{:S(2)}, u32[]{:S(2)}) collective-permute-start(bf16[64,1920]{1,0:T(8,128)(2,1)S(1)} %broadcast_select_fusion.11), channel_id=1, source_target_pairs={{0,4},{2,6},{4,0},{6,2},{8,12},{10,14},{12,8},{14,10},{16,20},{18,... | collective-permute-start | bytes 737288 | tf_op jit(solution)/shard_map/ppermute | solution.py:19
  77.3 16.4 %collective-permute-start.31 = (bf16[64,1920]{1,0:T(8,128)(2,1)}, bf16[64,1920]{1,0:T(8,128)(2,1)S(1)}, u32[]{:S(2)}, u32[]{:S(2)}) collective-permute-start(bf16[64,1920]{1,0:T(8,128)(2,1)} %select_select_fusion.2), channel_id=1, source_target_pairs={{0,8},{2,10},{4,12},{6,14},{8,0},{10,2},{12,4},{14,6},{16,24},{18,... | collective-permute-start | bytes 737288 | tf_op jit(solution)/shard_map/ppermute | solution.py:19
  81.4 14.2 %collective-permute-start.23 = (bf16[640,384]{1,0:T(8,128)(2,1)S(1)}, bf16[640,384]{1,0:T(8,128)(2,1)S(1)}, u32[]{:S(2)}, u32[]{:S(2)}) collective-permute-start(bf16[640,384]{1,0:T(8,128)(2,1)S(1)} %collective-permute-done.22.refs_16_), channel_id=1, source_target_pairs={{0,2},{2,0},{4,6},{6,4},{8,10},{10,8},{12,14},{14,12},{16,18},{18,... | collective-permute-start | bytes 1474568 | tf_op jit(solution)/shard_map/ppermute | solution.py:19
  92.5 13.5 %collective-permute-start.12 = (bf16[640,384]{1,0:T(8,128)(2,1)S(1)}, bf16[640,384]{1,0:T(8,128)(2,1)S(1)}, u32[]{:S(2)}, u32[]{:S(2)}) collective-permute-start(bf16[640,384]{1,0:T(8,128)(2,1)S(1)} %pad_maximum_fusion.13.refs_4_), channel_id=1, source_target_pairs={{0,4},{2,6},{4,0},{6,2},{8,12},{10,14},{12,8},{14,10},{16,20},{18,... | collective-permute-start | bytes 1474568 | tf_op jit(solution)/shard_map/ppermute | solution.py:19
  93.1 15.1 %collective-permute-start.11 = (bf16[640,384]{1,0:T(8,128)(2,1)S(1)}, bf16[640,384]{1,0:T(8,128)(2,1)S(1)}, u32[]{:S(2)}, u32[]{:S(2)}) collective-permute-start(bf16[640,384]{1,0:T(8,128)(2,1)S(1)} %pad_maximum_fusion.13.refs_4_), channel_id=1, source_target_pairs={{0,2},{2,0},{4,6},{6,4},{8,10},{10,8},{12,14},{14,12},{16,18},{18,... | collective-permute-start | bytes 1474568 | tf_op jit(solution)/shard_map/ppermute | solution.py:19
  93.1 25.9 %collective-permute-start.18 = (bf16[640,384]{1,0:T(8,128)(2,1)}, bf16[640,384]{1,0:T(8,128)(2,1)}, u32[]{:S(2)}, u32[]{:S(2)}) collective-permute-start(bf16[640,384]{1,0:T(8,128)(2,1)} %pad_maximum_fusion.15), channel_id=1, source_target_pairs={{0,16},{2,18},{4,20},{6,22},{8,24},{10,26},{12,28},{14,30},{16,0},... | collective-permute-start | bytes 1474568 | tf_op jit(solution)/shard_map/ppermute | solution.py:19
  93.7 26.8 %collective-permute-start.14 = (bf16[640,384]{1,0:T(8,128)(2,1)}, bf16[640,384]{1,0:T(8,128)(2,1)}, u32[]{:S(2)}, u32[]{:S(2)}) collective-permute-start(bf16[640,384]{1,0:T(8,128)(2,1)} %pad_maximum_fusion.14), channel_id=1, source_target_pairs={{0,8},{2,10},{4,12},{6,14},{8,0},{10,2},{12,4},{14,6},{16,24},{18,... | collective-permute-start | bytes 1474568 | tf_op jit(solution)/shard_map/ppermute | solution.py:19
  95.6 33.3 %collective-permute-start.32 = (bf16[64,1920]{1,0:T(8,128)(2,1)S(1)}, bf16[64,1920]{1,0:T(8,128)(2,1)S(1)}, u32[]{:S(2)}, u32[]{:S(2)}) collective-permute-start(bf16[64,1920]{1,0:T(8,128)(2,1)S(1)} %broadcast_select_fusion.8), channel_id=1, source_target_pairs={{0,16},{2,18},{4,20},{6,22},{8,24},{10,26},{12,28},{14,30},{16,0},... | collective-permute-start | bytes 737288 | tf_op jit(solution)/shard_map/ppermute | solution.py:19
  106.0 23.7 %collective-permute-start.25 = (bf16[640,384]{1,0:T(8,128)(2,1)S(1)}, bf16[640,384]{1,0:T(8,128)(2,1)S(1)}, u32[]{:S(2)}, u32[]{:S(2)}) collective-permute-start(bf16[640,384]{1,0:T(8,128)(2,1)S(1)} %collective-permute-done.24.refs_18_), channel_id=1, source_target_pairs={{0,2},{2,0},{4,6},{6,4},{8,10},{10,8},{12,14},{14,12},{16,18},{18,... | collective-permute-start | bytes 1474568 | tf_op jit(solution)/shard_map/ppermute | solution.py:19
  108.2 28.7 %collective-permute-start.13 = (bf16[640,384]{1,0:T(8,128)(2,1)S(1)}, bf16[640,384]{1,0:T(8,128)(2,1)}, u32[]{:S(2)}, u32[]{:S(2)}) collective-permute-start(bf16[640,384]{1,0:T(8,128)(2,1)S(1)} %collective-permute-done.12.refs_6_), channel_id=1, source_target_pairs={{0,2},{2,0},{4,6},{6,4},{8,10},{10,8},{12,14},{14,12},{16,18},{18,... | collective-permute-start | bytes 1474568 | tf_op jit(solution)/shard_map/ppermute | solution.py:19
  118.9 18.5 %collective-permute-start.20 = (bf16[640,384]{1,0:T(8,128)(2,1)}, bf16[640,384]{1,0:T(8,128)(2,1)}, u32[]{:S(2)}, u32[]{:S(2)}) collective-permute-start(bf16[640,384]{1,0:T(8,128)(2,1)} %collective-permute-done.18.refs_12_), channel_id=1, source_target_pairs={{0,4},{2,6},{4,0},{6,2},{8,12},{10,14},{12,8},{14,10},{16,20},{18,... | collective-permute-start | bytes 1474568 | tf_op jit(solution)/shard_map/ppermute | solution.py:19
  120.5 23.4 %collective-permute-start.16 = (bf16[640,384]{1,0:T(8,128)(2,1)}, bf16[640,384]{1,0:T(8,128)(2,1)}, u32[]{:S(2)}, u32[]{:S(2)}) collective-permute-start(bf16[640,384]{1,0:T(8,128)(2,1)} %collective-permute-done.14.refs_8_), channel_id=1, source_target_pairs={{0,4},{2,6},{4,0},{6,2},{8,12},{10,14},{12,8},{14,10},{16,20},{18,... | collective-permute-start | bytes 1474568 | tf_op jit(solution)/shard_map/ppermute | solution.py:19
  130.4 17.5 %collective-permute-start.33 = (bf16[64,1920]{1,0:T(8,128)(2,1)}, bf16[64,1920]{1,0:T(8,128)(2,1)}, u32[]{:S(2)}, u32[]{:S(2)}) collective-permute-start(bf16[64,1920]{1,0:T(8,128)(2,1)} %broadcast_select_fusion.9), channel_id=1, source_target_pairs={{0,4},{2,6},{4,0},{6,2},{8,12},{10,14},{12,8},{14,10},{16,20},{18,... | collective-permute-start | bytes 737288 | tf_op jit(solution)/shard_map/ppermute | solution.py:19
  136.9 12.2 %collective-permute-start.19 = (bf16[640,384]{1,0:T(8,128)(2,1)}, bf16[640,384]{1,0:T(8,128)(2,1)}, u32[]{:S(2)}, u32[]{:S(2)}) collective-permute-start(bf16[640,384]{1,0:T(8,128)(2,1)} %collective-permute-done.18.refs_12_), channel_id=1, source_target_pairs={{0,2},{2,0},{4,6},{6,4},{8,10},{10,8},{12,14},{14,12},{16,18},{18,... | collective-permute-start | bytes 1474568 | tf_op jit(solution)/shard_map/ppermute | solution.py:19
  136.9 12.6 %collective-permute-start.15 = (bf16[640,384]{1,0:T(8,128)(2,1)}, bf16[640,384]{1,0:T(8,128)(2,1)}, u32[]{:S(2)}, u32[]{:S(2)}) collective-permute-start(bf16[640,384]{1,0:T(8,128)(2,1)} %collective-permute-done.14.refs_8_), channel_id=1, source_target_pairs={{0,2},{2,0},{4,6},{6,4},{8,10},{10,8},{12,14},{14,12},{16,18},{18,... | collective-permute-start | bytes 1474568 | tf_op jit(solution)/shard_map/ppermute | solution.py:19
  137.4 12.1 %collective-permute-start.21 = (bf16[640,384]{1,0:T(8,128)(2,1)}, bf16[640,384]{1,0:T(8,128)(2,1)}, u32[]{:S(2)}, u32[]{:S(2)}) collective-permute-start(bf16[640,384]{1,0:T(8,128)(2,1)} %collective-permute-done.20.refs_14_), channel_id=1, source_target_pairs={{0,2},{2,0},{4,6},{6,4},{8,10},{10,8},{12,14},{14,12},{16,18},{18,... | collective-permute-start | bytes 1474568 | tf_op jit(solution)/shard_map/ppermute | solution.py:19
  147.9 23.3 %collective-permute-start.9 = (bf16[320,384]{1,0:T(8,128)(2,1)}, bf16[320,384]{1,0:T(8,128)(2,1)S(1)}, u32[]{:S(2)}, u32[]{:S(2)}) collective-permute-start(bf16[320,384]{1,0:T(8,128)(2,1)} %get-tuple-element.51), channel_id=1, source_target_pairs={{0,16},{2,18},{4,20},{6,22},{8,24},{10,26},{12,28},{14,30},{16,0},... | collective-permute-start | bytes 737288 | tf_op jit(solution)/shard_map/ppermute | solution.py:19
  149.1 31.8 %collective-permute-start.8 = (bf16[320,384]{1,0:T(8,128)(2,1)}, bf16[320,384]{1,0:T(8,128)(2,1)S(1)}, u32[]{:S(2)}, u32[]{:S(2)}) collective-permute-start(bf16[320,384]{1,0:T(8,128)(2,1)} %get-tuple-element.52), channel_id=1, source_target_pairs={{0,24},{2,26},{4,28},{6,30},{8,16},{10,18},{12,20},{14,22},{16,8},... | collective-permute-start | bytes 737288 | tf_op jit(solution)/shard_map/ppermute | solution.py:19
  164.3 49.0 %collective-permute-start.26 = (bf16[320,384]{1,0:T(8,128)(2,1)S(1)}, bf16[320,384]{1,0:T(8,128)(2,1)S(1)}, u32[]{:S(2)}, u32[]{:S(2)}) collective-permute-start(bf16[320,384]{1,0:T(8,128)(2,1)S(1)} %block_attention.4), channel_id=1, source_target_pairs={{0,8},{2,10},{4,12},{6,14},{8,0},{10,2},{12,4},{14,6},{16,24},{18,... | collective-permute-start | bytes 737288 | tf_op jit(solution)/shard_map/ppermute | solution.py:19
  180.7 32.6 %collective-permute-start.27 = (bf16[320,384]{1,0:T(8,128)(2,1)S(1)}, bf16[320,384]{1,0:T(8,128)(2,1)S(1)}, u32[]{:S(2)}, u32[]{:S(2)}) collective-permute-start(bf16[320,384]{1,0:T(8,128)(2,1)S(1)} %block_attention.5), channel_id=1, source_target_pairs={{0,16},{2,18},{4,20},{6,22},{8,24},{10,26},{12,28},{14,30},{16,0},... | collective-permute-start | bytes 737288 | tf_op jit(solution)/shard_map/ppermute | solution.py:19
  188.8 24.5 %collective-permute-start.28 = (bf16[320,384]{1,0:T(8,128)(2,1)S(1)}, bf16[320,384]{1,0:T(8,128)(2,1)S(1)}, u32[]{:S(2)}, u32[]{:S(2)}) collective-permute-start(bf16[320,384]{1,0:T(8,128)(2,1)S(1)} %block_attention.6), channel_id=1, source_target_pairs={{0,24},{2,26},{4,28},{6,30},{8,16},{10,18},{12,20},{14,22},{16,8},... | collective-permute-start | bytes 737288 | tf_op jit(solution)/shard_map/ppermute | solution.py:19
  197.7 15.9 %collective-permute-start.34 = (bf16[64,3840]{1,0:T(8,128)(2,1)S(1)}, bf16[64,3840]{1,0:T(8,128)(2,1)S(1)}, u32[]{:S(2)}, u32[]{:S(2)}) collective-permute-start(bf16[64,3840]{1,0:T(8,128)(2,1)S(1)} %pad_maximum_fusion.17), channel_id=1, source_target_pairs={{0,2},{2,0},{4,6},{6,4},{8,10},{10,8},{12,14},{14,12},{16,18},{18,... | collective-permute-start | bytes 1474568 | tf_op jit(solution)/shard_map/ppermute | solution.py:19
  237.0 14.1 %collective-permute-start.35 = (bf16[320,768]{1,0:T(8,128)(2,1)S(1)}, bf16[320,768]{1,0:T(8,128)(2,1)S(1)}, u32[]{:S(2)}, u32[]{:S(2)}) collective-permute-start(bf16[320,768]{1,0:T(8,128)(2,1)S(1)} %fusion.20), channel_id=1, source_target_pairs={{0,1},{1,0},{2,3},{3,2},{4,5},{5,4},{6,7},{7,6},{8,9},{9,8},{10,11... | collective-permute-start | bytes 1474568 | tf_op jit(solution)/shard_map/ppermute | solution.py:279
  238.5 23.1 %collective-permute-start.36 = (bf16[320,768]{1,0:T(8,128)(2,1)S(1)}, bf16[320,768]{1,0:T(8,128)(2,1)S(1)}, u32[]{:S(2)}, u32[]{:S(2)}) collective-permute-start(bf16[320,768]{1,0:T(8,128)(2,1)S(1)} %fusion.23), channel_id=1, source_target_pairs={{0,1},{1,0},{2,3},{3,2},{4,5},{5,4},{6,7},{7,6},{8,9},{9,8},{10,11... | collective-permute-start | bytes 1474568 | tf_op jit(solution)/shard_map/ppermute | solution.py:279
  239.1 33.1 %collective-permute-start.37 = (bf16[320,768]{1,0:T(8,128)(2,1)S(1)}, bf16[320,768]{1,0:T(8,128)(2,1)S(1)}, u32[]{:S(2)}, u32[]{:S(2)}) collective-permute-start(bf16[320,768]{1,0:T(8,128)(2,1)S(1)} %fusion.26), channel_id=1, source_target_pairs={{0,1},{1,0},{2,3},{3,2},{4,5},{5,4},{6,7},{7,6},{8,9},{9,8},{10,11... | collective-permute-start | bytes 1474568 | tf_op jit(solution)/shard_map/ppermute | solution.py:279
  240.6 41.7 %collective-permute-start.38 = (bf16[320,768]{1,0:T(8,128)(2,1)S(1)}, bf16[320,768]{1,0:T(8,128)(2,1)S(1)}, u32[]{:S(2)}, u32[]{:S(2)}) collective-permute-start(bf16[320,768]{1,0:T(8,128)(2,1)S(1)} %fusion.29), channel_id=1, source_target_pairs={{0,1},{1,0},{2,3},{3,2},{4,5},{5,4},{6,7},{7,6},{8,9},{9,8},{10,11... | collective-permute-start | bytes 1474568 | tf_op jit(solution)/shard_map/ppermute | solution.py:279
  (31 other events, 376.8 us)
